TPU v7x, 32 devices: a whole 2x2x4 slice. The times are simulated.
32 devices in a mesh: replica: 4 (over z), fsdp: 8 (over y, x, core).
Axes of the slice: x: 2, y: 2, z: 4, core: 2. Of those that a mesh axis runs over, the one named last changes fastest.
Arguments:
- grad_parts: bfloat16 [4, 32, 512, 512], P('replica', None, 'fsdp'), may hold values from -6 to 6
- moment: float32 [32, 512, 512], P(('replica', 'fsdp')), may hold values from -4 to 4
- second_moment: float32 [32, 512, 512], P(('replica', 'fsdp')), may hold values from 0.25 to 4
- left_factor: float32 [32, 512, 512], P(('replica', 'fsdp'))
- right_factor: float32 [32, 512, 512], P(('replica', 'fsdp'))
- left_basis: float32 [32, 512, 512], P(('replica', 'fsdp'))
- right_basis: float32 [32, 512, 512], P(('replica', 'fsdp'))
- block_order: int32 [32], replicated, may hold values from 0 to 31, as said below
- refresh_ids: int32 [3], replicated, may hold values from 0 to 29, as said below
Outputs:
- step_dir: bfloat16 [32, 512, 512], P('replica', 'fsdp')
- left_new: float32 [32, 512, 512], P(('replica', 'fsdp'))
- right_new: float32 [32, 512, 512], P(('replica', 'fsdp'))
Inputs may be any that keep to these rules, and one draw needn't show every extreme that they name: Slot s holds block block_order[s]; it is a permutation of the 32 blocks in which block_order[s] // 8 == s // 8. refresh_ids[j] lies in [10 j, 10 j + 9]; the ids are distinct and rising; the first is 0 and the last is 29.
All inputs are finite; a program needn't handle non-finite values.
Results may differ from a plain program's by a relative error of at most 0.011.
Values may be sent and summed in bfloat16 or wider, within the bound.
No kernel may reach another device: no remote copies, remote signals or barrier semaphores. Data moves between devices by JAX's collectives and lax.ppermute only.
A program may use at most 128 MiB of HBM per device.

v0:
```python
import functools

import jax
import jax.numpy as jnp
from jax import lax
from jax.experimental import pallas as pl
from jax.experimental.pallas import tpu as pltpu
from jax.sharding import PartitionSpec as P

F32 = jnp.float32
BF16 = jnp.bfloat16
NN = (((1,), (0,)), ((), ()))
NT = (((1,), (1,)), ((), ()))
VMEM_LIMIT = 24 * 1024 * 1024

START_BOUND = 4.0
END_BOUND = 0.016

FIRST_STEPS = 4
MORE_STEPS = 5
LAST_STEPS = 16


def dot(a, b, form=NN):
    return lax.dot_general(a, b, form, preferred_element_type=F32)


def split(x):
    hi = x.astype(BF16)
    return hi, (x - hi.astype(F32)).astype(BF16)


def store_split(hi_ref, lo_ref, x):
    hi, lo = split(x)
    hi_ref[...] = hi
    lo_ref[...] = lo


def halves(width):
    half = width // 2
    return ((slice(half, width), width), (slice(0, half), half))


def lower_step(gram, first_row):
    rows = lax.broadcasted_iota(jnp.int32, gram.shape, 0) + first_row
    cols = lax.broadcasted_iota(jnp.int32, gram.shape, 1)
    return jnp.where(rows > cols, gram, jnp.where(rows == cols, 0.5 * gram - 0.5, 0.0))


def triangle(hi_ref, step_ref):
    total = 0.0
    for rows, reach in halves(hi_ref.shape[0]):
        step = lower_step(dot(hi_ref[rows, :], hi_ref[:reach, :], NT), rows.start)
        total += jnp.sum(step * step)
        step_ref[rows, :reach] = step.astype(BF16)
    return total


def apply_step(q_ref, hi_ref, lo_ref, step_ref):
    for rows, reach in halves(q_ref.shape[0]):
        q_new = q_ref[rows, :] - dot(step_ref[rows, :reach], hi_ref[:reach, :])
        q_ref[rows, :] = q_new
        hi, lo = split(q_new)
        hi_ref[rows, :] = hi
        if lo_ref is not None:
            lo_ref[rows, :] = lo


def prepare_steps(most, q2, h2, s2, t2, th2):
    def body(carry):
        count, _ = carry
        worst = 0.0
        for side in range(2):
            worst = jnp.maximum(worst, triangle(h2.at[side], s2.at[side]))
        for side in range(2):
            apply_step(q2.at[side], h2.at[side], None, s2.at[side])
            apply_step(t2.at[side], th2.at[side], None, s2.at[side])
        return count + 1, worst

    lax.while_loop(
        lambda carry: (carry[0] < most) & (carry[1] > START_BOUND),
        body,
        (jnp.int32(0), jnp.float32(1e30)),
    )


def own_flag(order_ref, refresh_ref):
    owners = lax.axis_size("fsdp")
    block = order_ref[lax.axis_index("replica") * owners + lax.axis_index("fsdp")]
    flag = block == refresh_ref[0]
    for j in range(1, refresh_ref.shape[0]):
        flag |= block == refresh_ref[j]
    return flag


def start_copies(pairs, sems):
    copies = [pltpu.make_async_copy(src, dst, sems.at[i]) for i, (src, dst) in enumerate(pairs)]
    for copy in copies:
        copy.start()
    return copies


def wait_copies(copies):
    for copy in copies:
        copy.wait()


def prepare_first(order_ref, refresh_ref, lf_hbm, rf_hbm, lb_hbm, rb_hbm, h2, th2,
                  q2, t2, s2, f2, b2, sems):

    @pl.when(own_flag(order_ref, refresh_ref))
    def _():
        copies = start_copies(
            [(lf_hbm, f2.at[0]), (lb_hbm, b2.at[0]), (rf_hbm, f2.at[1]), (rb_hbm, b2.at[1])], sems
        )
        width = lf_hbm.shape[0]
        eye = (
            lax.broadcasted_iota(jnp.int32, (width, width), 0)
            == lax.broadcasted_iota(jnp.int32, (width, width), 1)
        )
        wait_copies(copies)
        for side in range(2):
            p = dot(f2[side].astype(BF16), b2[side].astype(BF16))
            scale = lax.rsqrt(jnp.sum(p * p, axis=0, keepdims=True))
            y = (p * scale).astype(BF16)
            h2[side] = y.T
            gram = dot(h2[side], h2[side], NT)
            reach = jnp.max(jnp.sum(jnp.abs(gram), axis=0, keepdims=True), axis=1, keepdims=True)
            factor_all = lax.rsqrt(0.5 * reach)
            start = h2[side].astype(F32) * factor_all
            q2[side] = start
            h2[side] = start.astype(BF16)
            diagonal = jnp.where(eye, scale * (factor_all / 0.95), 0.0)
            t2[side] = diagonal
            th2[side] = diagonal.astype(BF16)
        prepare_steps(FIRST_STEPS, q2, h2, s2, t2, th2)


def prepare_more(order_ref, refresh_ref, h_ref, th_ref, h2, th2, q2, t2, s2):
    @pl.when(own_flag(order_ref, refresh_ref))
    def _():
        for side in range(2):
            h2[side] = h_ref[side]
            th2[side] = th_ref[side]
            q2[side] = h_ref[side].astype(F32)
            t2[side] = th_ref[side].astype(F32)
        prepare_steps(MORE_STEPS, q2, h2, s2, t2, th2)


def prepare_last(order_ref, refresh_ref, h_ref, th_ref, lf_hbm, rf_hbm, lb_hbm, rb_hbm,
                 w2, q_out, h2, th2, q2, t2, s2, f2, b2, sems):

    @pl.when(own_flag(order_ref, refresh_ref))
    def _():
        copies = start_copies(
            [(lf_hbm, f2.at[0]), (lb_hbm, b2.at[0]), (rf_hbm, f2.at[1]), (rb_hbm, b2.at[1])], sems
        )
        for side in range(2):
            h2[side] = h_ref[side]
            th2[side] = th_ref[side]
            q2[side] = h_ref[side].astype(F32)
            t2[side] = th_ref[side].astype(F32)
        prepare_steps(LAST_STEPS, q2, h2, s2, t2, th2)
        wait_copies(copies)
        for side in range(2):
            basis_hi, basis_lo = split(b2[side].T)
            w = dot(th2[side], basis_hi) + dot(th2[side], basis_lo)
            w_hi, w_lo = split(w)
            factor_hi, factor_lo = split(f2[side])
            w2[side] = w_hi
            q_out[side] = 0.95 * (
                dot(w_hi, factor_hi, NT) + dot(w_hi, factor_lo, NT) + dot(w_lo, factor_hi, NT)
            )


def gram_schmidt(q_ref, hi_ref, lo_ref):
    width = q_ref.shape[0]
    rows = lax.broadcasted_iota(jnp.int32, (width, 1), 0)

    def one(at, carry):
        row = q_ref[pl.ds(at, 1), :]
        row = row * lax.rsqrt(jnp.sum(row * row))
        q = q_ref[...]
        share = jnp.sum(q * row, axis=1, keepdims=True)
        q_ref[...] = q - jnp.where(rows > at, share, 0.0) * row
        q_ref[pl.ds(at, 1), :] = row
        return carry

    lax.fori_loop(0, width, one, 0)
    store_split(hi_ref, lo_ref, q_ref[...])


def gather_kernel(steps, order_ref, parts_hbm, *rest):
    outs, sems = rest[:-1], rest[-1]
    replicas = lax.axis_size("replica")
    at = lax.axis_index("replica")
    slots, _, half = outs[0].shape
    pairs = []
    for number, step in enumerate(steps):
        for part in range(2):
            ahead = (2 * replicas - 1 - step) if part == 0 else (1 + step)
            first = lax.rem(at + ahead, replicas) * slots
            for i in range(slots):
                source = parts_hbm.at[order_ref[first + i], :, pl.ds(part * half, half)]
                pairs.append((source, outs[2 * number + part].at[i]))
    wait_copies(start_copies(pairs, sems))


def add_kernel(got_ref, own_ref, out_ref):
    out_ref[...] = (got_ref[...].astype(F32) + own_ref[...].astype(F32)).astype(BF16)


def place_kernel(order_ref, rows_ref, out_hbm, sems):
    slots = rows_ref.shape[0]
    first = lax.axis_index("replica") * slots
    wait_copies(start_copies(
        [(rows_ref.at[i], out_hbm.at[order_ref[first + i] - first]) for i in range(slots)], sems
    ))


def update_kernel(order_ref, refresh_ref, first_ref, last_ref, w_ref, q_ref,
                  lf_hbm, rf_hbm, lb_hbm, rb_hbm, moment_hbm, second_hbm,
                  update_ref, left_hbm, right_hbm,
                  q2, h2, l2, s2, f2, b2, moment_ref, second_ref, new2, grad_ref, sems, out_sems):
    flag = own_flag(order_ref, refresh_ref)
    copies = start_copies(
        [(lf_hbm, f2.at[0]), (rf_hbm, f2.at[1]), (lb_hbm, b2.at[0]), (rb_hbm, b2.at[1]),
         (moment_hbm, moment_ref), (second_hbm, second_ref)],
        sems,
    )
    width = grad_ref.shape[0]
    weight = 0.05 / width
    grad_ref[:, : width // 2] = first_ref[...]
    grad_ref[:, width // 2 :] = last_ref[...]
    grad = grad_ref[...]
    grad_t = grad.T
    new2[0] = weight * dot(grad, grad, NT)
    new2[1] = weight * dot(grad_t, grad_t, NT)

    wait_copies(copies[:4])
    for side in range(2):
        new2[side] += 0.95 * f2[side]
    out_copies = start_copies([(new2.at[0], left_hbm), (new2.at[1], right_hbm)], out_sems)

    @pl.when(jnp.logical_not(flag))
    def _():
        store_split(h2.at[0], l2.at[0], b2[0].T)
        store_split(h2.at[1], l2.at[1], b2[1].T)

    @pl.when(flag)
    def _():
        part = dot(w_ref[0], grad).astype(BF16)
        q_left = q_ref[0] + weight * dot(part, grad, NT)
        part = dot(w_ref[1], grad, NT).astype(BF16)
        q_right = q_ref[1] + weight * dot(part, grad)
        q2[0] = q_left
        h2[0] = q_left.astype(BF16)
        q2[1] = q_right
        h2[1] = q_right.astype(BF16)

        def body(carry):
            count, _ = carry
            worst = 0.0
            for side in range(2):
                worst = jnp.maximum(worst, triangle(h2.at[side], s2.at[side]))
            for side in range(2):
                apply_step(q2.at[side], h2.at[side], l2.at[side], s2.at[side])
            return count + 1, worst

        _, worst = lax.while_loop(
            lambda carry: (carry[0] < 20) & (carry[1] > END_BOUND),
            body,
            (jnp.int32(0), jnp.float32(1e30)),
        )

        @pl.when(jnp.logical_not(worst <= END_BOUND))
        def _():
            for side in range(2):
                q2[side] = lax.dot_general(
                    new2[side], b2[side], NN,
                    precision=lax.Precision.HIGHEST, preferred_element_type=F32,
                ).T
                gram_schmidt(q2.at[side], h2.at[side], l2.at[side])

    left_hi = h2[0]
    left_lo = l2[0]
    right_hi = h2[1]
    right_lo = l2[1]
    wait_copies(copies[4:])
    rotated = dot(dot(left_hi, grad).astype(BF16), right_hi, NT)
    moment_hi, moment_lo = split(0.9 * moment_ref[...] + 0.1 * grad.astype(F32))
    part = dot(left_hi, moment_hi) + dot(left_lo, moment_hi) + dot(left_hi, moment_lo)
    part_hi, part_lo = split(part)
    moment = (
        dot(part_hi, right_hi, NT) + dot(part_hi, right_lo, NT) + dot(part_lo, right_hi, NT)
    )
    second = 0.95 * second_ref[...] + 0.05 * rotated * rotated
    scaled = (moment / (jnp.sqrt(second) + 1e-8)).astype(BF16)
    part = (dot(left_hi.T, scaled) + dot(left_lo.T, scaled)).astype(BF16)
    update_ref[...] = (dot(part, right_hi) + dot(part, right_lo)).astype(BF16)
    wait_copies(out_copies)


SMEM_SPEC = pl.BlockSpec(memory_space=pltpu.SMEM)
VMEM_SPEC = pl.BlockSpec(memory_space=pltpu.VMEM)
HBM_SPEC = pl.BlockSpec(memory_space=pltpu.HBM)


def call(kernel, name, in_smem, in_vmem, in_hbm, out_vmem, out_hbm=(), scratch=(), sems=(), flops=0):
    operands = (*in_smem, *in_vmem, *in_hbm)
    return pl.pallas_call(
        kernel,
        out_shape=[jax.ShapeDtypeStruct(shape, dtype) for shape, dtype in (*out_vmem, *out_hbm)],
        in_specs=[SMEM_SPEC] * len(in_smem) + [VMEM_SPEC] * len(in_vmem) + [HBM_SPEC] * len(in_hbm),
        out_specs=[VMEM_SPEC] * len(out_vmem) + [HBM_SPEC] * len(out_hbm),
        scratch_shapes=[pltpu.VMEM(shape, dtype) for shape, dtype in scratch]
        + [pltpu.SemaphoreType.DMA((count,)) for count in sems],
        compiler_params=pltpu.CompilerParams(vmem_limit_bytes=VMEM_LIMIT),
        cost_estimate=pl.CostEstimate(
            flops=flops,
            bytes_accessed=sum(x.size * x.dtype.itemsize for x in in_vmem),
            transcendentals=0,
        ),
        name=name,
    )(*operands)


def on_device(
    grad_parts,
    moment,
    second_moment,
    left_factor,
    right_factor,
    left_basis,
    right_basis,
    block_order,
    refresh_ids,
):
    replicas = lax.axis_size("replica")
    owners = lax.axis_size("fsdp")
    group_size = grad_parts.shape[1] // replicas
    rows = grad_parts.shape[2]
    width = grad_parts.shape[3]
    square = (width, width)
    pair = (2,) + square
    work = [(pair, F32), (pair, F32), (pair, BF16)]
    loads = [(pair, F32), (pair, F32)]
    slots = (block_order, refresh_ids)
    state_arrays = (left_factor[0], right_factor[0], left_basis[0], right_basis[0])
    steps = replicas - 1

    chunk = ((group_size, rows, width // 2), BF16)

    def gather(name, at_steps):
        return call(
            functools.partial(gather_kernel, at_steps), name, (block_order,), (), (grad_parts[0],),
            [chunk] * (2 * len(at_steps)), sems=[2 * group_size * len(at_steps)],
        )

    def stage(at, tied, state):
        flops = 40 * width**3
        if at == 0:
            return call(
                prepare_first, "prepare_first", (tied, refresh_ids), (), state_arrays,
                [(pair, BF16)] * 2, scratch=work + loads, sems=[4], flops=flops,
            )
        if at == 1:
            return call(
                prepare_more, "prepare_more", (tied, refresh_ids), state, (),
                [(pair, BF16)] * 2, scratch=work, flops=flops,
            )
        return call(
            prepare_last, "prepare_last", (tied, refresh_ids), state, state_arrays,
            [(pair, BF16), (pair, F32)], scratch=[(pair, BF16)] * 2 + work + loads, sems=[4],
            flops=flops,
        )

    ways = (
        [(i, (i + 1) % replicas) for i in range(replicas)],
        [(i, (i - 1) % replicas) for i in range(replicas)],
    )
    send = list(gather("gather_first", (0,)))
    own = gather("gather_rest", tuple(range(1, replicas)))
    state = None
    for step in range(steps):
        mine = [own[2 * step], own[2 * step + 1]]
        if step < 3:
            tied, send[0] = lax.optimization_barrier((block_order, send[0]))
        got = [lax.ppermute(send[way], "replica", ways[way]) for way in range(2)]
        if step < 3:
            state = stage(step, tied, state)
            mine[0], *state = lax.optimization_barrier((mine[0], *state))
        send = [
            call(add_kernel, ("add_right", "add_left")[way], (), (got[way], mine[way]), (), [chunk])[0]
            for way in range(2)
        ]
    halves_of = [
        lax.all_to_all(send[way], "fsdp", split_axis=0, concat_axis=0, tiled=True).reshape(
            width, width // 2
        )
        for way in range(2)
    ]
    update, left_new, right_new = call(
        update_kernel, "update", slots, (*halves_of, *state),
        (*state_arrays, moment[0], second_moment[0]), [(square, BF16)], [(square, F32)] * 2,
        scratch=[(pair, F32), (pair, BF16), (pair, BF16), (pair, BF16), *loads,
                 (square, F32), (square, F32), (pair, F32), (square, BF16)],
        sems=[6, 2], flops=100 * width**3,
    )
    returned = lax.all_to_all(
        update.reshape(owners, rows, width), "fsdp", split_axis=0, concat_axis=0, tiled=True
    )
    (step_dir,) = call(
        place_kernel, "place", (block_order,), (returned,), (), (),
        [((group_size, rows, width), BF16)], sems=[group_size],
    )
    return step_dir, left_new[None], right_new[None]


def solution(mesh):
    placed = (
        P("replica", None, "fsdp", None),
        P(("replica", "fsdp"), None, None),
        P(("replica", "fsdp"), None, None),
        P(("replica", "fsdp"), None, None),
        P(("replica", "fsdp"), None, None),
        P(("replica", "fsdp"), None, None),
        P(("replica", "fsdp"), None, None),
        P(),
        P(),
    )
    return jax.shard_map(
        on_device,
        mesh=mesh,
        in_specs=placed,
        out_specs=(
            P("replica", "fsdp", None),
            P(("replica", "fsdp"), None, None),
            P(("replica", "fsdp"), None, None),
        ),
        check_vma=False,
    )
```

profile of v0, /device:TPU:0, one launch (start us, length us, event | category | flops | bytes accessed | tf_op | source)
XLA Modules:
  0.0 450.8 jit_solution(4828107863326440546)
XLA Ops:
  0.6 1.6 copy-done
  2.2 0.7 copy-done.1
  2.9 0.8 gather_first.1
  3.7 5.1 %collective-permute-start.3 = (bf16[8,64,256]{2,1,0:T(8,128)(2,1)S(1)}, bf16[8,64,256]{2,1,0:T(8,128)(2,1)S(1)}, u32[]{:S(2)}, u32[]{:S(2)}) collective-permute-start(bf16[8,64,256]{2,1,0:T(8,128)(2,1)S(1)} %get-tuple-element.58), channel_id=1, source_target_pairs={{0,24},{8,0},{16,8},{24,16},{1,25},{9,1},{17,9},{25,17},{2,26},{10... | collective-permute-start | bytes 786440 | tf_op jit(solution)/shard_map/ppermute | solution.py:389
  8.8 1.5 gather_rest.1
  10.3 5.2 %collective-permute-done.3.got_ref = bf16[8,64,256]{2,1,0:T(8,128)(2,1)S(1)} collective-permute-done((bf16[8,64,256]{2,1,0:T(8,128)(2,1)S(1)}, bf16[8,64,256]{2,1,0:T(8,128)(2,1)S(1)}, u32[]{:S(2)}, u32[]{:S(2)}) %collective-permute-start.3) | collective-permute-done | bytes 262176 | tf_op jit(solution)/shard_map/ppermute | solution.py:389
  15.6 4.3 collective-permute-start.4
  20.6 1.5 collective-permute-done.got_ref
  22.2 1.6 collective-permute-start.1
  23.8 2.6 collective-permute-done.4.got_ref
  26.5 3.8 collective-permute-start.5
  30.8 1.0 copy-done.16
  31.8 1.0 copy-done.18
  32.9 6.7 %collective-permute-done.5.got_ref = bf16[8,64,256]{2,1,0:T(8,128)(2,1)S(1)} collective-permute-done((bf16[8,64,256]{2,1,0:T(8,128)(2,1)S(1)}, bf16[8,64,256]{2,1,0:T(8,128)(2,1)S(1)}, u32[]{:S(2)}, u32[]{:S(2)}) %collective-permute-start.5) | collective-permute-done | bytes 262176 | tf_op jit(solution)/shard_map/ppermute | solution.py:389
  39.5 0.8 add_left.5
  40.3 3.4 all-to-all-start.1
  43.8 1.2 copy-done.6
  45.0 1.2 copy-done.9
  46.2 1.2 copy-done.17
  47.4 1.2 copy-done.19
  49.3 1.3 copy-done.14
  50.6 1.0 copy-done.20
  51.7 13.7 %all_to_all.15 = bf16[8,64,256]{2,1,0:T(8,128)(2,1)S(1)} all-to-all(bf16[8,64,256]{2,1,0:T(8,128)(2,1)S(1)} %add_right.5), channel_id=1, replica_groups=mesh['replica'=4,'fsdp'=8] {'fsdp'}, dimensions={0} | all-to-all | bytes 524288 | tf_op jit(solution)/shard_map/all_to_all | solution.py:398
  65.3 1.2 copy-done.7
  66.5 1.2 copy-done.10
  67.8 1.2 copy-done.11
  69.0 1.2 copy-done.12
  70.2 1.6 copy-done.15
  71.8 1.2 copy-done.21
  73.0 6.4 %update.1 = (bf16[512,512]{1,0:T(8,128)(2,1)S(1)}, f32[512,512]{1,0:T(8,128)}, f32[512,512]{1,0:T(8,128)}) custom-call(s32[32]{0:T(128)S(1)} %copy-done.2, s32[3]{0:T(128)S(1)} %copy-done.13, bf16[512,256]{1,0:T(8,128)(2,1)S(1)} %bitcast.16, bf16[512,256]{1,0:T(8,128)(2,1)S(1)} %bitcast.15, bf16[2,512,512]{2,1,0:T(8,128)(2,1)S(1)} %copy-done.21, ...), custom_call_target="tpu_custom_call" | custom-call | flops 13421772800 | bytes 3670016 | tf_op jit(solution)/shard_map/update/pallas_call | solution.py:311
  79.4 369.8 %all_to_all.16.rows_ref = bf16[8,64,512]{2,1,0:T(8,128)(2,1)S(1)} all-to-all(bf16[8,64,512]{2,1,0:T(8,128)(2,1)S(1)} %bitcast.14), channel_id=1, replica_groups=mesh['replica'=4,'fsdp'=8] {'fsdp'}, dimensions={0} | all-to-all | bytes 1048576 | tf_op jit(solution)/shard_map/all_to_all | solution.py:410
  449.2 1.4 place.1
  (41 shorter events, 2.2 us)
Async XLA Ops:
  0.6 1.6 copy-start
  2.2 0.7 copy-start.1
  2.9 17.1 %copy-start.3 = (f32[1,512,512]{2,1,0:T(8,128)S(1)}, f32[1,512,512]{2,1,0:T(8,128)}, u32[]{:S(2)}) copy-start(f32[1,512,512]{2,1,0:T(8,128)} %param.12) | copy-start | bytes 3145732
  2.9 17.1 %copy-start.4 = (f32[1,512,512]{2,1,0:T(8,128)S(1)}, f32[1,512,512]{2,1,0:T(8,128)}, u32[]{:S(2)}) copy-start(f32[1,512,512]{2,1,0:T(8,128)} %param.13) | copy-start | bytes 3145732
  2.9 17.1 %copy-start.5 = (f32[1,512,512]{2,1,0:T(8,128)S(1)}, f32[1,512,512]{2,1,0:T(8,128)}, u32[]{:S(2)}) copy-start(f32[1,512,512]{2,1,0:T(8,128)} %param.14) | copy-start | bytes 3145732
  2.9 17.1 %copy-start.8 = (f32[1,512,512]{2,1,0:T(8,128)S(1)}, f32[1,512,512]{2,1,0:T(8,128)}, u32[]{:S(2)}) copy-start(f32[1,512,512]{2,1,0:T(8,128)} %param.15) | copy-start | bytes 3145732
  2.9 17.1 %copy-start.13 = (s32[3]{0:T(128)S(1)}, s32[3]{0:T(128)}, u32[]{:S(2)}) copy-start(s32[3]{0:T(128)} %refresh_ref.7) | copy-start | bytes 40
  3.7 11.8 %collective-permute-start.3 = (bf16[8,64,256]{2,1,0:T(8,128)(2,1)S(1)}, bf16[8,64,256]{2,1,0:T(8,128)(2,1)S(1)}, u32[]{:S(2)}, u32[]{:S(2)}) collective-permute-start(bf16[8,64,256]{2,1,0:T(8,128)(2,1)S(1)} %get-tuple-element.58), channel_id=1, source_target_pairs={{0,24},{8,0},{16,8},{24,16},{1,25},{9,1},{17,9},{25,17},{2,26},{10... | collective-permute-start | bytes 786440 | tf_op jit(solution)/shard_map/ppermute | solution.py:389
  8.8 13.3 %collective-permute-start = (bf16[8,64,256]{2,1,0:T(8,128)(2,1)S(1)}, bf16[8,64,256]{2,1,0:T(8,128)(2,1)S(1)}, u32[]{:S(2)}, u32[]{:S(2)}) collective-permute-start(bf16[8,64,256]{2,1,0:T(8,128)(2,1)S(1)} %get-tuple-element.36), channel_id=1, source_target_pairs={{0,8},{8,16},{16,24},{24,0},{1,9},{9,17},{17,25},{25,1},{2,10},{10... | collective-permute-start | bytes 786440 | tf_op jit(solution)/shard_map/ppermute | solution.py:389
  15.6 10.8 %collective-permute-start.4 = (bf16[8,64,256]{2,1,0:T(8,128)(2,1)S(1)}, bf16[8,64,256]{2,1,0:T(8,128)(2,1)S(1)}, u32[]{:S(2)}, u32[]{:S(2)}) collective-permute-start(bf16[8,64,256]{2,1,0:T(8,128)(2,1)S(1)} %add_left.3), channel_id=1, source_target_pairs={{0,24},{8,0},{16,8},{24,16},{1,25},{9,1},{17,9},{25,17},{2,26},{10... | collective-permute-start | bytes 786440 | tf_op jit(solution)/shard_map/ppermute | solution.py:389
  22.2 10.6 %collective-permute-start.1 = (bf16[8,64,256]{2,1,0:T(8,128)(2,1)S(1)}, bf16[8,64,256]{2,1,0:T(8,128)(2,1)S(1)}, u32[]{:S(2)}, u32[]{:S(2)}) collective-permute-start(bf16[8,64,256]{2,1,0:T(8,128)(2,1)S(1)} %add_right.3), channel_id=1, source_target_pairs={{0,8},{8,16},{16,24},{24,0},{1,9},{9,17},{17,25},{25,1},{2,10},{10... | collective-permute-start | bytes 786440 | tf_op jit(solution)/shard_map/ppermute | solution.py:389
  26.5 13.1 %collective-permute-start.5 = (bf16[8,64,256]{2,1,0:T(8,128)(2,1)S(1)}, bf16[8,64,256]{2,1,0:T(8,128)(2,1)S(1)}, u32[]{:S(2)}, u32[]{:S(2)}) collective-permute-start(bf16[8,64,256]{2,1,0:T(8,128)(2,1)S(1)} %add_left.4), channel_id=1, source_target_pairs={{0,24},{8,0},{16,8},{24,16},{1,25},{9,1},{17,9},{25,17},{2,26},{10... | collective-permute-start | bytes 786440 | tf_op jit(solution)/shard_map/ppermute | solution.py:389
  30.8 1.0 copy-start.16
  31.8 1.0 copy-start.18
  32.8 11.0 %copy-start.2 = (s32[32]{0:T(128)S(1)}, s32[32]{0:T(128)}, u32[]{:S(2)}) copy-start(s32[32]{0:T(128)} %order_ref.10) | copy-start | bytes 388
  32.8 18.7 %collective-permute-start.2 = (bf16[8,64,256]{2,1,0:T(8,128)(2,1)S(1)}, bf16[8,64,256]{2,1,0:T(8,128)(2,1)S(1)}, u32[]{:S(2)}, u32[]{:S(2)}) collective-permute-start(bf16[8,64,256]{2,1,0:T(8,128)(2,1)S(1)} %add_right.4), channel_id=1, source_target_pairs={{0,8},{8,16},{16,24},{24,0},{1,9},{9,17},{17,25},{25,1},{2,10},{10... | collective-permute-start | bytes 786440 | tf_op jit(solution)/shard_map/ppermute | solution.py:389
  40.3 11.3 %all-to-all-start.1 = ((bf16[8,64,256]{2,1,0:T(8,128)(2,1)}), bf16[8,64,256]{2,1,0:T(8,128)(2,1)S(1)}, u32[]{:S(2)}, u32[]{:S(2)}) async-start(bf16[8,64,256]{2,1,0:T(8,128)(2,1)} %add_left.5), calls=%async_computation.1 | async-start | bytes 524288 | tf_op jit(solution)/shard_map/all_to_all | solution.py:398
  43.7 1.2 copy-start.6
  45.0 1.2 copy-start.9
  46.2 1.2 copy-start.17
  47.4 1.2 copy-start.19
  49.3 1.3 copy-start.14
  50.6 1.0 copy-start.20
  65.3 1.2 copy-start.7
  66.5 1.2 copy-start.10
  67.8 1.2 copy-start.11
  69.0 1.2 copy-start.12
  70.2 1.6 copy-start.15
  71.8 1.2 copy-start.21
where the time goes:
time: 453 us; the launch traced here: 451 us
  blocking collectives  383 us (85%)
  local copies, waits for them, and re-layouts  19.1 us (4%)
  starting transfers between devices  18.3 us (4%)
  waiting for transfers between devices  16 us (4%)
  Pallas kernels  13 us (3%)
    all_to_all x1, blocking collectives, on_device(): lax.all_to_all(update.reshape(owners, rows, width), 'fsdp', split_axis=0,...  370 us
    unnamed x44, local copies, waits for them, and re-layouts  19.1 us
    ppermute x6, waiting for transfers between devices, on_device(): got = [lax.ppermute(send[way], 'replica', ways[way]) for way in range(2)]  16 us
    ppermute x6, starting transfers between devices, on_device(): got = [lax.ppermute(send[way], 'replica', ways[way]) for way in range(2)]  14.9 us
    all_to_all x1, blocking collectives, on_device(): lax.all_to_all(send[way], 'fsdp', split_axis=0, concat_axis=0, tiled=True)  13.7 us
    pallas_call x13, Pallas kernels, call(): pl.pallas_call(kernel, out_shape=[jax.ShapeDtypeStruct(shape, dtype) for...  13 us
  transfers between devices with their start and end apart: 7, of which 4 were waited for; matrix products, arithmetic and copies ran while one was open for 0% of the time, Pallas kernels for 1%

commit v1 on v0

--- a/solution.py
+++ b/solution.py
@@ -210,6 +210,12 @@
     out_ref[...] = (got_ref[...].astype(F32) + own_ref[...].astype(F32)).astype(BF16)
 
 
+def finish_kernel(got_right_ref, got_left_ref, own_right_ref, own_left_ref, out_ref):
+    half = got_right_ref.shape[2]
+    add_kernel(got_right_ref, own_right_ref, out_ref.at[:, :, :half])
+    add_kernel(got_left_ref, own_left_ref, out_ref.at[:, :, half:])
+
+
 def place_kernel(order_ref, rows_ref, out_hbm, sems):
     slots = rows_ref.shape[0]
     first = lax.axis_index("replica") * slots
@@ -218,10 +224,10 @@
     ))
 
 
-def update_kernel(order_ref, refresh_ref, first_ref, last_ref, w_ref, q_ref,
+def update_kernel(order_ref, refresh_ref, grad_ref, w_ref, q_ref,
                   lf_hbm, rf_hbm, lb_hbm, rb_hbm, moment_hbm, second_hbm,
                   update_ref, left_hbm, right_hbm,
-                  q2, h2, l2, s2, f2, b2, moment_ref, second_ref, new2, grad_ref, sems, out_sems):
+                  q2, h2, l2, s2, f2, b2, moment_ref, second_ref, new2, sems, out_sems):
     flag = own_flag(order_ref, refresh_ref)
     copies = start_copies(
         [(lf_hbm, f2.at[0]), (rf_hbm, f2.at[1]), (lb_hbm, b2.at[0]), (rb_hbm, b2.at[1]),
@@ -230,8 +236,6 @@
     )
     width = grad_ref.shape[0]
     weight = 0.05 / width
-    grad_ref[:, : width // 2] = first_ref[...]
-    grad_ref[:, width // 2 :] = last_ref[...]
     grad = grad_ref[...]
     grad_t = grad.T
     new2[0] = weight * dot(grad, grad, NT)
@@ -390,21 +394,21 @@
         if step < 3:
             state = stage(step, tied, state)
             mine[0], *state = lax.optimization_barrier((mine[0], *state))
+        if step == steps - 1:
+            break
         send = [
             call(add_kernel, ("add_right", "add_left")[way], (), (got[way], mine[way]), (), [chunk])[0]
             for way in range(2)
         ]
-    halves_of = [
-        lax.all_to_all(send[way], "fsdp", split_axis=0, concat_axis=0, tiled=True).reshape(
-            width, width // 2
-        )
-        for way in range(2)
-    ]
+    (summed,) = call(
+        finish_kernel, "finish", (), (*got, *mine), (), [((group_size, rows, width), BF16)]
+    )
+    gradient = lax.all_to_all(summed, "fsdp", split_axis=0, concat_axis=0, tiled=True)
     update, left_new, right_new = call(
-        update_kernel, "update", slots, (*halves_of, *state),
+        update_kernel, "update", slots, (gradient.reshape(square), *state),
         (*state_arrays, moment[0], second_moment[0]), [(square, BF16)], [(square, F32)] * 2,
         scratch=[(pair, F32), (pair, BF16), (pair, BF16), (pair, BF16), *loads,
-                 (square, F32), (square, F32), (pair, F32), (square, BF16)],
+                 (square, F32), (square, F32), (pair, F32)],
         sems=[6, 2], flops=100 * width**3,
     )
     returned = lax.all_to_all(

time: 453 us -> 437 us (0.965)
  local copies, waits for them, and re-layouts: 19.1 us -> 2.27 us
  waiting for transfers between devices: 16 us -> 24.8 us
  starting transfers between devices: 18.3 us -> 13.2 us
    unnamed x44 -> x18, local copies, waits for them, and re-layouts: 19.1 us -> 2.27 us
    ppermute x6, waiting for transfers between devices: 16 us -> 24.8 us  [on_device(): got = [lax.ppermute(send[way], 'replica', ways[way]) for way in range(2)]]
    pallas_call x13 -> x12, Pallas kernels: 13 us -> 12.3 us  [call(): pl.pallas_call(kernel, out_shape=[jax.ShapeDtypeStruct(shape, dtype) for...]
  transfers between devices with their start and end apart: 7 -> 6, of which waited for: 4 -> 5; matrix products, arithmetic and copies ran while one was open for 0% -> 0% of each run, Pallas kernels for 1% -> 1%
where the time goes in v1:
time: 437 us; the launch traced here: 436 us
  blocking collectives  383 us (88%)
  waiting for transfers between devices  24.8 us (6%)
  starting transfers between devices  13.2 us (3%)
  Pallas kernels  12.3 us (3%)
    all_to_all x1, blocking collectives, on_device(): lax.all_to_all(update.reshape(owners, rows, width), 'fsdp', split_axis=0,...  370 us
    ppermute x6, waiting for transfers between devices, on_device(): got = [lax.ppermute(send[way], 'replica', ways[way]) for way in range(2)]  24.8 us
    ppermute x6, starting transfers between devices, on_device(): got = [lax.ppermute(send[way], 'replica', ways[way]) for way in range(2)]  13.2 us
    all_to_all x1, blocking collectives, on_device(): lax.all_to_all(summed, 'fsdp', split_axis=0, concat_axis=0, tiled=True)  13 us
    pallas_call x12, Pallas kernels, call(): pl.pallas_call(kernel, out_shape=[jax.ShapeDtypeStruct(shape, dtype) for...  12.3 us
  transfers between devices with their start and end apart: 6, of which 5 were waited for; matrix products, arithmetic and copies ran while one was open for 0% of the time, Pallas kernels for 1%

profile of v1, /device:TPU:0, one launch (start us, length us, event | category | flops | bytes accessed | tf_op | source)
XLA Modules:
  0.0 436.2 jit_solution(13198477255651915128)
XLA Ops:
  0.6 1.6 copy-done
  2.2 0.7 copy-done.1
  2.9 0.8 gather_first.1
  3.7 3.1 collective-permute-start
  6.8 2.1 collective-permute-start.3
  8.9 1.5 gather_rest.1
  10.4 0.0 copy-done.2
  10.4 0.0 copy-done.3
  10.5 0.6 prepare_first.1
  11.1 9.1 %collective-permute-done.3.got_ref = bf16[8,64,256]{2,1,0:T(8,128)(2,1)S(1)} collective-permute-done((bf16[8,64,256]{2,1,0:T(8,128)(2,1)S(1)}, bf16[8,64,256]{2,1,0:T(8,128)(2,1)S(1)}, u32[]{:S(2)}, u32[]{:S(2)}) %collective-permute-start.3) | collective-permute-done | bytes 262176 | tf_op jit(solution)/shard_map/ppermute | solution.py:393
  20.2 0.1 add_left.2
  20.3 2.3 collective-permute-start.4
  22.6 0.0 collective-permute-done.got_ref
  22.6 0.1 add_right.2
  22.6 0.1 collective-permute-start.1
  22.7 0.6 prepare_more.1
  23.3 6.4 %collective-permute-done.4.got_ref = bf16[8,64,256]{2,1,0:T(8,128)(2,1)S(1)} collective-permute-done((bf16[8,64,256]{2,1,0:T(8,128)(2,1)S(1)}, bf16[8,64,256]{2,1,0:T(8,128)(2,1)S(1)}, u32[]{:S(2)}, u32[]{:S(2)}) %collective-permute-start.4) | collective-permute-done | bytes 262176 | tf_op jit(solution)/shard_map/ppermute | solution.py:393
  29.7 0.1 add_left.3
  29.7 4.0 collective-permute-start.5
  33.7 2.1 collective-permute-done.1.got_ref
  35.8 0.1 add_right.3
  35.9 1.7 collective-permute-start.2
  37.6 0.6 prepare_last.1
  38.2 0.0 copy-start.6
  38.2 0.0 copy-start.7
  38.2 4.2 collective-permute-done.5.got_left_ref
  42.4 3.0 collective-permute-done.2.got_right_ref
  45.4 0.1 finish.1
  45.5 13.0 %all_to_all.10 = bf16[8,64,512]{2,1,0:T(8,128)(2,1)S(1)} all-to-all(bf16[8,64,512]{2,1,0:T(8,128)(2,1)S(1)} %finish.1), channel_id=1, replica_groups=mesh['replica'=4,'fsdp'=8] {'fsdp'}, dimensions={0} | all-to-all | bytes 1048576 | tf_op jit(solution)/shard_map/all_to_all | solution.py:406
  58.5 6.4 %update.1 = (bf16[512,512]{1,0:T(8,128)(2,1)S(1)}, f32[512,512]{1,0:T(8,128)}, f32[512,512]{1,0:T(8,128)}) custom-call(s32[32]{0:T(128)S(1)} %copy-done.1, s32[3]{0:T(128)S(1)} %copy-done.8, bf16[512,512]{1,0:T(8,128)(2,1)S(1)} %bitcast.13, bf16[2,512,512]{2,1,0:T(8,128)(2,1)S(1)} %get-tuple-element.62.w_ref, f32[2,512,512]{2,1,0:T(8,128)S(1)} %get-tuple-element.63.q_ref, ...), custom_call_target="tpu_custom_call" | custom-call | flops 13421772800 | bytes 3670016 | tf_op jit(solution)/shard_map/update/pallas_call | solution.py:315
  64.9 369.7 %all_to_all.11.rows_ref = bf16[8,64,512]{2,1,0:T(8,128)(2,1)S(1)} all-to-all(bf16[8,64,512]{2,1,0:T(8,128)(2,1)S(1)} %bitcast.14), channel_id=1, replica_groups=mesh['replica'=4,'fsdp'=8] {'fsdp'}, dimensions={0} | all-to-all | bytes 1048576 | tf_op jit(solution)/shard_map/all_to_all | solution.py:414
  434.7 1.4 place.1
  (12 shorter events, 0.0 us)
Async XLA Ops:
  0.6 1.6 copy-start
  2.2 0.7 copy-start.1
  2.9 7.5 %copy-start.2 = (f32[1,512,512]{2,1,0:T(8,128)S(1)}, f32[1,512,512]{2,1,0:T(8,128)}, u32[]{:S(2)}) copy-start(f32[1,512,512]{2,1,0:T(8,128)} %param.12) | copy-start | bytes 3145732
  2.9 7.5 %copy-start.3 = (f32[1,512,512]{2,1,0:T(8,128)S(1)}, f32[1,512,512]{2,1,0:T(8,128)}, u32[]{:S(2)}) copy-start(f32[1,512,512]{2,1,0:T(8,128)} %param.13) | copy-start | bytes 3145732
  2.9 7.5 %copy-start.4 = (f32[1,512,512]{2,1,0:T(8,128)S(1)}, f32[1,512,512]{2,1,0:T(8,128)}, u32[]{:S(2)}) copy-start(f32[1,512,512]{2,1,0:T(8,128)} %param.14) | copy-start | bytes 3145732
  2.9 7.6 %copy-start.5 = (f32[1,512,512]{2,1,0:T(8,128)S(1)}, f32[1,512,512]{2,1,0:T(8,128)}, u32[]{:S(2)}) copy-start(f32[1,512,512]{2,1,0:T(8,128)} %param.15) | copy-start | bytes 3145732
  2.9 7.6 %copy-start.8 = (s32[3]{0:T(128)S(1)}, s32[3]{0:T(128)}, u32[]{:S(2)}) copy-start(s32[3]{0:T(128)} %refresh_ref.7) | copy-start | bytes 40
  3.7 18.8 %collective-permute-start = (bf16[8,64,256]{2,1,0:T(8,128)(2,1)S(1)}, bf16[8,64,256]{2,1,0:T(8,128)(2,1)S(1)}, u32[]{:S(2)}, u32[]{:S(2)}) collective-permute-start(bf16[8,64,256]{2,1,0:T(8,128)(2,1)S(1)} %get-tuple-element.36), channel_id=1, source_target_pairs={{0,8},{8,16},{16,24},{24,0},{1,9},{9,17},{17,25},{25,1},{2,10},{10... | collective-permute-start | bytes 786440 | tf_op jit(solution)/shard_map/ppermute | solution.py:393
  6.8 13.4 %collective-permute-start.3 = (bf16[8,64,256]{2,1,0:T(8,128)(2,1)S(1)}, bf16[8,64,256]{2,1,0:T(8,128)(2,1)S(1)}, u32[]{:S(2)}, u32[]{:S(2)}) collective-permute-start(bf16[8,64,256]{2,1,0:T(8,128)(2,1)S(1)} %get-tuple-element.51), channel_id=1, source_target_pairs={{0,24},{8,0},{16,8},{24,16},{1,25},{9,1},{17,9},{25,17},{2,26},{10... | collective-permute-start | bytes 786440 | tf_op jit(solution)/shard_map/ppermute | solution.py:393
  20.3 9.4 %collective-permute-start.4 = (bf16[8,64,256]{2,1,0:T(8,128)(2,1)S(1)}, bf16[8,64,256]{2,1,0:T(8,128)(2,1)S(1)}, u32[]{:S(2)}, u32[]{:S(2)}) collective-permute-start(bf16[8,64,256]{2,1,0:T(8,128)(2,1)S(1)} %add_left.2), channel_id=1, source_target_pairs={{0,24},{8,0},{16,8},{24,16},{1,25},{9,1},{17,9},{25,17},{2,26},{10... | collective-permute-start | bytes 786440 | tf_op jit(solution)/shard_map/ppermute | solution.py:393
  22.6 13.2 %collective-permute-start.1 = (bf16[8,64,256]{2,1,0:T(8,128)(2,1)S(1)}, bf16[8,64,256]{2,1,0:T(8,128)(2,1)S(1)}, u32[]{:S(2)}, u32[]{:S(2)}) collective-permute-start(bf16[8,64,256]{2,1,0:T(8,128)(2,1)S(1)} %add_right.2), channel_id=1, source_target_pairs={{0,8},{8,16},{16,24},{24,0},{1,9},{9,17},{17,25},{25,1},{2,10},{10... | collective-permute-start | bytes 786440 | tf_op jit(solution)/shard_map/ppermute | solution.py:393
  29.7 12.7 %collective-permute-start.5 = (bf16[8,64,256]{2,1,0:T(8,128)(2,1)S(1)}, bf16[8,64,256]{2,1,0:T(8,128)(2,1)S(1)}, u32[]{:S(2)}, u32[]{:S(2)}) collective-permute-start(bf16[8,64,256]{2,1,0:T(8,128)(2,1)S(1)} %add_left.3), channel_id=1, source_target_pairs={{0,24},{8,0},{16,8},{24,16},{1,25},{9,1},{17,9},{25,17},{2,26},{10... | collective-permute-start | bytes 786440 | tf_op jit(solution)/shard_map/ppermute | solution.py:393
  35.9 9.5 %collective-permute-start.2 = (bf16[8,64,256]{2,1,0:T(8,128)(2,1)S(1)}, bf16[8,64,256]{2,1,0:T(8,128)(2,1)S(1)}, u32[]{:S(2)}, u32[]{:S(2)}) collective-permute-start(bf16[8,64,256]{2,1,0:T(8,128)(2,1)S(1)} %add_right.3), channel_id=1, source_target_pairs={{0,8},{8,16},{16,24},{24,0},{1,9},{9,17},{17,25},{25,1},{2,10},{10... | collective-permute-start | bytes 786440 | tf_op jit(solution)/shard_map/ppermute | solution.py:393
  38.2 20.3 %copy-start.6 = (f32[1,512,512]{2,1,0:T(8,128)S(1)}, f32[1,512,512]{2,1,0:T(8,128)}, u32[]{:S(2)}) copy-start(f32[1,512,512]{2,1,0:T(8,128)} %param.10) | copy-start | bytes 3145732
  38.2 20.3 %copy-start.7 = (f32[1,512,512]{2,1,0:T(8,128)S(1)}, f32[1,512,512]{2,1,0:T(8,128)}, u32[]{:S(2)}) copy-start(f32[1,512,512]{2,1,0:T(8,128)} %param.11) | copy-start | bytes 3145732

commit v2 on v1

--- a/solution.py
+++ b/solution.py
@@ -12,13 +12,10 @@
 NN = (((1,), (0,)), ((), ()))
 NT = (((1,), (1,)), ((), ()))
 VMEM_LIMIT = 24 * 1024 * 1024
+VMEM_MOST = 56 * 1024 * 1024
 
 START_BOUND = 4.0
 END_BOUND = 0.016
-
-FIRST_STEPS = 4
-MORE_STEPS = 5
-LAST_STEPS = 16
 
 
 def dot(a, b, form=NN):
@@ -66,6 +63,20 @@
             lo_ref[rows, :] = lo
 
 
+def boosted_steps(number, q2, h2, s2, t2, th2):
+    for _ in range(number):
+        for side in range(2):
+            triangle(h2.at[side], s2.at[side])
+        for side in range(2):
+            for full, low in ((q2, h2), (t2, th2)):
+                for rows, reach in halves(q2.shape[1]):
+                    new = 1.3 * full[side, rows, :] - 1.4 * dot(
+                        s2[side, rows, :reach], low[side, :reach, :]
+                    )
+                    full[side, rows, :] = new
+                    low[side, rows, :] = new.astype(BF16)
+
+
 def prepare_steps(most, q2, h2, s2, t2, th2):
     def body(carry):
         count, _ = carry
@@ -105,8 +116,7 @@
         copy.wait()
 
 
-def prepare_first(order_ref, refresh_ref, lf_hbm, rf_hbm, lb_hbm, rb_hbm, h2, th2,
-                  q2, t2, s2, f2, b2, sems):
+def prepare_start(order_ref, refresh_ref, lf_hbm, rf_hbm, lb_hbm, rb_hbm, h2, th2, f2, b2, sems):
 
     @pl.when(own_flag(order_ref, refresh_ref))
     def _():
@@ -118,53 +128,53 @@
             lax.broadcasted_iota(jnp.int32, (width, width), 0)
             == lax.broadcasted_iota(jnp.int32, (width, width), 1)
         )
-        wait_copies(copies)
-        for side in range(2):
+        for side in range(2):
+            wait_copies(copies[2 * side : 2 * side + 2])
             p = dot(f2[side].astype(BF16), b2[side].astype(BF16))
             scale = lax.rsqrt(jnp.sum(p * p, axis=0, keepdims=True))
             y = (p * scale).astype(BF16)
-            h2[side] = y.T
-            gram = dot(h2[side], h2[side], NT)
-            reach = jnp.max(jnp.sum(jnp.abs(gram), axis=0, keepdims=True), axis=1, keepdims=True)
-            factor_all = lax.rsqrt(0.5 * reach)
-            start = h2[side].astype(F32) * factor_all
-            q2[side] = start
-            h2[side] = start.astype(BF16)
-            diagonal = jnp.where(eye, scale * (factor_all / 0.95), 0.0)
-            t2[side] = diagonal
-            th2[side] = diagonal.astype(BF16)
-        prepare_steps(FIRST_STEPS, q2, h2, s2, t2, th2)
-
-
-def prepare_more(order_ref, refresh_ref, h_ref, th_ref, h2, th2, q2, t2, s2):
+            gram = dot(y.T, y).astype(BF16)
+            square = jnp.abs(dot(gram, gram))
+            reach = jnp.max(jnp.sum(square, axis=0, keepdims=True), axis=1, keepdims=True)
+            factor_all = lax.rsqrt(0.5 * jnp.sqrt(reach))
+            h2[side] = (y.astype(F32) * factor_all).astype(BF16).T
+            th2[side] = jnp.where(eye, scale * (factor_all / 0.95), 0.0).astype(BF16)
+
+
+def load_state(h_ref, th_ref, h2, th2, q2, t2):
+    for side in range(2):
+        h2[side] = h_ref[side]
+        th2[side] = th_ref[side]
+        q2[side] = h_ref[side].astype(F32)
+        t2[side] = th_ref[side].astype(F32)
+
+
+def prepare_boost(order_ref, refresh_ref, h_ref, th_ref, h2, th2, q2, t2, s2):
     @pl.when(own_flag(order_ref, refresh_ref))
     def _():
-        for side in range(2):
-            h2[side] = h_ref[side]
-            th2[side] = th_ref[side]
-            q2[side] = h_ref[side].astype(F32)
-            t2[side] = th_ref[side].astype(F32)
-        prepare_steps(MORE_STEPS, q2, h2, s2, t2, th2)
+        load_state(h_ref, th_ref, h2, th2, q2, t2)
+        boosted_steps(2, q2, h2, s2, t2, th2)
+
+
+def prepare_more(most, order_ref, refresh_ref, h_ref, th_ref, h2, th2, q2, t2, s2):
+    @pl.when(own_flag(order_ref, refresh_ref))
+    def _():
+        load_state(h_ref, th_ref, h2, th2, q2, t2)
+        prepare_steps(most, q2, h2, s2, t2, th2)
 
 
 def prepare_last(order_ref, refresh_ref, h_ref, th_ref, lf_hbm, rf_hbm, lb_hbm, rb_hbm,
-                 w2, q_out, h2, th2, q2, t2, s2, f2, b2, sems):
+                 w2, q_out, f2, b2, sems):
 
     @pl.when(own_flag(order_ref, refresh_ref))
     def _():
         copies = start_copies(
-            [(lf_hbm, f2.at[0]), (lb_hbm, b2.at[0]), (rf_hbm, f2.at[1]), (rb_hbm, b2.at[1])], sems
-        )
-        for side in range(2):
-            h2[side] = h_ref[side]
-            th2[side] = th_ref[side]
-            q2[side] = h_ref[side].astype(F32)
-            t2[side] = th_ref[side].astype(F32)
-        prepare_steps(LAST_STEPS, q2, h2, s2, t2, th2)
-        wait_copies(copies)
-        for side in range(2):
+            [(lb_hbm, b2.at[0]), (lf_hbm, f2.at[0]), (rb_hbm, b2.at[1]), (rf_hbm, f2.at[1])], sems
+        )
+        for side in range(2):
+            wait_copies(copies[2 * side : 2 * side + 2])
             basis_hi, basis_lo = split(b2[side].T)
-            w = dot(th2[side], basis_hi) + dot(th2[side], basis_lo)
+            w = dot(th_ref[side], basis_hi) + dot(th_ref[side], basis_lo)
             w_hi, w_lo = split(w)
             factor_hi, factor_lo = split(f2[side])
             w2[side] = w_hi
@@ -310,7 +320,8 @@
 HBM_SPEC = pl.BlockSpec(memory_space=pltpu.HBM)
 
 
-def call(kernel, name, in_smem, in_vmem, in_hbm, out_vmem, out_hbm=(), scratch=(), sems=(), flops=0):
+def call(kernel, name, in_smem, in_vmem, in_hbm, out_vmem, out_hbm=(), scratch=(), sems=(), flops=0,
+         limit=VMEM_LIMIT):
     operands = (*in_smem, *in_vmem, *in_hbm)
     return pl.pallas_call(
         kernel,
@@ -319,7 +330,7 @@
         out_specs=[VMEM_SPEC] * len(out_vmem) + [HBM_SPEC] * len(out_hbm),
         scratch_shapes=[pltpu.VMEM(shape, dtype) for shape, dtype in scratch]
         + [pltpu.SemaphoreType.DMA((count,)) for count in sems],
-        compiler_params=pltpu.CompilerParams(vmem_limit_bytes=VMEM_LIMIT),
+        compiler_params=pltpu.CompilerParams(vmem_limit_bytes=limit),
         cost_estimate=pl.CostEstimate(
             flops=flops,
             bytes_accessed=sum(x.size * x.dtype.itemsize for x in in_vmem),
@@ -355,51 +366,56 @@
 
     chunk = ((group_size, rows, width // 2), BF16)
 
-    def gather(name, at_steps):
+    def gather(name, at_steps, limit):
         return call(
             functools.partial(gather_kernel, at_steps), name, (block_order,), (), (grad_parts[0],),
-            [chunk] * (2 * len(at_steps)), sems=[2 * group_size * len(at_steps)],
+            [chunk] * (2 * len(at_steps)), sems=[2 * group_size * len(at_steps)], limit=limit,
         )
 
     def stage(at, tied, state):
-        flops = 40 * width**3
+        flops = 20 * width**3
+        given = (tied, refresh_ids)
         if at == 0:
             return call(
-                prepare_first, "prepare_first", (tied, refresh_ids), (), state_arrays,
-                [(pair, BF16)] * 2, scratch=work + loads, sems=[4], flops=flops,
+                prepare_start, "prepare_start", given, (), state_arrays,
+                [(pair, BF16)] * 2, scratch=loads, sems=[4], flops=flops,
             )
-        if at == 1:
+        if at == 5:
             return call(
-                prepare_more, "prepare_more", (tied, refresh_ids), state, (),
-                [(pair, BF16)] * 2, scratch=work, flops=flops,
+                prepare_last, "prepare_last", given, state, state_arrays,
+                [(pair, BF16), (pair, F32)], scratch=loads, sems=[4], flops=flops,
             )
+        kernel = prepare_boost if at == 1 else functools.partial(prepare_more, 2 if at < 4 else 16)
         return call(
-            prepare_last, "prepare_last", (tied, refresh_ids), state, state_arrays,
-            [(pair, BF16), (pair, F32)], scratch=[(pair, BF16)] * 2 + work + loads, sems=[4],
-            flops=flops,
+            kernel, "prepare_boost" if at == 1 else "prepare_more", given, state, (),
+            [(pair, BF16)] * 2, scratch=work, flops=flops,
         )
 
     ways = (
         [(i, (i + 1) % replicas) for i in range(replicas)],
         [(i, (i - 1) % replicas) for i in range(replicas)],
     )
-    send = list(gather("gather_first", (0,)))
-    own = gather("gather_rest", tuple(range(1, replicas)))
-    state = None
-    for step in range(steps):
-        mine = [own[2 * step], own[2 * step + 1]]
-        if step < 3:
-            tied, send[0] = lax.optimization_barrier((block_order, send[0]))
-        got = [lax.ppermute(send[way], "replica", ways[way]) for way in range(2)]
-        if step < 3:
-            state = stage(step, tied, state)
-            mine[0], *state = lax.optimization_barrier((mine[0], *state))
-        if step == steps - 1:
-            break
-        send = [
-            call(add_kernel, ("add_right", "add_left")[way], (), (got[way], mine[way]), (), [chunk])[0]
-            for way in range(2)
-        ]
+    send = list(gather("gather_first", (0,), VMEM_MOST))
+    own = list(gather("gather_rest", tuple(range(1, replicas)), VMEM_LIMIT))
+    got = [None, None]
+    state = ()
+    for event in range(2 * steps):
+        step, way = divmod(event, 2)
+        if event == 0:
+            tied, *send = lax.optimization_barrier((block_order, *send))
+            got = [lax.ppermute(send[k], "replica", ways[k]) for k in range(2)]
+        if event < 6:
+            state = stage(event, tied, state)
+            own[event], *state = lax.optimization_barrier((own[event], *state))
+        if step < steps - 1:
+            (send[way],) = call(
+                add_kernel, ("add_right", "add_left")[way], (), (got[way], own[event]), (), [chunk]
+            )
+            tied, send[way] = lax.optimization_barrier((block_order, send[way]))
+            got[way] = lax.ppermute(send[way], "replica", ways[way])
+        elif way == 0:
+            tied, got[0] = lax.optimization_barrier((block_order, got[0]))
+    mine = own[-2:]
     (summed,) = call(
         finish_kernel, "finish", (), (*got, *mine), (), [((group_size, rows, width), BF16)]
     )

time: 437 us -> 437 us (level)
    pallas_call x12 -> x15, Pallas kernels: 12.3 us -> 16.3 us  [call(): pl.pallas_call(kernel, out_shape=[jax.ShapeDtypeStruct(shape, dtype) for...]
  transfers between devices with their start and end apart: 6 -> 6, of which waited for: 5 -> 6; matrix products, arithmetic and copies ran while one was open for 0% -> 0% of each run, Pallas kernels for 1% -> 1%
where the time goes in v2:
time: 437 us; the launch traced here: 436 us
  blocking collectives  382 us (87%)
  waiting for transfers between devices  23.7 us (5%)
  Pallas kernels  16.3 us (4%)
  starting transfers between devices  9.06 us (2%)
    all_to_all x1, blocking collectives, on_device(): lax.all_to_all(update.reshape(owners, rows, width), 'fsdp', split_axis=0,...  370 us
    ppermute x4, waiting for transfers between devices, on_device(): got[way] = lax.ppermute(send[way], 'replica', ways[way])  18.5 us
    pallas_call x15, Pallas kernels, call(): pl.pallas_call(kernel, out_shape=[jax.ShapeDtypeStruct(shape, dtype) for...  16.3 us
    all_to_all x1, blocking collectives, on_device(): lax.all_to_all(summed, 'fsdp', split_axis=0, concat_axis=0, tiled=True)  12.6 us
  transfers between devices with their start and end apart: 6, of which 6 were waited for; matrix products, arithmetic and copies ran while one was open for 0% of the time, Pallas kernels for 1%

profile of v2, /device:TPU:0, one launch (start us, length us, event | category | flops | bytes accessed | tf_op | source)
XLA Modules:
  0.0 435.9 jit_solution(2964978754220067969)
XLA Ops:
  0.7 2.7 gather_first.1
  3.4 3.1 collective-permute-start
  6.5 2.1 collective-permute-start.2
  8.6 1.2 copy-done.4
  9.8 1.2 copy-done.6
  11.1 0.6 prepare_start.1
  11.7 1.0 copy-done
  12.6 1.5 gather_rest.1
  14.1 1.8 collective-permute-done.got_ref
  15.9 0.1 add_right.2
  16.0 0.1 collective-permute-start.1
  16.0 0.6 prepare_boost.1
  16.6 3.5 collective-permute-done.2.got_ref
  20.1 0.1 add_left.2
  20.2 3.1 collective-permute-start.4
  23.2 0.6 prepare_more.3
  23.8 5.2 %collective-permute-done.1.got_ref = bf16[8,64,256]{2,1,0:T(8,128)(2,1)S(1)} collective-permute-done((bf16[8,64,256]{2,1,0:T(8,128)(2,1)S(1)}, bf16[8,64,256]{2,1,0:T(8,128)(2,1)S(1)}, u32[]{:S(2)}, u32[]{:S(2)}) %collective-permute-start.1) | collective-permute-done | bytes 262176 | tf_op jit(solution)/shard_map/ppermute | solution.py:415
  29.0 0.1 add_right.3
  29.1 0.1 collective-permute-start.3
  29.1 0.6 prepare_more.4
  29.7 4.9 %collective-permute-done.4.got_ref = bf16[8,64,256]{2,1,0:T(8,128)(2,1)S(1)} collective-permute-done((bf16[8,64,256]{2,1,0:T(8,128)(2,1)S(1)}, bf16[8,64,256]{2,1,0:T(8,128)(2,1)S(1)}, u32[]{:S(2)}, u32[]{:S(2)}) %collective-permute-start.4) | collective-permute-done | bytes 262176 | tf_op jit(solution)/shard_map/ppermute | solution.py:415
  34.6 0.1 add_left.3
  34.7 0.7 collective-permute-start.5
  35.4 0.7 prepare_more.5
  36.2 4.7 %collective-permute-done.3.got_right_ref = bf16[8,64,256]{2,1,0:T(8,128)(2,1)S(1)} collective-permute-done((bf16[8,64,256]{2,1,0:T(8,128)(2,1)S(1)}, bf16[8,64,256]{2,1,0:T(8,128)(2,1)S(1)}, u32[]{:S(2)}, u32[]{:S(2)}) %collective-permute-start.3) | collective-permute-done | bytes 262176 | tf_op jit(solution)/shard_map/ppermute | solution.py:415
  40.8 0.6 prepare_last.1
  41.5 3.7 collective-permute-done.5.got_left_ref
  45.2 0.1 finish.1
  45.3 12.6 %all_to_all.10 = bf16[8,64,512]{2,1,0:T(8,128)(2,1)S(1)} all-to-all(bf16[8,64,512]{2,1,0:T(8,128)(2,1)S(1)} %finish.1), channel_id=1, replica_groups=mesh['replica'=4,'fsdp'=8] {'fsdp'}, dimensions={0} | all-to-all | bytes 1048576 | tf_op jit(solution)/shard_map/all_to_all | solution.py:422
  58.0 6.6 %update.1 = (bf16[512,512]{1,0:T(8,128)(2,1)S(1)}, f32[512,512]{1,0:T(8,128)}, f32[512,512]{1,0:T(8,128)}) custom-call(s32[32]{0:T(128)S(1)} %copy-done.1, s32[3]{0:T(128)S(1)} %copy-done.10, bf16[512,512]{1,0:T(8,128)(2,1)S(1)} %bitcast.13, bf16[2,512,512]{2,1,0:T(8,128)(2,1)S(1)} %get-tuple-element.106.w_ref, f32[2,512,512]{2,1,0:T(8,128)S(1)} %get-tuple-element.107.q_ref, ...), custom_call_target="tpu_custom_call" | custom-call | flops 13421772800 | bytes 3670016 | tf_op jit(solution)/shard_map/update/pallas_call | solution.py:326
  64.6 369.8 %all_to_all.11.rows_ref = bf16[8,64,512]{2,1,0:T(8,128)(2,1)S(1)} all-to-all(bf16[8,64,512]{2,1,0:T(8,128)(2,1)S(1)} %bitcast.14), channel_id=1, replica_groups=mesh['replica'=4,'fsdp'=8] {'fsdp'}, dimensions={0} | all-to-all | bytes 1048576 | tf_op jit(solution)/shard_map/all_to_all | solution.py:430
  434.3 1.4 place.1
  (19 shorter events, 0.0 us)
Async XLA Ops:
  0.6 8.0 %copy-start.1 = (s32[32]{0:T(128)S(1)}, s32[32]{0:T(128)}, u32[]{:S(2)}) copy-start(s32[32]{0:T(128)} %order_ref.13) | copy-start | bytes 388
  0.6 7.9 %copy-start.10 = (s32[3]{0:T(128)S(1)}, s32[3]{0:T(128)}, u32[]{:S(2)}) copy-start(s32[3]{0:T(128)} %refresh_ref.13) | copy-start | bytes 40
  0.7 7.9 %copy-start.3 = (f32[1,512,512]{2,1,0:T(8,128)S(1)}, f32[1,512,512]{2,1,0:T(8,128)}, u32[]{:S(2)}) copy-start(f32[1,512,512]{2,1,0:T(8,128)} %param.13) | copy-start | bytes 3145732
  0.7 7.9 %copy-start.2 = (f32[1,512,512]{2,1,0:T(8,128)S(1)}, f32[1,512,512]{2,1,0:T(8,128)}, u32[]{:S(2)}) copy-start(f32[1,512,512]{2,1,0:T(8,128)} %param.12) | copy-start | bytes 3145732
  3.4 12.5 %collective-permute-start = (bf16[8,64,256]{2,1,0:T(8,128)(2,1)}, bf16[8,64,256]{2,1,0:T(8,128)(2,1)S(1)}, u32[]{:S(2)}, u32[]{:S(2)}) collective-permute-start(bf16[8,64,256]{2,1,0:T(8,128)(2,1)} %get-tuple-element.59), channel_id=1, source_target_pairs={{0,8},{8,16},{16,24},{24,0},{1,9},{9,17},{17,25},{25,1},{2,10},{10... | collective-permute-start | bytes 786440 | tf_op jit(solution)/shard_map/ppermute | solution.py:406
  6.5 13.6 %collective-permute-start.2 = (bf16[8,64,256]{2,1,0:T(8,128)(2,1)}, bf16[8,64,256]{2,1,0:T(8,128)(2,1)S(1)}, u32[]{:S(2)}, u32[]{:S(2)}) collective-permute-start(bf16[8,64,256]{2,1,0:T(8,128)(2,1)} %get-tuple-element.67), channel_id=1, source_target_pairs={{0,24},{8,0},{16,8},{24,16},{1,25},{9,1},{17,9},{25,17},{2,26},{10... | collective-permute-start | bytes 786440 | tf_op jit(solution)/shard_map/ppermute | solution.py:406
  8.6 1.2 copy-start.4
  9.8 1.2 copy-start.6
  11.1 1.6 copy-start
  16.0 13.0 %collective-permute-start.1 = (bf16[8,64,256]{2,1,0:T(8,128)(2,1)S(1)}, bf16[8,64,256]{2,1,0:T(8,128)(2,1)S(1)}, u32[]{:S(2)}, u32[]{:S(2)}) collective-permute-start(bf16[8,64,256]{2,1,0:T(8,128)(2,1)S(1)} %add_right.2), channel_id=1, source_target_pairs={{0,8},{8,16},{16,24},{24,0},{1,9},{9,17},{17,25},{25,1},{2,10},{10... | collective-permute-start | bytes 786440 | tf_op jit(solution)/shard_map/ppermute | solution.py:415
  20.2 14.5 %collective-permute-start.4 = (bf16[8,64,256]{2,1,0:T(8,128)(2,1)S(1)}, bf16[8,64,256]{2,1,0:T(8,128)(2,1)S(1)}, u32[]{:S(2)}, u32[]{:S(2)}) collective-permute-start(bf16[8,64,256]{2,1,0:T(8,128)(2,1)S(1)} %add_left.2), channel_id=1, source_target_pairs={{0,24},{8,0},{16,8},{24,16},{1,25},{9,1},{17,9},{25,17},{2,26},{10... | collective-permute-start | bytes 786440 | tf_op jit(solution)/shard_map/ppermute | solution.py:415
  29.1 11.7 %collective-permute-start.3 = (bf16[8,64,256]{2,1,0:T(8,128)(2,1)S(1)}, bf16[8,64,256]{2,1,0:T(8,128)(2,1)S(1)}, u32[]{:S(2)}, u32[]{:S(2)}) collective-permute-start(bf16[8,64,256]{2,1,0:T(8,128)(2,1)S(1)} %add_right.3), channel_id=1, source_target_pairs={{0,8},{8,16},{16,24},{24,0},{1,9},{9,17},{17,25},{25,1},{2,10},{10... | collective-permute-start | bytes 786440 | tf_op jit(solution)/shard_map/ppermute | solution.py:415
  34.7 6.1 %copy-start.5 = (f32[1,512,512]{2,1,0:T(8,128)S(1)}, f32[1,512,512]{2,1,0:T(8,128)}, u32[]{:S(2)}) copy-start(f32[1,512,512]{2,1,0:T(8,128)} %param.14) | copy-start | bytes 3145732
  34.7 6.1 %copy-start.7 = (f32[1,512,512]{2,1,0:T(8,128)S(1)}, f32[1,512,512]{2,1,0:T(8,128)}, u32[]{:S(2)}) copy-start(f32[1,512,512]{2,1,0:T(8,128)} %param.15) | copy-start | bytes 3145732
  34.7 10.5 %collective-permute-start.5 = (bf16[8,64,256]{2,1,0:T(8,128)(2,1)S(1)}, bf16[8,64,256]{2,1,0:T(8,128)(2,1)S(1)}, u32[]{:S(2)}, u32[]{:S(2)}) collective-permute-start(bf16[8,64,256]{2,1,0:T(8,128)(2,1)S(1)} %add_left.3), channel_id=1, source_target_pairs={{0,24},{8,0},{16,8},{24,16},{1,25},{9,1},{17,9},{25,17},{2,26},{10... | collective-permute-start | bytes 786440 | tf_op jit(solution)/shard_map/ppermute | solution.py:415
  41.4 16.5 %copy-start.8 = (f32[1,512,512]{2,1,0:T(8,128)S(1)}, f32[1,512,512]{2,1,0:T(8,128)}, u32[]{:S(2)}) copy-start(f32[1,512,512]{2,1,0:T(8,128)} %param.10) | copy-start | bytes 3145732
  41.4 16.5 %copy-start.9 = (f32[1,512,512]{2,1,0:T(8,128)S(1)}, f32[1,512,512]{2,1,0:T(8,128)}, u32[]{:S(2)}) copy-start(f32[1,512,512]{2,1,0:T(8,128)} %param.11) | copy-start | bytes 3145732

commit v3 on v2

--- a/solution.py
+++ b/solution.py
@@ -12,7 +12,6 @@
 NN = (((1,), (0,)), ((), ()))
 NT = (((1,), (1,)), ((), ()))
 VMEM_LIMIT = 24 * 1024 * 1024
-VMEM_MOST = 56 * 1024 * 1024
 
 START_BOUND = 4.0
 END_BOUND = 0.016
@@ -200,30 +199,33 @@
     store_split(hi_ref, lo_ref, q_ref[...])
 
 
-def gather_kernel(steps, order_ref, parts_hbm, *rest):
+def slice_kernel(parts_hbm, *rest):
     outs, sems = rest[:-1], rest[-1]
     replicas = lax.axis_size("replica")
-    at = lax.axis_index("replica")
     slots, _, half = outs[0].shape
     pairs = []
-    for number, step in enumerate(steps):
-        for part in range(2):
-            ahead = (2 * replicas - 1 - step) if part == 0 else (1 + step)
-            first = lax.rem(at + ahead, replicas) * slots
-            for i in range(slots):
-                source = parts_hbm.at[order_ref[first + i], :, pl.ds(part * half, half)]
-                pairs.append((source, outs[2 * number + part].at[i]))
+    for event, out in enumerate(outs):
+        step, way = divmod(event, 2)
+        first = passing_group(step + 1, way, replicas) * slots
+        pairs.append((parts_hbm.at[pl.ds(first, slots), :, pl.ds(way * half, half)], out))
     wait_copies(start_copies(pairs, sems))
+
+
+def passing_group(step, way, replicas):
+    ahead = (2 * replicas - 1 - step) if way == 0 else (1 + step)
+    return lax.rem(lax.axis_index("replica") + ahead, replicas)
 
 
 def add_kernel(got_ref, own_ref, out_ref):
     out_ref[...] = (got_ref[...].astype(F32) + own_ref[...].astype(F32)).astype(BF16)
 
 
-def finish_kernel(got_right_ref, got_left_ref, own_right_ref, own_left_ref, out_ref):
-    half = got_right_ref.shape[2]
-    add_kernel(got_right_ref, own_right_ref, out_ref.at[:, :, :half])
-    add_kernel(got_left_ref, own_left_ref, out_ref.at[:, :, half:])
+def finish_kernel(order_ref, got_ref, own_ref, out_ref):
+    slots = out_ref.shape[0]
+    first = lax.axis_index("replica") * slots
+    for i in range(slots):
+        at = order_ref[first + i] - first
+        out_ref[i] = (got_ref[at].astype(F32) + own_ref[at].astype(F32)).astype(BF16)
 
 
 def place_kernel(order_ref, rows_ref, out_hbm, sems):
@@ -234,10 +236,10 @@
     ))
 
 
-def update_kernel(order_ref, refresh_ref, grad_ref, w_ref, q_ref,
+def update_kernel(order_ref, refresh_ref, first_ref, last_ref, w_ref, q_ref,
                   lf_hbm, rf_hbm, lb_hbm, rb_hbm, moment_hbm, second_hbm,
                   update_ref, left_hbm, right_hbm,
-                  q2, h2, l2, s2, f2, b2, moment_ref, second_ref, new2, sems, out_sems):
+                  q2, h2, l2, s2, f2, b2, moment_ref, second_ref, new2, grad_ref, sems, out_sems):
     flag = own_flag(order_ref, refresh_ref)
     copies = start_copies(
         [(lf_hbm, f2.at[0]), (rf_hbm, f2.at[1]), (lb_hbm, b2.at[0]), (rb_hbm, b2.at[1]),
@@ -246,6 +248,8 @@
     )
     width = grad_ref.shape[0]
     weight = 0.05 / width
+    grad_ref[:, : width // 2] = first_ref[...]
+    grad_ref[:, width // 2 :] = last_ref[...]
     grad = grad_ref[...]
     grad_t = grad.T
     new2[0] = weight * dot(grad, grad, NT)
@@ -320,8 +324,7 @@
 HBM_SPEC = pl.BlockSpec(memory_space=pltpu.HBM)
 
 
-def call(kernel, name, in_smem, in_vmem, in_hbm, out_vmem, out_hbm=(), scratch=(), sems=(), flops=0,
-         limit=VMEM_LIMIT):
+def call(kernel, name, in_smem, in_vmem, in_hbm, out_vmem, out_hbm=(), scratch=(), sems=(), flops=0):
     operands = (*in_smem, *in_vmem, *in_hbm)
     return pl.pallas_call(
         kernel,
@@ -330,7 +333,7 @@
         out_specs=[VMEM_SPEC] * len(out_vmem) + [HBM_SPEC] * len(out_hbm),
         scratch_shapes=[pltpu.VMEM(shape, dtype) for shape, dtype in scratch]
         + [pltpu.SemaphoreType.DMA((count,)) for count in sems],
-        compiler_params=pltpu.CompilerParams(vmem_limit_bytes=limit),
+        compiler_params=pltpu.CompilerParams(vmem_limit_bytes=VMEM_LIMIT),
         cost_estimate=pl.CostEstimate(
             flops=flops,
             bytes_accessed=sum(x.size * x.dtype.itemsize for x in in_vmem),
@@ -366,12 +369,6 @@
 
     chunk = ((group_size, rows, width // 2), BF16)
 
-    def gather(name, at_steps, limit):
-        return call(
-            functools.partial(gather_kernel, at_steps), name, (block_order,), (), (grad_parts[0],),
-            [chunk] * (2 * len(at_steps)), sems=[2 * group_size * len(at_steps)], limit=limit,
-        )
-
     def stage(at, tied, state):
         flops = 20 * width**3
         given = (tied, refresh_ids)
@@ -395,36 +392,52 @@
         [(i, (i + 1) % replicas) for i in range(replicas)],
         [(i, (i - 1) % replicas) for i in range(replicas)],
     )
-    send = list(gather("gather_first", (0,), VMEM_MOST))
-    own = list(gather("gather_rest", tuple(range(1, replicas)), VMEM_LIMIT))
-    got = [None, None]
+    half = width // 2
+    send = [
+        lax.dynamic_slice(
+            grad_parts[0],
+            (passing_group(0, way, replicas) * group_size, 0, way * half),
+            (group_size, rows, half),
+        )
+        for way in range(2)
+    ]
+    tied, *send = lax.optimization_barrier((block_order, *send))
+    got = [lax.ppermute(send[way], "replica", ways[way]) for way in range(2)]
+    own = list(
+        call(
+            slice_kernel, "own_blocks", (), (), (grad_parts[0],), [chunk] * (2 * steps),
+            sems=[2 * steps],
+        )
+    )
     state = ()
-    for event in range(2 * steps):
-        step, way = divmod(event, 2)
-        if event == 0:
-            tied, *send = lax.optimization_barrier((block_order, *send))
-            got = [lax.ppermute(send[k], "replica", ways[k]) for k in range(2)]
-        if event < 6:
+    for event in range(2 * steps - 2):
+        way = event % 2
+        if event < 4:
             state = stage(event, tied, state)
             own[event], *state = lax.optimization_barrier((own[event], *state))
-        if step < steps - 1:
-            (send[way],) = call(
-                add_kernel, ("add_right", "add_left")[way], (), (got[way], own[event]), (), [chunk]
-            )
-            tied, send[way] = lax.optimization_barrier((block_order, send[way]))
-            got[way] = lax.ppermute(send[way], "replica", ways[way])
-        elif way == 0:
-            tied, got[0] = lax.optimization_barrier((block_order, got[0]))
-    mine = own[-2:]
-    (summed,) = call(
-        finish_kernel, "finish", (), (*got, *mine), (), [((group_size, rows, width), BF16)]
-    )
-    gradient = lax.all_to_all(summed, "fsdp", split_axis=0, concat_axis=0, tiled=True)
+        (send[way],) = call(
+            add_kernel, ("add_right", "add_left")[way], (), (got[way], own[event]), (), [chunk]
+        )
+        tied, send[way] = lax.optimization_barrier((block_order, send[way]))
+        got[way] = lax.ppermute(send[way], "replica", ways[way])
+    state = stage(5, tied, stage(4, tied, state))
+    parts = []
+    for way in range(2):
+        mine = own[2 * steps - 2 + way]
+        mine, *state = lax.optimization_barrier((mine, *state))
+        (summed,) = call(
+            finish_kernel, ("finish_right", "finish_left")[way], (block_order,), (got[way], mine),
+            (), [chunk],
+        )
+        part = lax.all_to_all(summed, "fsdp", split_axis=0, concat_axis=0, tiled=True)
+        if way == 0:
+            part, own[-1] = lax.optimization_barrier((part, own[-1]))
+        parts.append(part.reshape(width, half))
     update, left_new, right_new = call(
-        update_kernel, "update", slots, (gradient.reshape(square), *state),
+        update_kernel, "update", slots, (*parts, *state),
         (*state_arrays, moment[0], second_moment[0]), [(square, BF16)], [(square, F32)] * 2,
         scratch=[(pair, F32), (pair, BF16), (pair, BF16), (pair, BF16), *loads,
-                 (square, F32), (square, F32), (pair, F32)],
+                 (square, F32), (square, F32), (pair, F32), (square, BF16)],
         sems=[6, 2], flops=100 * width**3,
     )
     returned = lax.all_to_all(

time: 437 us -> 443 us (1.014)
  blocking collectives: 382 us -> 390 us
  local copies, waits for them, and re-layouts: 3.47 us -> 8.3 us
  waiting for transfers between devices: 23.7 us -> 19.2 us
    all_to_all x1 -> x2, blocking collectives: 12.6 us -> 19.8 us  [on_device(): lax.all_to_all(summed, 'fsdp', split_axis=0, concat_axis=0, tiled=True)]
  transfers between devices with their start and end apart: 6 -> 6, of which waited for: 6 -> 4; matrix products, arithmetic and copies ran while one was open for 0% -> 0% of each run, Pallas kernels for 1% -> 1%
where the time goes in v3:
time: 443 us; the launch traced here: 442 us
  blocking collectives  390 us (88%)
  waiting for transfers between devices  19.2 us (4%)
  Pallas kernels  13.3 us (3%)
  starting transfers between devices  10.7 us (2%)
  local copies, waits for them, and re-layouts  8.3 us (2%)
    all_to_all x1, blocking collectives, on_device(): lax.all_to_all(update.reshape(owners, rows, width), 'fsdp', split_axis=0,...  370 us
    all_to_all x2, blocking collectives, on_device(): lax.all_to_all(summed, 'fsdp', split_axis=0, concat_axis=0, tiled=True)  19.8 us
    ppermute x4, waiting for transfers between devices, on_device(): got[way] = lax.ppermute(send[way], 'replica', ways[way])  16.6 us
    pallas_call x15, Pallas kernels, call(): pl.pallas_call(kernel, out_shape=[jax.ShapeDtypeStruct(shape, dtype) for...  13.3 us
  transfers between devices with their start and end apart: 6, of which 4 were waited for; matrix products, arithmetic and copies ran while one was open for 0% of the time, Pallas kernels for 1%

profile of v3, /device:TPU:0, one launch (start us, length us, event | category | flops | bytes accessed | tf_op | source)
XLA Modules:
  0.0 442.3 jit_solution(6364331522570674096)
XLA Ops:
  0.6 1.1 dynamic-slice_bitcast_fusion
  1.7 3.1 collective-permute-start
  4.8 2.1 collective-permute-start.2
  6.9 0.7 copy-done.1
  7.5 1.2 copy-done.2
  8.8 1.2 copy-done.4
  10.0 1.2 copy-done.6
  11.2 1.2 copy-done.8
  12.4 0.7 copy-done.12
  13.1 0.6 prepare_start.1
  13.7 1.0 copy-done
  14.7 0.2 own_blocks.1
  14.9 0.1 add_right.2
  15.0 0.6 prepare_boost.1
  15.6 2.6 collective-permute-done.2.got_ref
  18.2 0.1 add_left.2
  18.2 3.2 collective-permute-start.4
  21.4 0.6 prepare_more.3
  22.0 5.0 %collective-permute-done.1.got_ref = bf16[8,64,256]{2,1,0:T(8,128)(2,1)S(1)} collective-permute-done((bf16[8,64,256]{2,1,0:T(8,128)(2,1)S(1)}, bf16[8,64,256]{2,1,0:T(8,128)(2,1)S(1)}, u32[]{:S(2)}, u32[]{:S(2)}) %collective-permute-start.1) | collective-permute-done | bytes 262176 | tf_op jit(solution)/shard_map/ppermute | solution.py:422
  27.1 0.6 prepare_more.4
  27.6 2.5 collective-permute-done.4.got_ref
  30.3 2.3 collective-permute-start.5
  32.6 0.7 prepare_more.5
  33.4 0.6 prepare_last.1
  34.0 9.0 %collective-permute-done.3.got_ref = bf16[8,64,256]{2,1,0:T(8,128)(2,1)S(1)} collective-permute-done((bf16[8,64,256]{2,1,0:T(8,128)(2,1)S(1)}, bf16[8,64,256]{2,1,0:T(8,128)(2,1)S(1)}, u32[]{:S(2)}, u32[]{:S(2)}) %collective-permute-start.3) | collective-permute-done | bytes 262176 | tf_op jit(solution)/shard_map/ppermute | solution.py:422
  43.0 0.6 finish_right.1
  43.7 10.5 %all_to_all.15 = bf16[8,64,256]{2,1,0:T(8,128)(2,1)S(1)} all-to-all(bf16[8,64,256]{2,1,0:T(8,128)(2,1)S(1)} %finish_right.1), channel_id=1, replica_groups=mesh['replica'=4,'fsdp'=8] {'fsdp'}, dimensions={0} | all-to-all | bytes 524288 | tf_op jit(solution)/shard_map/all_to_all | solution.py:432
  54.1 0.6 finish_left.1
  54.7 9.3 %all_to_all.16 = bf16[8,64,256]{2,1,0:T(8,128)(2,1)S(1)} all-to-all(bf16[8,64,256]{2,1,0:T(8,128)(2,1)S(1)} %finish_left.1), channel_id=1, replica_groups=mesh['replica'=4,'fsdp'=8] {'fsdp'}, dimensions={0} | all-to-all | bytes 524288 | tf_op jit(solution)/shard_map/all_to_all | solution.py:432
  64.1 6.6 %update.1 = (bf16[512,512]{1,0:T(8,128)(2,1)S(1)}, f32[512,512]{1,0:T(8,128)}, f32[512,512]{1,0:T(8,128)}) custom-call(s32[32]{0:T(128)S(1)} %copy-done.1, s32[3]{0:T(128)S(1)} %copy-done.12, bf16[512,256]{1,0:T(8,128)(2,1)S(1)} %bitcast.18, bf16[512,256]{1,0:T(8,128)(2,1)S(1)} %bitcast.19, bf16[2,512,512]{2,1,0:T(8,128)(2,1)S(1)} %get-tuple-element.102.w_ref, ...), custom_call_target="tpu_custom_call" | custom-call | flops 13421772800 | bytes 3670016 | tf_op jit(solution)/shard_map/update/pallas_call | solution.py:329
  70.7 370.0 %all_to_all.17.rows_ref = bf16[8,64,512]{2,1,0:T(8,128)(2,1)S(1)} all-to-all(bf16[8,64,512]{2,1,0:T(8,128)(2,1)S(1)} %bitcast.17), channel_id=1, replica_groups=mesh['replica'=4,'fsdp'=8] {'fsdp'}, dimensions={0} | all-to-all | bytes 1048576 | tf_op jit(solution)/shard_map/all_to_all | solution.py:443
  440.7 1.4 place.1
  (25 shorter events, 0.2 us)
Async XLA Ops:
  1.7 13.2 %collective-permute-start = (bf16[8,64,256]{2,1,0:T(8,128)(2,1)S(1)}, bf16[8,64,256]{2,1,0:T(8,128)(2,1)S(1)}, u32[]{:S(2)}, u32[]{:S(2)}) collective-permute-start(bf16[8,64,256]{2,1,0:T(8,128)(2,1)S(1)} %get-tuple-element.55), channel_id=1, source_target_pairs={{0,8},{8,16},{16,24},{24,0},{1,9},{9,17},{17,25},{25,1},{2,10},{10... | collective-permute-start | bytes 786440 | tf_op jit(solution)/shard_map/ppermute | solution.py:405
  4.8 13.4 %collective-permute-start.2 = (bf16[8,64,256]{2,1,0:T(8,128)(2,1)S(1)}, bf16[8,64,256]{2,1,0:T(8,128)(2,1)S(1)}, u32[]{:S(2)}, u32[]{:S(2)}) collective-permute-start(bf16[8,64,256]{2,1,0:T(8,128)(2,1)S(1)} %get-tuple-element.63), channel_id=1, source_target_pairs={{0,24},{8,0},{16,8},{24,16},{1,25},{9,1},{17,9},{25,17},{2,26},{10... | collective-permute-start | bytes 786440 | tf_op jit(solution)/shard_map/ppermute | solution.py:405
  6.9 0.7 copy-start.1
  7.5 1.2 copy-start.2
  8.8 1.2 copy-start.4
  10.0 1.2 copy-start.6
  11.2 1.2 copy-start.8
  12.4 0.7 copy-start.12
  13.1 1.6 copy-start
  15.0 12.1 %collective-permute-start.1 = (bf16[8,64,256]{2,1,0:T(8,128)(2,1)S(1)}, bf16[8,64,256]{2,1,0:T(8,128)(2,1)S(1)}, u32[]{:S(2)}, u32[]{:S(2)}) collective-permute-start(bf16[8,64,256]{2,1,0:T(8,128)(2,1)S(1)} %add_right.2), channel_id=1, source_target_pairs={{0,8},{8,16},{16,24},{24,0},{1,9},{9,17},{17,25},{25,1},{2,10},{10... | collective-permute-start | bytes 786440 | tf_op jit(solution)/shard_map/ppermute | solution.py:422
  18.2 11.9 %collective-permute-start.4 = (bf16[8,64,256]{2,1,0:T(8,128)(2,1)S(1)}, bf16[8,64,256]{2,1,0:T(8,128)(2,1)S(1)}, u32[]{:S(2)}, u32[]{:S(2)}) collective-permute-start(bf16[8,64,256]{2,1,0:T(8,128)(2,1)S(1)} %add_left.2), channel_id=1, source_target_pairs={{0,24},{8,0},{16,8},{24,16},{1,25},{9,1},{17,9},{25,17},{2,26},{10... | collective-permute-start | bytes 786440 | tf_op jit(solution)/shard_map/ppermute | solution.py:422
  30.3 3.1 copy-start.3
  30.3 3.1 copy-start.5
  30.3 3.1 copy-start.7
  30.3 3.1 copy-start.9
  30.3 23.8 %collective-permute-start.5 = (bf16[8,64,256]{2,1,0:T(8,128)(2,1)S(1)}, bf16[8,64,256]{2,1,0:T(8,128)(2,1)S(1)}, u32[]{:S(2)}, u32[]{:S(2)}) collective-permute-start(bf16[8,64,256]{2,1,0:T(8,128)(2,1)S(1)} %add_left.3), channel_id=1, source_target_pairs={{0,24},{8,0},{16,8},{24,16},{1,25},{9,1},{17,9},{25,17},{2,26},{10... | collective-permute-start | bytes 786440 | tf_op jit(solution)/shard_map/ppermute | solution.py:422
  32.6 10.4 %collective-permute-start.3 = (bf16[8,64,256]{2,1,0:T(8,128)(2,1)S(1)}, bf16[8,64,256]{2,1,0:T(8,128)(2,1)S(1)}, u32[]{:S(2)}, u32[]{:S(2)}) collective-permute-start(bf16[8,64,256]{2,1,0:T(8,128)(2,1)S(1)} %add_right.3), channel_id=1, source_target_pairs={{0,8},{8,16},{16,24},{24,0},{1,9},{9,17},{17,25},{25,1},{2,10},{10... | collective-permute-start | bytes 786440 | tf_op jit(solution)/shard_map/ppermute | solution.py:422
  34.0 30.1 %copy-start.10 = (f32[1,512,512]{2,1,0:T(8,128)S(1)}, f32[1,512,512]{2,1,0:T(8,128)}, u32[]{:S(2)}) copy-start(f32[1,512,512]{2,1,0:T(8,128)} %param.10) | copy-start | bytes 3145732
  34.0 30.1 %copy-start.11 = (f32[1,512,512]{2,1,0:T(8,128)S(1)}, f32[1,512,512]{2,1,0:T(8,128)}, u32[]{:S(2)}) copy-start(f32[1,512,512]{2,1,0:T(8,128)} %param.11) | copy-start | bytes 3145732

commit v4 on v3

--- a/solution.py
+++ b/solution.py
@@ -11,7 +11,7 @@
 BF16 = jnp.bfloat16
 NN = (((1,), (0,)), ((), ()))
 NT = (((1,), (1,)), ((), ()))
-VMEM_LIMIT = 24 * 1024 * 1024
+VMEM_LIMIT = 20 * 1024 * 1024
 
 START_BOUND = 4.0
 END_BOUND = 0.016
@@ -32,66 +32,62 @@
     lo_ref[...] = lo
 
 
-def halves(width):
-    half = width // 2
-    return ((slice(half, width), width), (slice(0, half), half))
-
-
-def lower_step(gram, first_row):
-    rows = lax.broadcasted_iota(jnp.int32, gram.shape, 0) + first_row
-    cols = lax.broadcasted_iota(jnp.int32, gram.shape, 1)
-    return jnp.where(rows > cols, gram, jnp.where(rows == cols, 0.5 * gram - 0.5, 0.0))
+def ranges(width):
+    return slice(0, width // 2), slice(width // 2, width)
 
 
 def triangle(hi_ref, step_ref):
-    total = 0.0
-    for rows, reach in halves(hi_ref.shape[0]):
-        step = lower_step(dot(hi_ref[rows, :], hi_ref[:reach, :], NT), rows.start)
-        total += jnp.sum(step * step)
-        step_ref[rows, :reach] = step.astype(BF16)
-    return total
-
-
-def apply_step(q_ref, hi_ref, lo_ref, step_ref):
-    for rows, reach in halves(q_ref.shape[0]):
-        q_new = q_ref[rows, :] - dot(step_ref[rows, :reach], hi_ref[:reach, :])
+    first, last = ranges(hi_ref.shape[0])
+    square = (first.stop, first.stop)
+    rows = lax.broadcasted_iota(jnp.int32, square, 0)
+    cols = lax.broadcasted_iota(jnp.int32, square, 1)
+    weight = jnp.where(rows > cols, 1.0, jnp.where(rows == cols, 0.5, 0.0))
+    half_eye = jnp.where(rows == cols, 0.5, 0.0)
+    step = dot(hi_ref[last, :], hi_ref[first, :], NT)
+    total = step * step
+    step_ref[last, first] = step.astype(BF16)
+    for part in (first, last):
+        step = dot(hi_ref[part, :], hi_ref[part, :], NT) * weight - half_eye
+        total += step * step
+        step_ref[part, part] = step.astype(BF16)
+    return jnp.sum(total)
+
+
+def apply_step(q_ref, hi_ref, step_ref, keep=1.0, gain=1.0):
+    first, last = ranges(q_ref.shape[0])
+    for rows, reach in ((last, q_ref.shape[0]), (first, first.stop)):
+        q_new = keep * q_ref[rows, :] - gain * dot(step_ref[rows, :reach], hi_ref[:reach, :])
         q_ref[rows, :] = q_new
-        hi, lo = split(q_new)
-        hi_ref[rows, :] = hi
-        if lo_ref is not None:
-            lo_ref[rows, :] = lo
-
-
-def boosted_steps(number, q2, h2, s2, t2, th2):
-    for _ in range(number):
-        for side in range(2):
-            triangle(h2.at[side], s2.at[side])
-        for side in range(2):
-            for full, low in ((q2, h2), (t2, th2)):
-                for rows, reach in halves(q2.shape[1]):
-                    new = 1.3 * full[side, rows, :] - 1.4 * dot(
-                        s2[side, rows, :reach], low[side, :reach, :]
-                    )
-                    full[side, rows, :] = new
-                    low[side, rows, :] = new.astype(BF16)
-
-
-def prepare_steps(most, q2, h2, s2, t2, th2):
-    def body(carry):
-        count, _ = carry
-        worst = 0.0
-        for side in range(2):
-            worst = jnp.maximum(worst, triangle(h2.at[side], s2.at[side]))
-        for side in range(2):
-            apply_step(q2.at[side], h2.at[side], None, s2.at[side])
-            apply_step(t2.at[side], th2.at[side], None, s2.at[side])
-        return count + 1, worst
-
-    lax.while_loop(
-        lambda carry: (carry[0] < most) & (carry[1] > START_BOUND),
-        body,
+        hi_ref[rows, :] = q_new.astype(BF16)
+
+
+def apply_triangle(t_ref, hi_ref, step_ref, keep=1.0, gain=1.0):
+    first, last = ranges(t_ref.shape[0])
+    for rows, cols, reach in (
+        (last, first, slice(0, last.stop)), (last, last, last), (first, first, first)
+    ):
+        new = keep * t_ref[rows, cols] - gain * dot(step_ref[rows, reach], hi_ref[reach, cols])
+        t_ref[rows, cols] = new
+        hi_ref[rows, cols] = new.astype(BF16)
+
+
+def one_step(q2, h2, s2, t2, th2, keep=1.0, gain=1.0):
+    worst = 0.0
+    for side in range(2):
+        worst = jnp.maximum(worst, triangle(h2.at[side], s2.at[side]))
+    for side in range(2):
+        apply_step(q2.at[side], h2.at[side], s2.at[side], keep, gain)
+        if t2 is not None:
+            apply_triangle(t2.at[side], th2.at[side], s2.at[side], keep, gain)
+    return worst
+
+
+def steps_until(bound, most, *refs):
+    return lax.while_loop(
+        lambda carry: (carry[0] < most) & (carry[1] > bound),
+        lambda carry: (carry[0] + 1, one_step(*refs)),
         (jnp.int32(0), jnp.float32(1e30)),
-    )
+    )[1]
 
 
 def own_flag(order_ref, refresh_ref):
@@ -152,14 +148,16 @@
     @pl.when(own_flag(order_ref, refresh_ref))
     def _():
         load_state(h_ref, th_ref, h2, th2, q2, t2)
-        boosted_steps(2, q2, h2, s2, t2, th2)
+        for _ in range(2):
+            one_step(q2, h2, s2, t2, th2, 1.3, 1.4)
+        one_step(q2, h2, s2, t2, th2)
 
 
 def prepare_more(most, order_ref, refresh_ref, h_ref, th_ref, h2, th2, q2, t2, s2):
     @pl.when(own_flag(order_ref, refresh_ref))
     def _():
         load_state(h_ref, th_ref, h2, th2, q2, t2)
-        prepare_steps(most, q2, h2, s2, t2, th2)
+        steps_until(START_BOUND, most, q2, h2, s2, t2, th2)
 
 
 def prepare_last(order_ref, refresh_ref, h_ref, th_ref, lf_hbm, rf_hbm, lb_hbm, rb_hbm,
@@ -182,7 +180,7 @@
             )
 
 
-def gram_schmidt(q_ref, hi_ref, lo_ref):
+def gram_schmidt(q_ref):
     width = q_ref.shape[0]
     rows = lax.broadcasted_iota(jnp.int32, (width, 1), 0)
 
@@ -196,7 +194,6 @@
         return carry
 
     lax.fori_loop(0, width, one, 0)
-    store_split(hi_ref, lo_ref, q_ref[...])
 
 
 def slice_kernel(parts_hbm, *rest):
@@ -220,12 +217,17 @@
     out_ref[...] = (got_ref[...].astype(F32) + own_ref[...].astype(F32)).astype(BF16)
 
 
-def finish_kernel(order_ref, got_ref, own_ref, out_ref):
+def finish_kernel(order_ref, got_right_ref, got_left_ref, own_right_ref, own_left_ref, out_ref):
     slots = out_ref.shape[0]
+    half = got_right_ref.shape[2]
     first = lax.axis_index("replica") * slots
     for i in range(slots):
         at = order_ref[first + i] - first
-        out_ref[i] = (got_ref[at].astype(F32) + own_ref[at].astype(F32)).astype(BF16)
+        for got_ref, own_ref, cols in (
+            (got_right_ref, own_right_ref, slice(0, half)),
+            (got_left_ref, own_left_ref, slice(half, 2 * half)),
+        ):
+            out_ref[i, :, cols] = (got_ref[at].astype(F32) + own_ref[at].astype(F32)).astype(BF16)
 
 
 def place_kernel(order_ref, rows_ref, out_hbm, sems):
@@ -236,34 +238,22 @@
     ))
 
 
-def update_kernel(order_ref, refresh_ref, first_ref, last_ref, w_ref, q_ref,
-                  lf_hbm, rf_hbm, lb_hbm, rb_hbm, moment_hbm, second_hbm,
-                  update_ref, left_hbm, right_hbm,
-                  q2, h2, l2, s2, f2, b2, moment_ref, second_ref, new2, grad_ref, sems, out_sems):
+def update_kernel(order_ref, refresh_ref, grad_ref, w_ref, q_ref, lf_ref, rf_ref, lb_ref, rb_ref,
+                  moment_ref, second_ref, update_ref, left_hbm, right_hbm,
+                  q2, h2, l2, s2, new2, out_sems):
     flag = own_flag(order_ref, refresh_ref)
-    copies = start_copies(
-        [(lf_hbm, f2.at[0]), (rf_hbm, f2.at[1]), (lb_hbm, b2.at[0]), (rb_hbm, b2.at[1]),
-         (moment_hbm, moment_ref), (second_hbm, second_ref)],
-        sems,
-    )
     width = grad_ref.shape[0]
     weight = 0.05 / width
-    grad_ref[:, : width // 2] = first_ref[...]
-    grad_ref[:, width // 2 :] = last_ref[...]
     grad = grad_ref[...]
     grad_t = grad.T
-    new2[0] = weight * dot(grad, grad, NT)
-    new2[1] = weight * dot(grad_t, grad_t, NT)
-
-    wait_copies(copies[:4])
-    for side in range(2):
-        new2[side] += 0.95 * f2[side]
+    new2[0] = 0.95 * lf_ref[...] + weight * dot(grad, grad, NT)
+    new2[1] = 0.95 * rf_ref[...] + weight * dot(grad_t, grad_t, NT)
     out_copies = start_copies([(new2.at[0], left_hbm), (new2.at[1], right_hbm)], out_sems)
 
     @pl.when(jnp.logical_not(flag))
     def _():
-        store_split(h2.at[0], l2.at[0], b2[0].T)
-        store_split(h2.at[1], l2.at[1], b2[1].T)
+        store_split(h2.at[0], l2.at[0], lb_ref[...].T)
+        store_split(h2.at[1], l2.at[1], rb_ref[...].T)
 
     @pl.when(flag)
     def _():
@@ -276,35 +266,24 @@
         q2[1] = q_right
         h2[1] = q_right.astype(BF16)
 
-        def body(carry):
-            count, _ = carry
-            worst = 0.0
-            for side in range(2):
-                worst = jnp.maximum(worst, triangle(h2.at[side], s2.at[side]))
-            for side in range(2):
-                apply_step(q2.at[side], h2.at[side], l2.at[side], s2.at[side])
-            return count + 1, worst
-
-        _, worst = lax.while_loop(
-            lambda carry: (carry[0] < 20) & (carry[1] > END_BOUND),
-            body,
-            (jnp.int32(0), jnp.float32(1e30)),
-        )
+        worst = steps_until(END_BOUND, 20, q2, h2, s2, None, None)
 
         @pl.when(jnp.logical_not(worst <= END_BOUND))
         def _():
-            for side in range(2):
+            for side, basis in enumerate((lb_ref, rb_ref)):
                 q2[side] = lax.dot_general(
-                    new2[side], b2[side], NN,
+                    new2[side], basis[...], NN,
                     precision=lax.Precision.HIGHEST, preferred_element_type=F32,
                 ).T
-                gram_schmidt(q2.at[side], h2.at[side], l2.at[side])
+                gram_schmidt(q2.at[side])
+
+        for side in range(2):
+            store_split(h2.at[side], l2.at[side], q2[side])
 
     left_hi = h2[0]
     left_lo = l2[0]
     right_hi = h2[1]
     right_lo = l2[1]
-    wait_copies(copies[4:])
     rotated = dot(dot(left_hi, grad).astype(BF16), right_hi, NT)
     moment_hi, moment_lo = split(0.9 * moment_ref[...] + 0.1 * grad.astype(F32))
     part = dot(left_hi, moment_hi) + dot(left_lo, moment_hi) + dot(left_hi, moment_lo)
@@ -377,12 +356,12 @@
                 prepare_start, "prepare_start", given, (), state_arrays,
                 [(pair, BF16)] * 2, scratch=loads, sems=[4], flops=flops,
             )
-        if at == 5:
+        if at == 4:
             return call(
                 prepare_last, "prepare_last", given, state, state_arrays,
                 [(pair, BF16), (pair, F32)], scratch=loads, sems=[4], flops=flops,
             )
-        kernel = prepare_boost if at == 1 else functools.partial(prepare_more, 2 if at < 4 else 16)
+        kernel = prepare_boost if at == 1 else functools.partial(prepare_more, 3 if at == 2 else 16)
         return call(
             kernel, "prepare_boost" if at == 1 else "prepare_more", given, state, (),
             [(pair, BF16)] * 2, scratch=work, flops=flops,
@@ -410,35 +389,30 @@
         )
     )
     state = ()
-    for event in range(2 * steps - 2):
+    for event in range(2 * steps):
         way = event % 2
-        if event < 4:
-            state = stage(event, tied, state)
+        if 0 < event < 6:
+            state = stage(event - 1, tied, state)
             own[event], *state = lax.optimization_barrier((own[event], *state))
-        (send[way],) = call(
-            add_kernel, ("add_right", "add_left")[way], (), (got[way], own[event]), (), [chunk]
-        )
-        tied, send[way] = lax.optimization_barrier((block_order, send[way]))
-        got[way] = lax.ppermute(send[way], "replica", ways[way])
-    state = stage(5, tied, stage(4, tied, state))
-    parts = []
-    for way in range(2):
-        mine = own[2 * steps - 2 + way]
-        mine, *state = lax.optimization_barrier((mine, *state))
-        (summed,) = call(
-            finish_kernel, ("finish_right", "finish_left")[way], (block_order,), (got[way], mine),
-            (), [chunk],
-        )
-        part = lax.all_to_all(summed, "fsdp", split_axis=0, concat_axis=0, tiled=True)
-        if way == 0:
-            part, own[-1] = lax.optimization_barrier((part, own[-1]))
-        parts.append(part.reshape(width, half))
+        if event < 2 * steps - 2:
+            (send[way],) = call(
+                add_kernel, ("add_right", "add_left")[way], (), (got[way], own[event]), (), [chunk]
+            )
+            tied, send[way] = lax.optimization_barrier((block_order, send[way]))
+            got[way] = lax.ppermute(send[way], "replica", ways[way])
+        elif way == 0:
+            tied, got[0] = lax.optimization_barrier((block_order, got[0]))
+    (summed,) = call(
+        finish_kernel, "finish", (block_order,), (*got, *own[-2:]), (),
+        [((group_size, rows, width), BF16)],
+    )
+    gradient = lax.all_to_all(summed, "fsdp", split_axis=0, concat_axis=0, tiled=True)
     update, left_new, right_new = call(
-        update_kernel, "update", slots, (*parts, *state),
-        (*state_arrays, moment[0], second_moment[0]), [(square, BF16)], [(square, F32)] * 2,
-        scratch=[(pair, F32), (pair, BF16), (pair, BF16), (pair, BF16), *loads,
-                 (square, F32), (square, F32), (pair, F32), (square, BF16)],
-        sems=[6, 2], flops=100 * width**3,
+        update_kernel, "update", slots,
+        (gradient.reshape(square), *state, *state_arrays, moment[0], second_moment[0]), (),
+        [(square, BF16)], [(square, F32)] * 2,
+        scratch=[(pair, F32), (pair, BF16), (pair, BF16), (pair, BF16), (pair, F32)],
+        sems=[2], flops=100 * width**3,
     )
     returned = lax.all_to_all(
         update.reshape(owners, rows, width), "fsdp", split_axis=0, concat_axis=0, tiled=True

time: 443 us -> 434 us (0.980)
  Pallas kernels: 13.3 us -> 386 us
  blocking collectives: 390 us -> 24.3 us
  waiting for transfers between devices: 19.2 us -> 11.5 us
    pallas_call x15 -> x13, Pallas kernels: 13.3 us -> 386 us  [call(): pl.pallas_call(kernel, out_shape=[jax.ShapeDtypeStruct(shape, dtype) for...]
    all_to_all x1, blocking collectives: 370 us -> 12.2 us  [on_device(): lax.all_to_all(update.reshape(owners, rows, width), 'fsdp', split_axis=0,...]
    ppermute x4, waiting for transfers between devices: 16.6 us -> 6.2 us  [on_device(): got[way] = lax.ppermute(send[way], 'replica', ways[way])]
    all_to_all x2 -> x1, blocking collectives: 19.8 us -> 12.2 us  [on_device(): lax.all_to_all(summed, 'fsdp', split_axis=0, concat_axis=0, tiled=True)]
  transfers between devices with their start and end apart: 6 -> 6, of which waited for: 4 -> 4; matrix products, arithmetic and copies ran while one was open for 0% -> 0% of each run, Pallas kernels for 1% -> 4%
where the time goes in v4:
time: 434 us
  Pallas kernels  386 us (89%)
  blocking collectives  24.3 us (6%)
  waiting for transfers between devices  11.5 us (3%)
  starting transfers between devices  7.45 us (2%)
    pallas_call x13, Pallas kernels, call(): pl.pallas_call(kernel, out_shape=[jax.ShapeDtypeStruct(shape, dtype) for...  386 us
    all_to_all x1, blocking collectives, on_device(): lax.all_to_all(summed, 'fsdp', split_axis=0, concat_axis=0, tiled=True)  12.2 us
    all_to_all x1, blocking collectives, on_device(): lax.all_to_all(update.reshape(owners, rows, width), 'fsdp', split_axis=0,...  12.2 us
  transfers between devices with their start and end apart: 6, of which 4 were waited for; matrix products, arithmetic and copies ran while one was open for 0% of the time, Pallas kernels for 4%

profile of v4, /device:TPU:0, one launch (start us, length us, event | category | flops | bytes accessed | tf_op | source)
XLA Modules:
  0.0 434.1 jit_solution(4262310081482672635)
XLA Ops:
  0.7 1.2 dynamic-slice_bitcast_fusion
  1.8 3.1 collective-permute-start
  4.9 2.1 collective-permute-start.2
  7.0 1.6 copy-done
  8.6 0.2 own_blocks.1
  8.8 5.3 %collective-permute-done.got_ref = bf16[8,64,256]{2,1,0:T(8,128)(2,1)S(1)} collective-permute-done((bf16[8,64,256]{2,1,0:T(8,128)(2,1)S(1)}, bf16[8,64,256]{2,1,0:T(8,128)(2,1)S(1)}, u32[]{:S(2)}, u32[]{:S(2)}) %collective-permute-start) | collective-permute-done | bytes 262176 | tf_op jit(solution)/shard_map/ppermute | solution.py:384
  14.1 0.1 add_right.2
  14.2 0.1 collective-permute-start.1
  14.3 0.0 copy-start.5
  14.3 1.2 copy-done.5
  15.5 4.3 prepare_start.1
  19.9 0.1 add_left.2
  19.9 1.9 collective-permute-start.4
  21.8 4.3 prepare_boost.1
  26.1 0.9 collective-permute-done.1.got_ref
  27.0 0.1 add_right.3
  27.1 0.1 collective-permute-start.3
  27.1 3.6 prepare_more.2
  30.7 1.9 collective-permute-done.4.got_ref
  32.6 0.1 add_left.3
  32.7 0.0 copy-start.6
  32.7 0.3 collective-permute-start.5
  33.0 2.3 prepare_more.3
  35.3 3.5 collective-permute-done.3.got_right_ref
  38.7 4.5 %prepare_last.1 = (bf16[2,512,512]{2,1,0:T(8,128)(2,1)S(1)}, f32[2,512,512]{2,1,0:T(8,128)S(1)}) custom-call(s32[32]{0:T(128)S(1)} %copy-done.1, s32[3]{0:T(128)S(1)} %copy-done.9, bf16[2,512,512]{2,1,0:T(8,128)(2,1)S(1)} %get-tuple-element.85.h_ref, bf16[2,512,512]{2,1,0:T(8,128)(2,1)S(1)} %get-tuple-element.86.th_ref, f32[512,512]{1,0:T(8,128)S(1)} %bitcast.19, ...), custom_call_target="tpu_custom_call" | custom-call | flops 2684354560 | bytes 2097152 | tf_op jit(solution)/shard_map/prepare_last/pallas_call | solution.py:308
  43.3 0.0 copy-start.7
  43.3 0.0 copy-start.8
  43.3 0.7 finish.1
  44.0 12.2 %all_to_all.10 = bf16[8,64,512]{2,1,0:T(8,128)(2,1)S(1)} all-to-all(bf16[8,64,512]{2,1,0:T(8,128)(2,1)S(1)} %finish.1), channel_id=1, replica_groups=mesh['replica'=4,'fsdp'=8] {'fsdp'}, dimensions={0} | all-to-all | bytes 1048576 | tf_op jit(solution)/shard_map/all_to_all | solution.py:409
  56.2 364.2 %update.1 = (bf16[512,512]{1,0:T(8,128)(2,1)S(1)}, f32[512,512]{1,0:T(8,128)}, f32[512,512]{1,0:T(8,128)}) custom-call(s32[32]{0:T(128)S(1)} %copy-done.1, s32[3]{0:T(128)S(1)} %copy-done.9, bf16[512,512]{1,0:T(8,128)(2,1)S(1)} %bitcast.16, bf16[2,512,512]{2,1,0:T(8,128)(2,1)S(1)} %get-tuple-element.90.w_ref, f32[2,512,512]{2,1,0:T(8,128)S(1)} %get-tuple-element.91.q_ref, ...), custom_call_target="tpu_custom_call" | custom-call | flops 13421772800 | bytes 9961472 | tf_op jit(solution)/shard_map/update/pallas_call | solution.py:308
  420.3 12.2 %all_to_all.11.rows_ref = bf16[8,64,512]{2,1,0:T(8,128)(2,1)S(1)} all-to-all(bf16[8,64,512]{2,1,0:T(8,128)(2,1)S(1)} %bitcast.17), channel_id=1, replica_groups=mesh['replica'=4,'fsdp'=8] {'fsdp'}, dimensions={0} | all-to-all | bytes 1048576 | tf_op jit(solution)/shard_map/all_to_all | solution.py:417
  432.5 1.4 place.1
  (16 shorter events, 0.0 us)
Async XLA Ops:
  0.6 13.6 %copy-start.1 = (s32[32]{0:T(128)S(1)}, s32[32]{0:T(128)}, u32[]{:S(2)}) copy-start(s32[32]{0:T(128)} %order_ref.10) | copy-start | bytes 388
  0.6 13.6 %copy-start.9 = (s32[3]{0:T(128)S(1)}, s32[3]{0:T(128)}, u32[]{:S(2)}) copy-start(s32[3]{0:T(128)} %refresh_ref.11) | copy-start | bytes 40
  0.7 13.6 %copy-start.2 = (f32[1,512,512]{2,1,0:T(8,128)S(1)}, f32[1,512,512]{2,1,0:T(8,128)}, u32[]{:S(2)}) copy-start(f32[1,512,512]{2,1,0:T(8,128)} %param.12) | copy-start | bytes 3145732
  1.8 12.3 %collective-permute-start = (bf16[8,64,256]{2,1,0:T(8,128)(2,1)S(1)}, bf16[8,64,256]{2,1,0:T(8,128)(2,1)S(1)}, u32[]{:S(2)}, u32[]{:S(2)}) collective-permute-start(bf16[8,64,256]{2,1,0:T(8,128)(2,1)S(1)} %get-tuple-element.49), channel_id=1, source_target_pairs={{0,8},{8,16},{16,24},{24,0},{1,9},{9,17},{17,25},{25,1},{2,10},{10... | collective-permute-start | bytes 786440 | tf_op jit(solution)/shard_map/ppermute | solution.py:384
  4.9 14.9 %collective-permute-start.2 = (bf16[8,64,256]{2,1,0:T(8,128)(2,1)S(1)}, bf16[8,64,256]{2,1,0:T(8,128)(2,1)S(1)}, u32[]{:S(2)}, u32[]{:S(2)}) collective-permute-start(bf16[8,64,256]{2,1,0:T(8,128)(2,1)S(1)} %get-tuple-element.53), channel_id=1, source_target_pairs={{0,24},{8,0},{16,8},{24,16},{1,25},{9,1},{17,9},{25,17},{2,26},{10... | collective-permute-start | bytes 786440 | tf_op jit(solution)/shard_map/ppermute | solution.py:384
  7.0 1.6 copy-start
  8.6 5.7 %copy-start.3 = (f32[1,512,512]{2,1,0:T(8,128)S(1)}, f32[1,512,512]{2,1,0:T(8,128)}, u32[]{:S(2)}) copy-start(f32[1,512,512]{2,1,0:T(8,128)} %param.13) | copy-start | bytes 3145732
  8.6 5.7 %copy-start.4 = (f32[1,512,512]{2,1,0:T(8,128)S(1)}, f32[1,512,512]{2,1,0:T(8,128)}, u32[]{:S(2)}) copy-start(f32[1,512,512]{2,1,0:T(8,128)} %param.14) | copy-start | bytes 3145732
  14.2 12.8 %collective-permute-start.1 = (bf16[8,64,256]{2,1,0:T(8,128)(2,1)S(1)}, bf16[8,64,256]{2,1,0:T(8,128)(2,1)S(1)}, u32[]{:S(2)}, u32[]{:S(2)}) collective-permute-start(bf16[8,64,256]{2,1,0:T(8,128)(2,1)S(1)} %add_right.2), channel_id=1, source_target_pairs={{0,8},{8,16},{16,24},{24,0},{1,9},{9,17},{17,25},{25,1},{2,10},{10... | collective-permute-start | bytes 786440 | tf_op jit(solution)/shard_map/ppermute | solution.py:402
  14.3 1.2 copy-start.5
  19.9 12.7 %collective-permute-start.4 = (bf16[8,64,256]{2,1,0:T(8,128)(2,1)S(1)}, bf16[8,64,256]{2,1,0:T(8,128)(2,1)S(1)}, u32[]{:S(2)}, u32[]{:S(2)}) collective-permute-start(bf16[8,64,256]{2,1,0:T(8,128)(2,1)S(1)} %add_left.2), channel_id=1, source_target_pairs={{0,24},{8,0},{16,8},{24,16},{1,25},{9,1},{17,9},{25,17},{2,26},{10... | collective-permute-start | bytes 786440 | tf_op jit(solution)/shard_map/ppermute | solution.py:402
  27.1 11.7 %collective-permute-start.3 = (bf16[8,64,256]{2,1,0:T(8,128)(2,1)S(1)}, bf16[8,64,256]{2,1,0:T(8,128)(2,1)S(1)}, u32[]{:S(2)}, u32[]{:S(2)}) collective-permute-start(bf16[8,64,256]{2,1,0:T(8,128)(2,1)S(1)} %add_right.3), channel_id=1, source_target_pairs={{0,8},{8,16},{16,24},{24,0},{1,9},{9,17},{17,25},{25,1},{2,10},{10... | collective-permute-start | bytes 786440 | tf_op jit(solution)/shard_map/ppermute | solution.py:402
  32.7 6.1 %copy-start.6 = (f32[1,512,512]{2,1,0:T(8,128)S(1)}, f32[1,512,512]{2,1,0:T(8,128)}, u32[]{:S(2)}) copy-start(f32[1,512,512]{2,1,0:T(8,128)} %param.15) | copy-start | bytes 3145732
  32.7 10.6 %collective-permute-start.5 = (bf16[8,64,256]{2,1,0:T(8,128)(2,1)S(1)}, bf16[8,64,256]{2,1,0:T(8,128)(2,1)S(1)}, u32[]{:S(2)}, u32[]{:S(2)}) collective-permute-start(bf16[8,64,256]{2,1,0:T(8,128)(2,1)S(1)} %add_left.3), channel_id=1, source_target_pairs={{0,24},{8,0},{16,8},{24,16},{1,25},{9,1},{17,9},{25,17},{2,26},{10... | collective-permute-start | bytes 786440 | tf_op jit(solution)/shard_map/ppermute | solution.py:402
  43.3 12.9 %copy-start.7 = (f32[1,512,512]{2,1,0:T(8,128)S(1)}, f32[1,512,512]{2,1,0:T(8,128)}, u32[]{:S(2)}) copy-start(f32[1,512,512]{2,1,0:T(8,128)} %param.10) | copy-start | bytes 3145732
  43.3 12.9 %copy-start.8 = (f32[1,512,512]{2,1,0:T(8,128)S(1)}, f32[1,512,512]{2,1,0:T(8,128)}, u32[]{:S(2)}) copy-start(f32[1,512,512]{2,1,0:T(8,128)} %param.11) | copy-start | bytes 3145732

commit v5 on v4

--- a/solution.py
+++ b/solution.py
@@ -50,7 +50,7 @@
         step = dot(hi_ref[part, :], hi_ref[part, :], NT) * weight - half_eye
         total += step * step
         step_ref[part, part] = step.astype(BF16)
-    return jnp.sum(total)
+    return total
 
 
 def apply_step(q_ref, hi_ref, step_ref, keep=1.0, gain=1.0):
@@ -72,20 +72,18 @@
 
 
 def one_step(q2, h2, s2, t2, th2, keep=1.0, gain=1.0):
-    worst = 0.0
-    for side in range(2):
-        worst = jnp.maximum(worst, triangle(h2.at[side], s2.at[side]))
+    totals = [triangle(h2.at[side], s2.at[side]) for side in range(2)]
     for side in range(2):
         apply_step(q2.at[side], h2.at[side], s2.at[side], keep, gain)
         if t2 is not None:
             apply_triangle(t2.at[side], th2.at[side], s2.at[side], keep, gain)
-    return worst
+    return totals
 
 
 def steps_until(bound, most, *refs):
     return lax.while_loop(
         lambda carry: (carry[0] < most) & (carry[1] > bound),
-        lambda carry: (carry[0] + 1, one_step(*refs)),
+        lambda carry: (carry[0] + 1, jnp.maximum(*map(jnp.sum, one_step(*refs)))),
         (jnp.int32(0), jnp.float32(1e30)),
     )[1]
 
@@ -111,21 +109,17 @@
         copy.wait()
 
 
-def prepare_start(order_ref, refresh_ref, lf_hbm, rf_hbm, lb_hbm, rb_hbm, h2, th2, f2, b2, sems):
+def prepare_start(order_ref, refresh_ref, lf_ref, rf_ref, lb_ref, rb_ref, h2, th2):
 
     @pl.when(own_flag(order_ref, refresh_ref))
     def _():
-        copies = start_copies(
-            [(lf_hbm, f2.at[0]), (lb_hbm, b2.at[0]), (rf_hbm, f2.at[1]), (rb_hbm, b2.at[1])], sems
-        )
-        width = lf_hbm.shape[0]
+        width = lf_ref.shape[0]
         eye = (
             lax.broadcasted_iota(jnp.int32, (width, width), 0)
             == lax.broadcasted_iota(jnp.int32, (width, width), 1)
         )
-        for side in range(2):
-            wait_copies(copies[2 * side : 2 * side + 2])
-            p = dot(f2[side].astype(BF16), b2[side].astype(BF16))
+        for side, (factor, basis) in enumerate(((lf_ref, lb_ref), (rf_ref, rb_ref))):
+            p = dot(factor[...].astype(BF16), basis[...].astype(BF16))
             scale = lax.rsqrt(jnp.sum(p * p, axis=0, keepdims=True))
             y = (p * scale).astype(BF16)
             gram = dot(y.T, y).astype(BF16)
@@ -157,23 +151,22 @@
     @pl.when(own_flag(order_ref, refresh_ref))
     def _():
         load_state(h_ref, th_ref, h2, th2, q2, t2)
-        steps_until(START_BOUND, most, q2, h2, s2, t2, th2)
-
-
-def prepare_last(order_ref, refresh_ref, h_ref, th_ref, lf_hbm, rf_hbm, lb_hbm, rb_hbm,
-                 w2, q_out, f2, b2, sems):
+        if most:
+            steps_until(START_BOUND, most, q2, h2, s2, t2, th2)
+        else:
+            one_step(q2, h2, s2, t2, th2)
+            one_step(q2, h2, s2, t2, th2)
+
+
+def prepare_last(order_ref, refresh_ref, h_ref, th_ref, lf_ref, rf_ref, lb_ref, rb_ref, w2, q_out):
 
     @pl.when(own_flag(order_ref, refresh_ref))
     def _():
-        copies = start_copies(
-            [(lb_hbm, b2.at[0]), (lf_hbm, f2.at[0]), (rb_hbm, b2.at[1]), (rf_hbm, f2.at[1])], sems
-        )
-        for side in range(2):
-            wait_copies(copies[2 * side : 2 * side + 2])
-            basis_hi, basis_lo = split(b2[side].T)
+        for side, (factor, basis) in enumerate(((lf_ref, lb_ref), (rf_ref, rb_ref))):
+            basis_hi, basis_lo = split(basis[...].T)
             w = dot(th_ref[side], basis_hi) + dot(th_ref[side], basis_lo)
             w_hi, w_lo = split(w)
-            factor_hi, factor_lo = split(f2[side])
+            factor_hi, factor_lo = split(factor[...])
             w2[side] = w_hi
             q_out[side] = 0.95 * (
                 dot(w_hi, factor_hi, NT) + dot(w_hi, factor_lo, NT) + dot(w_lo, factor_hi, NT)
@@ -266,6 +259,8 @@
         q2[1] = q_right
         h2[1] = q_right.astype(BF16)
 
+        one_step(q2, h2, s2, None, None)
+        one_step(q2, h2, s2, None, None)
         worst = steps_until(END_BOUND, 20, q2, h2, s2, None, None)
 
         @pl.when(jnp.logical_not(worst <= END_BOUND))
@@ -341,7 +336,6 @@
     square = (width, width)
     pair = (2,) + square
     work = [(pair, F32), (pair, F32), (pair, BF16)]
-    loads = [(pair, F32), (pair, F32)]
     slots = (block_order, refresh_ids)
     state_arrays = (left_factor[0], right_factor[0], left_basis[0], right_basis[0])
     steps = replicas - 1
@@ -353,15 +347,15 @@
         given = (tied, refresh_ids)
         if at == 0:
             return call(
-                prepare_start, "prepare_start", given, (), state_arrays,
-                [(pair, BF16)] * 2, scratch=loads, sems=[4], flops=flops,
+                prepare_start, "prepare_start", given, state_arrays, (),
+                [(pair, BF16)] * 2, flops=flops,
             )
         if at == 4:
             return call(
-                prepare_last, "prepare_last", given, state, state_arrays,
-                [(pair, BF16), (pair, F32)], scratch=loads, sems=[4], flops=flops,
+                prepare_last, "prepare_last", given, (*state, *state_arrays), (),
+                [(pair, BF16), (pair, F32)], flops=flops,
             )
-        kernel = prepare_boost if at == 1 else functools.partial(prepare_more, 3 if at == 2 else 16)
+        kernel = prepare_boost if at == 1 else functools.partial(prepare_more, 0 if at == 2 else 16)
         return call(
             kernel, "prepare_boost" if at == 1 else "prepare_more", given, state, (),
             [(pair, BF16)] * 2, scratch=work, flops=flops,

time: 434 us -> 433 us (level)
  Pallas kernels: 386 us -> 11.4 us
  blocking collectives: 24.3 us -> 382 us
  waiting for transfers between devices: 11.5 us -> 25.7 us
    pallas_call x13, Pallas kernels: 386 us -> 11.4 us  [call(): pl.pallas_call(kernel, out_shape=[jax.ShapeDtypeStruct(shape, dtype) for...]
    all_to_all x1, blocking collectives: 12.2 us -> 369 us  [on_device(): lax.all_to_all(update.reshape(owners, rows, width), 'fsdp', split_axis=0,...]
    ppermute x4, waiting for transfers between devices: 6.2 us -> 17.9 us  [on_device(): got[way] = lax.ppermute(send[way], 'replica', ways[way])]
  transfers between devices with their start and end apart: 6 -> 6, of which waited for: 4 -> 6; matrix products, arithmetic and copies ran while one was open for 0% -> 0% of each run, Pallas kernels for 4% -> 1%
where the time goes in v5:
time: 433 us
  blocking collectives  382 us (88%)
  waiting for transfers between devices  25.7 us (6%)
  Pallas kernels  11.4 us (3%)
  starting transfers between devices  8.76 us (2%)
    all_to_all x1, blocking collectives, on_device(): lax.all_to_all(update.reshape(owners, rows, width), 'fsdp', split_axis=0,...  369 us
    ppermute x4, waiting for transfers between devices, on_device(): got[way] = lax.ppermute(send[way], 'replica', ways[way])  17.9 us
    all_to_all x1, blocking collectives, on_device(): lax.all_to_all(summed, 'fsdp', split_axis=0, concat_axis=0, tiled=True)  12.7 us
    pallas_call x13, Pallas kernels, call(): pl.pallas_call(kernel, out_shape=[jax.ShapeDtypeStruct(shape, dtype) for...  11.4 us
  transfers between devices with their start and end apart: 6, of which 6 were waited for; matrix products, arithmetic and copies ran while one was open for 0% of the time, Pallas kernels for 1%

profile of v5, /device:TPU:0, one launch (start us, length us, event | category | flops | bytes accessed | tf_op | source)
XLA Modules:
  0.0 432.7 jit_solution(8729593284320435297)
XLA Ops:
  0.7 1.2 dynamic-slice_bitcast_fusion
  1.8 3.1 collective-permute-start
  4.9 2.1 collective-permute-start.2
  7.0 1.6 copy-done
  8.6 0.2 own_blocks.1
  8.8 5.3 %collective-permute-done.got_ref = bf16[8,64,256]{2,1,0:T(8,128)(2,1)S(1)} collective-permute-done((bf16[8,64,256]{2,1,0:T(8,128)(2,1)S(1)}, bf16[8,64,256]{2,1,0:T(8,128)(2,1)S(1)}, u32[]{:S(2)}, u32[]{:S(2)}) %collective-permute-start) | collective-permute-done | bytes 262176 | tf_op jit(solution)/shard_map/ppermute | solution.py:378
  14.1 0.1 add_right.2
  14.2 0.1 collective-permute-start.1
  14.3 0.0 copy-start.5
  14.3 1.2 copy-done.5
  15.5 0.6 prepare_start.1
  16.1 2.4 collective-permute-done.2.got_ref
  18.5 0.1 add_left.2
  18.6 3.2 collective-permute-start.4
  21.8 0.6 prepare_boost.1
  22.3 4.7 %collective-permute-done.1.got_ref = bf16[8,64,256]{2,1,0:T(8,128)(2,1)S(1)} collective-permute-done((bf16[8,64,256]{2,1,0:T(8,128)(2,1)S(1)}, bf16[8,64,256]{2,1,0:T(8,128)(2,1)S(1)}, u32[]{:S(2)}, u32[]{:S(2)}) %collective-permute-start.1) | collective-permute-done | bytes 262176 | tf_op jit(solution)/shard_map/ppermute | solution.py:396
  27.0 0.1 add_right.3
  27.1 0.1 collective-permute-start.3
  27.1 0.6 prepare_more.2
  27.7 4.9 %collective-permute-done.4.got_ref = bf16[8,64,256]{2,1,0:T(8,128)(2,1)S(1)} collective-permute-done((bf16[8,64,256]{2,1,0:T(8,128)(2,1)S(1)}, bf16[8,64,256]{2,1,0:T(8,128)(2,1)S(1)}, u32[]{:S(2)}, u32[]{:S(2)}) %collective-permute-start.4) | collective-permute-done | bytes 262176 | tf_op jit(solution)/shard_map/ppermute | solution.py:396
  32.6 0.1 add_left.3
  32.7 0.3 collective-permute-start.5
  33.0 0.6 prepare_more.3
  33.6 5.2 %collective-permute-done.3.got_right_ref = bf16[8,64,256]{2,1,0:T(8,128)(2,1)S(1)} collective-permute-done((bf16[8,64,256]{2,1,0:T(8,128)(2,1)S(1)}, bf16[8,64,256]{2,1,0:T(8,128)(2,1)S(1)}, u32[]{:S(2)}, u32[]{:S(2)}) %collective-permute-start.3) | collective-permute-done | bytes 262176 | tf_op jit(solution)/shard_map/ppermute | solution.py:396
  38.7 0.7 prepare_last.1
  39.5 0.0 copy-start.8
  39.5 3.2 collective-permute-done.5.got_left_ref
  42.7 0.7 finish.1
  43.4 12.7 %all_to_all.10 = bf16[8,64,512]{2,1,0:T(8,128)(2,1)S(1)} all-to-all(bf16[8,64,512]{2,1,0:T(8,128)(2,1)S(1)} %finish.1), channel_id=1, replica_groups=mesh['replica'=4,'fsdp'=8] {'fsdp'}, dimensions={0} | all-to-all | bytes 1048576 | tf_op jit(solution)/shard_map/all_to_all | solution.py:403
  56.1 5.9 %update.1 = (bf16[512,512]{1,0:T(8,128)(2,1)S(1)}, f32[512,512]{1,0:T(8,128)}, f32[512,512]{1,0:T(8,128)}) custom-call(s32[32]{0:T(128)S(1)} %copy-done.1, s32[3]{0:T(128)S(1)} %copy-done.9, bf16[512,512]{1,0:T(8,128)(2,1)S(1)} %bitcast.16, bf16[2,512,512]{2,1,0:T(8,128)(2,1)S(1)} %get-tuple-element.90.w_ref, f32[2,512,512]{2,1,0:T(8,128)S(1)} %get-tuple-element.91.q_ref, ...), custom_call_target="tpu_custom_call" | custom-call | flops 13421772800 | bytes 9961472 | tf_op jit(solution)/shard_map/update/pallas_call | solution.py:303
  62.0 369.1 %all_to_all.11.rows_ref = bf16[8,64,512]{2,1,0:T(8,128)(2,1)S(1)} all-to-all(bf16[8,64,512]{2,1,0:T(8,128)(2,1)S(1)} %bitcast.17), channel_id=1, replica_groups=mesh['replica'=4,'fsdp'=8] {'fsdp'}, dimensions={0} | all-to-all | bytes 1048576 | tf_op jit(solution)/shard_map/all_to_all | solution.py:411
  431.1 1.4 place.1
  (16 shorter events, 0.0 us)
Async XLA Ops:
  0.6 13.6 %copy-start.1 = (s32[32]{0:T(128)S(1)}, s32[32]{0:T(128)}, u32[]{:S(2)}) copy-start(s32[32]{0:T(128)} %order_ref.10) | copy-start | bytes 388
  0.6 13.6 %copy-start.9 = (s32[3]{0:T(128)S(1)}, s32[3]{0:T(128)}, u32[]{:S(2)}) copy-start(s32[3]{0:T(128)} %refresh_ref.11) | copy-start | bytes 40
  0.7 13.6 %copy-start.2 = (f32[1,512,512]{2,1,0:T(8,128)S(1)}, f32[1,512,512]{2,1,0:T(8,128)}, u32[]{:S(2)}) copy-start(f32[1,512,512]{2,1,0:T(8,128)} %param.12) | copy-start | bytes 3145732
  1.8 12.3 %collective-permute-start = (bf16[8,64,256]{2,1,0:T(8,128)(2,1)S(1)}, bf16[8,64,256]{2,1,0:T(8,128)(2,1)S(1)}, u32[]{:S(2)}, u32[]{:S(2)}) collective-permute-start(bf16[8,64,256]{2,1,0:T(8,128)(2,1)S(1)} %get-tuple-element.49), channel_id=1, source_target_pairs={{0,8},{8,16},{16,24},{24,0},{1,9},{9,17},{17,25},{25,1},{2,10},{10... | collective-permute-start | bytes 786440 | tf_op jit(solution)/shard_map/ppermute | solution.py:378
  4.9 13.6 %collective-permute-start.2 = (bf16[8,64,256]{2,1,0:T(8,128)(2,1)S(1)}, bf16[8,64,256]{2,1,0:T(8,128)(2,1)S(1)}, u32[]{:S(2)}, u32[]{:S(2)}) collective-permute-start(bf16[8,64,256]{2,1,0:T(8,128)(2,1)S(1)} %get-tuple-element.53), channel_id=1, source_target_pairs={{0,24},{8,0},{16,8},{24,16},{1,25},{9,1},{17,9},{25,17},{2,26},{10... | collective-permute-start | bytes 786440 | tf_op jit(solution)/shard_map/ppermute | solution.py:378
  7.0 1.6 copy-start
  8.6 5.7 %copy-start.3 = (f32[1,512,512]{2,1,0:T(8,128)S(1)}, f32[1,512,512]{2,1,0:T(8,128)}, u32[]{:S(2)}) copy-start(f32[1,512,512]{2,1,0:T(8,128)} %param.13) | copy-start | bytes 3145732
  8.6 5.7 %copy-start.4 = (f32[1,512,512]{2,1,0:T(8,128)S(1)}, f32[1,512,512]{2,1,0:T(8,128)}, u32[]{:S(2)}) copy-start(f32[1,512,512]{2,1,0:T(8,128)} %param.14) | copy-start | bytes 3145732
  14.2 12.8 %collective-permute-start.1 = (bf16[8,64,256]{2,1,0:T(8,128)(2,1)S(1)}, bf16[8,64,256]{2,1,0:T(8,128)(2,1)S(1)}, u32[]{:S(2)}, u32[]{:S(2)}) collective-permute-start(bf16[8,64,256]{2,1,0:T(8,128)(2,1)S(1)} %add_right.2), channel_id=1, source_target_pairs={{0,8},{8,16},{16,24},{24,0},{1,9},{9,17},{17,25},{25,1},{2,10},{10... | collective-permute-start | bytes 786440 | tf_op jit(solution)/shard_map/ppermute | solution.py:396
  14.3 1.2 copy-start.5
  18.6 14.0 %collective-permute-start.4 = (bf16[8,64,256]{2,1,0:T(8,128)(2,1)S(1)}, bf16[8,64,256]{2,1,0:T(8,128)(2,1)S(1)}, u32[]{:S(2)}, u32[]{:S(2)}) collective-permute-start(bf16[8,64,256]{2,1,0:T(8,128)(2,1)S(1)} %add_left.2), channel_id=1, source_target_pairs={{0,24},{8,0},{16,8},{24,16},{1,25},{9,1},{17,9},{25,17},{2,26},{10... | collective-permute-start | bytes 786440 | tf_op jit(solution)/shard_map/ppermute | solution.py:396
  27.1 11.7 %collective-permute-start.3 = (bf16[8,64,256]{2,1,0:T(8,128)(2,1)S(1)}, bf16[8,64,256]{2,1,0:T(8,128)(2,1)S(1)}, u32[]{:S(2)}, u32[]{:S(2)}) collective-permute-start(bf16[8,64,256]{2,1,0:T(8,128)(2,1)S(1)} %add_right.3), channel_id=1, source_target_pairs={{0,8},{8,16},{16,24},{24,0},{1,9},{9,17},{17,25},{25,1},{2,10},{10... | collective-permute-start | bytes 786440 | tf_op jit(solution)/shard_map/ppermute | solution.py:396
  32.7 6.1 %copy-start.6 = (f32[1,512,512]{2,1,0:T(8,128)S(1)}, f32[1,512,512]{2,1,0:T(8,128)}, u32[]{:S(2)}) copy-start(f32[1,512,512]{2,1,0:T(8,128)} %param.15) | copy-start | bytes 3145732
  32.7 10.0 %collective-permute-start.5 = (bf16[8,64,256]{2,1,0:T(8,128)(2,1)S(1)}, bf16[8,64,256]{2,1,0:T(8,128)(2,1)S(1)}, u32[]{:S(2)}, u32[]{:S(2)}) collective-permute-start(bf16[8,64,256]{2,1,0:T(8,128)(2,1)S(1)} %add_left.3), channel_id=1, source_target_pairs={{0,24},{8,0},{16,8},{24,16},{1,25},{9,1},{17,9},{25,17},{2,26},{10... | collective-permute-start | bytes 786440 | tf_op jit(solution)/shard_map/ppermute | solution.py:396
  39.5 16.6 %copy-start.7 = (f32[1,512,512]{2,1,0:T(8,128)S(1)}, f32[1,512,512]{2,1,0:T(8,128)}, u32[]{:S(2)}) copy-start(f32[1,512,512]{2,1,0:T(8,128)} %param.10) | copy-start | bytes 3145732
  39.5 16.6 %copy-start.8 = (f32[1,512,512]{2,1,0:T(8,128)S(1)}, f32[1,512,512]{2,1,0:T(8,128)}, u32[]{:S(2)}) copy-start(f32[1,512,512]{2,1,0:T(8,128)} %param.11) | copy-start | bytes 3145732

commit v6 on v5

--- a/solution.py
+++ b/solution.py
@@ -189,38 +189,40 @@
     lax.fori_loop(0, width, one, 0)
 
 
-def slice_kernel(parts_hbm, *rest):
+def target_group(hop, turn, replicas):
+    return jnp.where(lax.axis_index("replica") == hop, replicas - 1 - turn, turn)
+
+
+def slice_kernel(sends, parts_hbm, *rest):
     outs, sems = rest[:-1], rest[-1]
     replicas = lax.axis_size("replica")
     slots, _, half = outs[0].shape
+    groups = [target_group(hop, turn, replicas) for hop, turn in sends]
+    groups.append(lax.axis_index("replica"))
     pairs = []
-    for event, out in enumerate(outs):
-        step, way = divmod(event, 2)
-        first = passing_group(step + 1, way, replicas) * slots
-        pairs.append((parts_hbm.at[pl.ds(first, slots), :, pl.ds(way * half, half)], out))
+    for at, out in enumerate(outs):
+        number, part = divmod(at, 2)
+        source = parts_hbm.at[pl.ds(groups[number] * slots, slots), :, pl.ds(part * half, half)]
+        pairs.append((source, out))
     wait_copies(start_copies(pairs, sems))
-
-
-def passing_group(step, way, replicas):
-    ahead = (2 * replicas - 1 - step) if way == 0 else (1 + step)
-    return lax.rem(lax.axis_index("replica") + ahead, replicas)
 
 
 def add_kernel(got_ref, own_ref, out_ref):
     out_ref[...] = (got_ref[...].astype(F32) + own_ref[...].astype(F32)).astype(BF16)
 
 
-def finish_kernel(order_ref, got_right_ref, got_left_ref, own_right_ref, own_left_ref, out_ref):
-    slots = out_ref.shape[0]
-    half = got_right_ref.shape[2]
+def finish_kernel(order_ref, *rest):
+    refs, out_ref = rest[:-1], rest[-1]
+    slots, _, width = out_ref.shape
+    half = width // 2
     first = lax.axis_index("replica") * slots
     for i in range(slots):
         at = order_ref[first + i] - first
-        for got_ref, own_ref, cols in (
-            (got_right_ref, own_right_ref, slice(0, half)),
-            (got_left_ref, own_left_ref, slice(half, 2 * half)),
-        ):
-            out_ref[i, :, cols] = (got_ref[at].astype(F32) + own_ref[at].astype(F32)).astype(BF16)
+        for part in range(2):
+            total = refs[part][at].astype(F32)
+            for ref in refs[part + 2 :: 2]:
+                total += ref[at].astype(F32)
+            out_ref[i, :, pl.ds(part * half, half)] = total.astype(BF16)
 
 
 def place_kernel(order_ref, rows_ref, out_hbm, sems):
@@ -287,7 +289,8 @@
         dot(part_hi, right_hi, NT) + dot(part_hi, right_lo, NT) + dot(part_lo, right_hi, NT)
     )
     second = 0.95 * second_ref[...] + 0.05 * rotated * rotated
-    scaled = (moment / (jnp.sqrt(second) + 1e-8)).astype(BF16)
+    root = second * lax.rsqrt(second) + 1e-8
+    scaled = (moment * pl.reciprocal(root, approx=True)).astype(BF16)
     part = (dot(left_hi.T, scaled) + dot(left_lo.T, scaled)).astype(BF16)
     update_ref[...] = (dot(part, right_hi) + dot(part, right_lo)).astype(BF16)
     wait_copies(out_copies)
@@ -338,7 +341,6 @@
     work = [(pair, F32), (pair, F32), (pair, BF16)]
     slots = (block_order, refresh_ids)
     state_arrays = (left_factor[0], right_factor[0], left_basis[0], right_basis[0])
-    steps = replicas - 1
 
     chunk = ((group_size, rows, width // 2), BF16)
 
@@ -361,43 +363,47 @@
             [(pair, BF16)] * 2, scratch=work, flops=flops,
         )
 
-    ways = (
-        [(i, (i + 1) % replicas) for i in range(replicas)],
-        [(i, (i - 1) % replicas) for i in range(replicas)],
-    )
     half = width // 2
-    send = [
-        lax.dynamic_slice(
-            grad_parts[0],
-            (passing_group(0, way, replicas) * group_size, 0, way * half),
-            (group_size, rows, half),
+    places = [(hop, turn) for hop in range(replicas - 1) for turn in range(replicas - 1 - hop)]
+    blocks = call(
+        functools.partial(slice_kernel, places[1:]), "own_blocks", (), (), (grad_parts[0],),
+        [chunk] * (2 * len(places)), sems=[2 * len(places)],
+    )
+    own = {place: blocks[2 * i : 2 * i + 2] for i, place in enumerate(places[1:])}
+    first = target_group(0, 0, replicas) * group_size
+    send = {}
+    for part in range(2):
+        piece = lax.dynamic_slice(
+            grad_parts[0], (first, 0, part * half), (group_size, rows, half)
         )
-        for way in range(2)
-    ]
-    tied, *send = lax.optimization_barrier((block_order, *send))
-    got = [lax.ppermute(send[way], "replica", ways[way]) for way in range(2)]
-    own = list(
-        call(
-            slice_kernel, "own_blocks", (), (), (grad_parts[0],), [chunk] * (2 * steps),
-            sems=[2 * steps],
-        )
-    )
+        send[0, 0, part] = piece
+    got = {}
     state = ()
-    for event in range(2 * steps):
-        way = event % 2
-        if 0 < event < 6:
-            state = stage(event - 1, tied, state)
-            own[event], *state = lax.optimization_barrier((own[event], *state))
-        if event < 2 * steps - 2:
-            (send[way],) = call(
-                add_kernel, ("add_right", "add_left")[way], (), (got[way], own[event]), (), [chunk]
+    waves = sorted(places, key=lambda place: (place[0] + place[1], place[0]))
+    for hop, turn in waves:
+        for part in range(2):
+            if hop == 0 and turn > 0:
+                send[0, turn, part], got[0, turn - 1, part] = lax.optimization_barrier(
+                    (own[0, turn][part], got[0, turn - 1, part])
+                )
+            if hop > 0:
+                (send[hop, turn, part],) = call(
+                    add_kernel, f"add_{hop}_{turn}_{part}", (),
+                    (got[hop - 1, turn, part], own[hop, turn][part]), (), [chunk],
+                )
+            got[hop, turn, part] = lax.ppermute(
+                send[hop, turn, part], "replica",
+                [(hop, hop + 1), (replicas - 1 - hop, replicas - 2 - hop)],
             )
-            tied, send[way] = lax.optimization_barrier((block_order, send[way]))
-            got[way] = lax.ppermute(send[way], "replica", ways[way])
-        elif way == 0:
-            tied, got[0] = lax.optimization_barrier((block_order, got[0]))
+    mine = list(blocks[-2:])
+    for piece in range(5):
+        turn, part = divmod(piece, 2)
+        tied, got[0, turn, part] = lax.optimization_barrier((block_order, got[0, turn, part]))
+        state = stage(piece, tied, state)
+    mine[0], *state = lax.optimization_barrier((mine[0], *state))
+    ends = [got[hop, replicas - 2 - hop, part] for hop in range(replicas - 1) for part in range(2)]
     (summed,) = call(
-        finish_kernel, "finish", (block_order,), (*got, *own[-2:]), (),
+        finish_kernel, "finish", (block_order,), (*mine, *ends), (),
         [((group_size, rows, width), BF16)],
     )
     gradient = lax.all_to_all(summed, "fsdp", split_axis=0, concat_axis=0, tiled=True)

time: 433 us -> 447 us (1.032)
  starting transfers between devices: 8.76 us -> 33.5 us
  waiting for transfers between devices: 25.7 us -> 8.83 us
  blocking collectives: 382 us -> 387 us
    ppermute x6 -> x12, starting transfers between devices: 8.76 us -> 33.5 us  [on_device(): lax.ppermute(send[hop, turn, part], 'replica', [(hop, hop + 1), (replicas...]
    ppermute x6 -> x12, waiting for transfers between devices: 25.7 us -> 8.83 us  [on_device(): lax.ppermute(send[hop, turn, part], 'replica', [(hop, hop + 1), (replicas...]
    all_to_all x1, blocking collectives: 12.7 us -> 17.2 us  [on_device(): lax.all_to_all(summed, 'fsdp', split_axis=0, concat_axis=0, tiled=True)]
    pallas_call x13 -> x15, Pallas kernels: 11.4 us -> 11.7 us  [call(): pl.pallas_call(kernel, out_shape=[jax.ShapeDtypeStruct(shape, dtype) for...]
  transfers between devices with their start and end apart: 6 -> 12, of which waited for: 6 -> 3; matrix products, arithmetic and copies ran while one was open for 0% -> 0% of each run, Pallas kernels for 1% -> 1%
where the time goes in v6:
time: 447 us; the launch traced here: 445 us
  blocking collectives  387 us (87%)
  starting transfers between devices  33.5 us (7%)
  Pallas kernels  11.7 us (3%)
  waiting for transfers between devices  8.83 us (2%)
    all_to_all x1, blocking collectives, on_device(): lax.all_to_all(update.reshape(owners, rows, width), 'fsdp', split_axis=0,...  370 us
    ppermute x12, starting transfers between devices, on_device(): lax.ppermute(send[hop, turn, part], 'replica', [(hop, hop + 1), (replicas...  33.5 us
    all_to_all x1, blocking collectives, on_device(): lax.all_to_all(summed, 'fsdp', split_axis=0, concat_axis=0, tiled=True)  17.2 us
    pallas_call x15, Pallas kernels, call(): pl.pallas_call(kernel, out_shape=[jax.ShapeDtypeStruct(shape, dtype) for...  11.7 us
  transfers between devices with their start and end apart: 12, of which 3 were waited for; matrix products, arithmetic and copies ran while one was open for 0% of the time, Pallas kernels for 1%

profile of v6, /device:TPU:0, one launch (start us, length us, event | category | flops | bytes accessed | tf_op | source)
XLA Modules:
  0.0 444.7 jit_solution(16341228949619451468)
XLA Ops:
  0.6 1.2 dynamic-slice_bitcast_fusion
  1.8 4.9 %collective-permute-start = (bf16[8,64,256]{2,1,0:T(8,128)(2,1)S(1)}, bf16[8,64,256]{2,1,0:T(8,128)(2,1)S(1)}, u32[]{:S(2)}, u32[]{:S(2)}) collective-permute-start(bf16[8,64,256]{2,1,0:T(8,128)(2,1)S(1)} %get-tuple-element.88), channel_id=1, source_target_pairs={{0,8},{24,16},{1,9},{25,17},{2,10},{26,18},{3,11},{27,19},{4,12},{... | collective-permute-start | bytes 786440 | tf_op jit(solution)/shard_map/ppermute | solution.py:394
  6.8 1.3 collective-permute-start.3
  8.1 1.6 copy-done
  9.7 0.3 own_blocks.1
  10.1 3.4 collective-permute-done.got_ref
  13.5 4.4 collective-permute-start.1
  17.9 0.1 add_1_0_0.1
  17.9 1.1 collective-permute-done.3.got_ref
  19.1 0.7 collective-permute-start.10
  19.8 7.2 %collective-permute-start.4 = (bf16[8,64,256]{2,1,0:T(8,128)(2,1)S(1)}, bf16[8,64,256]{2,1,0:T(8,128)(2,1)S(1)}, u32[]{:S(2)}, u32[]{:S(2)}) collective-permute-start(bf16[8,64,256]{2,1,0:T(8,128)(2,1)S(1)} %get-tuple-element.53), channel_id=1, source_target_pairs={{0,8},{24,16},{1,9},{25,17},{2,10},{26,18},{3,11},{27,19},{4,12},{... | collective-permute-start | bytes 786440 | tf_op jit(solution)/shard_map/ppermute | solution.py:394
  27.0 0.7 collective-permute-start.8
  27.8 0.6 prepare_start.1
  28.4 3.0 collective-permute-start.2
  31.4 0.6 prepare_boost.1
  31.9 0.1 add_2_0_1.1
  32.0 1.3 collective-permute-start.11
  33.4 0.7 collective-permute-start.7
  34.1 7.4 %collective-permute-start.5 = (bf16[8,64,256]{2,1,0:T(8,128)(2,1)S(1)}, bf16[8,64,256]{2,1,0:T(8,128)(2,1)S(1)}, u32[]{:S(2)}, u32[]{:S(2)}) collective-permute-start(bf16[8,64,256]{2,1,0:T(8,128)(2,1)S(1)} %get-tuple-element.75), channel_id=1, source_target_pairs={{0,8},{24,16},{1,9},{25,17},{2,10},{26,18},{3,11},{27,19},{4,12},{... | collective-permute-start | bytes 786440 | tf_op jit(solution)/shard_map/ppermute | solution.py:394
  41.5 0.1 add_2_0_0.1
  41.5 1.3 collective-permute-start.9
  42.8 0.1 add_1_1_0.1
  42.9 0.6 prepare_more.2
  43.5 0.7 collective-permute-start.6
  44.2 0.6 prepare_more.3
  44.8 0.7 prepare_last.1
  45.6 4.2 collective-permute-done.9.rest_6_
  49.8 0.8 finish.1
  50.6 17.2 %all_to_all.10 = bf16[8,64,512]{2,1,0:T(8,128)(2,1)S(1)} all-to-all(bf16[8,64,512]{2,1,0:T(8,128)(2,1)S(1)} %finish.1), channel_id=1, replica_groups=mesh['replica'=4,'fsdp'=8] {'fsdp'}, dimensions={0} | all-to-all | bytes 1048576 | tf_op jit(solution)/shard_map/all_to_all | solution.py:409
  67.8 5.7 %update.1 = (bf16[512,512]{1,0:T(8,128)(2,1)S(1)}, f32[512,512]{1,0:T(8,128)}, f32[512,512]{1,0:T(8,128)}) custom-call(s32[32]{0:T(128)S(1)} %copy-done.1, s32[3]{0:T(128)S(1)} %copy-done.8, bf16[512,512]{1,0:T(8,128)(2,1)S(1)} %bitcast.16, bf16[2,512,512]{2,1,0:T(8,128)(2,1)S(1)} %get-tuple-element.82.w_ref, f32[2,512,512]{2,1,0:T(8,128)S(1)} %get-tuple-element.83.q_ref, ...), custom_call_target="tpu_custom_call" | custom-call | flops 13421772800 | bytes 9961472 | tf_op jit(solution)/shard_map/update/pallas_call | solution.py:306
  73.6 369.5 %all_to_all.11.rows_ref = bf16[8,64,512]{2,1,0:T(8,128)(2,1)S(1)} all-to-all(bf16[8,64,512]{2,1,0:T(8,128)(2,1)S(1)} %bitcast.17), channel_id=1, replica_groups=mesh['replica'=4,'fsdp'=8] {'fsdp'}, dimensions={0} | all-to-all | bytes 1048576 | tf_op jit(solution)/shard_map/all_to_all | solution.py:417
  443.1 1.4 place.1
  (28 shorter events, 0.2 us)
Async XLA Ops:
  0.6 27.1 %copy-start.2 = (f32[1,512,512]{2,1,0:T(8,128)S(1)}, f32[1,512,512]{2,1,0:T(8,128)}, u32[]{:S(2)}) copy-start(f32[1,512,512]{2,1,0:T(8,128)} %param.12) | copy-start | bytes 3145732
  1.8 25.9 %copy-start.1 = (s32[32]{0:T(128)S(1)}, s32[32]{0:T(128)}, u32[]{:S(2)}) copy-start(s32[32]{0:T(128)} %order_ref.10) | copy-start | bytes 388
  1.8 25.9 %copy-start.8 = (s32[3]{0:T(128)S(1)}, s32[3]{0:T(128)}, u32[]{:S(2)}) copy-start(s32[3]{0:T(128)} %refresh_ref.11) | copy-start | bytes 40
  1.8 11.6 %collective-permute-start = (bf16[8,64,256]{2,1,0:T(8,128)(2,1)S(1)}, bf16[8,64,256]{2,1,0:T(8,128)(2,1)S(1)}, u32[]{:S(2)}, u32[]{:S(2)}) collective-permute-start(bf16[8,64,256]{2,1,0:T(8,128)(2,1)S(1)} %get-tuple-element.88), channel_id=1, source_target_pairs={{0,8},{24,16},{1,9},{25,17},{2,10},{26,18},{3,11},{27,19},{4,12},{... | collective-permute-start | bytes 786440 | tf_op jit(solution)/shard_map/ppermute | solution.py:394
  6.8 12.3 %collective-permute-start.3 = (bf16[8,64,256]{2,1,0:T(8,128)(2,1)S(1)}, bf16[8,64,256]{2,1,0:T(8,128)(2,1)S(1)}, u32[]{:S(2)}, u32[]{:S(2)}) collective-permute-start(bf16[8,64,256]{2,1,0:T(8,128)(2,1)S(1)} %get-tuple-element.87), channel_id=1, source_target_pairs={{0,8},{24,16},{1,9},{25,17},{2,10},{26,18},{3,11},{27,19},{4,12},{... | collective-permute-start | bytes 786440 | tf_op jit(solution)/shard_map/ppermute | solution.py:394
  8.1 1.6 copy-start
  9.7 18.1 %copy-start.3 = (f32[1,512,512]{2,1,0:T(8,128)S(1)}, f32[1,512,512]{2,1,0:T(8,128)}, u32[]{:S(2)}) copy-start(f32[1,512,512]{2,1,0:T(8,128)} %param.13) | copy-start | bytes 3145732
  9.7 18.1 %copy-start.4 = (f32[1,512,512]{2,1,0:T(8,128)S(1)}, f32[1,512,512]{2,1,0:T(8,128)}, u32[]{:S(2)}) copy-start(f32[1,512,512]{2,1,0:T(8,128)} %param.14) | copy-start | bytes 3145732
  9.7 18.1 %copy-start.5 = (f32[1,512,512]{2,1,0:T(8,128)S(1)}, f32[1,512,512]{2,1,0:T(8,128)}, u32[]{:S(2)}) copy-start(f32[1,512,512]{2,1,0:T(8,128)} %param.15) | copy-start | bytes 3145732
  13.5 14.9 %collective-permute-start.1 = (bf16[8,64,256]{2,1,0:T(8,128)(2,1)S(1)}, bf16[8,64,256]{2,1,0:T(8,128)(2,1)S(1)}, u32[]{:S(2)}, u32[]{:S(2)}) collective-permute-start(bf16[8,64,256]{2,1,0:T(8,128)(2,1)S(1)} %get-tuple-element.48), channel_id=1, source_target_pairs={{0,8},{24,16},{1,9},{25,17},{2,10},{26,18},{3,11},{27,19},{4,12},{... | collective-permute-start | bytes 786440 | tf_op jit(solution)/shard_map/ppermute | solution.py:394
  19.1 12.8 %collective-permute-start.10 = (bf16[8,64,256]{2,1,0:T(8,128)(2,1)S(1)}, bf16[8,64,256]{2,1,0:T(8,128)(2,1)S(1)}, u32[]{:S(2)}, u32[]{:S(2)}) collective-permute-start(bf16[8,64,256]{2,1,0:T(8,128)(2,1)S(1)} %add_1_0_1.1), channel_id=1, source_target_pairs={{8,16},{16,8},{9,17},{17,9},{10,18},{18,10},{11,19},{19,11},{12,20... | collective-permute-start | bytes 786440 | tf_op jit(solution)/shard_map/ppermute | solution.py:394
  19.8 13.5 %collective-permute-start.4 = (bf16[8,64,256]{2,1,0:T(8,128)(2,1)S(1)}, bf16[8,64,256]{2,1,0:T(8,128)(2,1)S(1)}, u32[]{:S(2)}, u32[]{:S(2)}) collective-permute-start(bf16[8,64,256]{2,1,0:T(8,128)(2,1)S(1)} %get-tuple-element.53), channel_id=1, source_target_pairs={{0,8},{24,16},{1,9},{25,17},{2,10},{26,18},{3,11},{27,19},{4,12},{... | collective-permute-start | bytes 786440 | tf_op jit(solution)/shard_map/ppermute | solution.py:394
  27.0 14.4 %collective-permute-start.8 = (bf16[8,64,256]{2,1,0:T(8,128)(2,1)S(1)}, bf16[8,64,256]{2,1,0:T(8,128)(2,1)S(1)}, u32[]{:S(2)}, u32[]{:S(2)}) collective-permute-start(bf16[8,64,256]{2,1,0:T(8,128)(2,1)S(1)} %add_1_0_0.1), channel_id=1, source_target_pairs={{8,16},{16,8},{9,17},{17,9},{10,18},{18,10},{11,19},{19,11},{12,20... | collective-permute-start | bytes 786440 | tf_op jit(solution)/shard_map/ppermute | solution.py:394
  28.4 15.1 %collective-permute-start.2 = (bf16[8,64,256]{2,1,0:T(8,128)(2,1)S(1)}, bf16[8,64,256]{2,1,0:T(8,128)(2,1)S(1)}, u32[]{:S(2)}, u32[]{:S(2)}) collective-permute-start(bf16[8,64,256]{2,1,0:T(8,128)(2,1)S(1)} %get-tuple-element.49), channel_id=1, source_target_pairs={{0,8},{24,16},{1,9},{25,17},{2,10},{26,18},{3,11},{27,19},{4,12},{... | collective-permute-start | bytes 786440 | tf_op jit(solution)/shard_map/ppermute | solution.py:394
  32.0 13.5 %collective-permute-start.11 = (bf16[8,64,256]{2,1,0:T(8,128)(2,1)S(1)}, bf16[8,64,256]{2,1,0:T(8,128)(2,1)S(1)}, u32[]{:S(2)}, u32[]{:S(2)}) collective-permute-start(bf16[8,64,256]{2,1,0:T(8,128)(2,1)S(1)} %add_2_0_1.1), channel_id=1, source_target_pairs={{16,24},{8,0},{17,25},{9,1},{18,26},{10,2},{19,27},{11,3},{20,28},... | collective-permute-start | bytes 786440 | tf_op jit(solution)/shard_map/ppermute | solution.py:394
  33.4 12.2 %collective-permute-start.7 = (bf16[8,64,256]{2,1,0:T(8,128)(2,1)S(1)}, bf16[8,64,256]{2,1,0:T(8,128)(2,1)S(1)}, u32[]{:S(2)}, u32[]{:S(2)}) collective-permute-start(bf16[8,64,256]{2,1,0:T(8,128)(2,1)S(1)} %add_1_1_1.1), channel_id=1, source_target_pairs={{8,16},{16,8},{9,17},{17,9},{10,18},{18,10},{11,19},{19,11},{12,20... | collective-permute-start | bytes 786440 | tf_op jit(solution)/shard_map/ppermute | solution.py:394
  34.1 11.5 %collective-permute-start.5 = (bf16[8,64,256]{2,1,0:T(8,128)(2,1)S(1)}, bf16[8,64,256]{2,1,0:T(8,128)(2,1)S(1)}, u32[]{:S(2)}, u32[]{:S(2)}) collective-permute-start(bf16[8,64,256]{2,1,0:T(8,128)(2,1)S(1)} %get-tuple-element.75), channel_id=1, source_target_pairs={{0,8},{24,16},{1,9},{25,17},{2,10},{26,18},{3,11},{27,19},{4,12},{... | collective-permute-start | bytes 786440 | tf_op jit(solution)/shard_map/ppermute | solution.py:394
  41.5 8.3 %collective-permute-start.9 = (bf16[8,64,256]{2,1,0:T(8,128)(2,1)S(1)}, bf16[8,64,256]{2,1,0:T(8,128)(2,1)S(1)}, u32[]{:S(2)}, u32[]{:S(2)}) collective-permute-start(bf16[8,64,256]{2,1,0:T(8,128)(2,1)S(1)} %add_2_0_0.1), channel_id=1, source_target_pairs={{16,24},{8,0},{17,25},{9,1},{18,26},{10,2},{19,27},{11,3},{20,28},... | collective-permute-start | bytes 786440 | tf_op jit(solution)/shard_map/ppermute | solution.py:394
  43.5 6.3 %collective-permute-start.6 = (bf16[8,64,256]{2,1,0:T(8,128)(2,1)S(1)}, bf16[8,64,256]{2,1,0:T(8,128)(2,1)S(1)}, u32[]{:S(2)}, u32[]{:S(2)}) collective-permute-start(bf16[8,64,256]{2,1,0:T(8,128)(2,1)S(1)} %add_1_1_0.1), channel_id=1, source_target_pairs={{8,16},{16,8},{9,17},{17,9},{10,18},{18,10},{11,19},{19,11},{12,20... | collective-permute-start | bytes 786440 | tf_op jit(solution)/shard_map/ppermute | solution.py:394
  45.5 22.3 %copy-start.6 = (f32[1,512,512]{2,1,0:T(8,128)S(1)}, f32[1,512,512]{2,1,0:T(8,128)}, u32[]{:S(2)}) copy-start(f32[1,512,512]{2,1,0:T(8,128)} %param.10) | copy-start | bytes 3145732
  45.5 22.3 %copy-start.7 = (f32[1,512,512]{2,1,0:T(8,128)S(1)}, f32[1,512,512]{2,1,0:T(8,128)}, u32[]{:S(2)}) copy-start(f32[1,512,512]{2,1,0:T(8,128)} %param.11) | copy-start | bytes 3145732

commit v7 on v5

--- a/solution.py
+++ b/solution.py
@@ -144,18 +144,15 @@
         load_state(h_ref, th_ref, h2, th2, q2, t2)
         for _ in range(2):
             one_step(q2, h2, s2, t2, th2, 1.3, 1.4)
+
+
+def prepare_more(order_ref, refresh_ref, h_ref, th_ref, h2, th2, q2, t2, s2):
+    @pl.when(own_flag(order_ref, refresh_ref))
+    def _():
+        load_state(h_ref, th_ref, h2, th2, q2, t2)
         one_step(q2, h2, s2, t2, th2)
-
-
-def prepare_more(most, order_ref, refresh_ref, h_ref, th_ref, h2, th2, q2, t2, s2):
-    @pl.when(own_flag(order_ref, refresh_ref))
-    def _():
-        load_state(h_ref, th_ref, h2, th2, q2, t2)
-        if most:
-            steps_until(START_BOUND, most, q2, h2, s2, t2, th2)
-        else:
-            one_step(q2, h2, s2, t2, th2)
-            one_step(q2, h2, s2, t2, th2)
+        one_step(q2, h2, s2, t2, th2)
+        steps_until(START_BOUND, 16, q2, h2, s2, t2, th2)
 
 
 def prepare_last(order_ref, refresh_ref, h_ref, th_ref, lf_ref, rf_ref, lb_ref, rb_ref, w2, q_out):
@@ -287,7 +284,8 @@
         dot(part_hi, right_hi, NT) + dot(part_hi, right_lo, NT) + dot(part_lo, right_hi, NT)
     )
     second = 0.95 * second_ref[...] + 0.05 * rotated * rotated
-    scaled = (moment / (jnp.sqrt(second) + 1e-8)).astype(BF16)
+    root = second * lax.rsqrt(second) + 1e-8
+    scaled = (moment * pl.reciprocal(root, approx=True)).astype(BF16)
     part = (dot(left_hi.T, scaled) + dot(left_lo.T, scaled)).astype(BF16)
     update_ref[...] = (dot(part, right_hi) + dot(part, right_lo)).astype(BF16)
     wait_copies(out_copies)
@@ -350,15 +348,14 @@
                 prepare_start, "prepare_start", given, state_arrays, (),
                 [(pair, BF16)] * 2, flops=flops,
             )
-        if at == 4:
+        if at == 3:
             return call(
                 prepare_last, "prepare_last", given, (*state, *state_arrays), (),
                 [(pair, BF16), (pair, F32)], flops=flops,
             )
-        kernel = prepare_boost if at == 1 else functools.partial(prepare_more, 0 if at == 2 else 16)
         return call(
-            kernel, "prepare_boost" if at == 1 else "prepare_more", given, state, (),
-            [(pair, BF16)] * 2, scratch=work, flops=flops,
+            prepare_boost if at == 1 else prepare_more, "prepare_boost" if at == 1 else "prepare_more",
+            given, state, (), [(pair, BF16)] * 2, scratch=work, flops=flops,
         )
 
     ways = (
@@ -385,8 +382,8 @@
     state = ()
     for event in range(2 * steps):
         way = event % 2
-        if 0 < event < 6:
-            state = stage(event - 1, tied, state)
+        if 1 < event < 6:
+            state = stage(event - 2, tied, state)
             own[event], *state = lax.optimization_barrier((own[event], *state))
         if event < 2 * steps - 2:
             (send[way],) = call(

time: 433 us -> 434 us (level)
    pallas_call x13 -> x12, Pallas kernels: 11.4 us -> 10.5 us  [call(): pl.pallas_call(kernel, out_shape=[jax.ShapeDtypeStruct(shape, dtype) for...]
where the time goes in v7:
time: 434 us
  blocking collectives  383 us (88%)
  waiting for transfers between devices  27.7 us (6%)
  Pallas kernels  10.5 us (2%)
  starting transfers between devices  8.71 us (2%)
    all_to_all x1, blocking collectives, on_device(): lax.all_to_all(update.reshape(owners, rows, width), 'fsdp', split_axis=0,...  369 us
    ppermute x4, waiting for transfers between devices, on_device(): got[way] = lax.ppermute(send[way], 'replica', ways[way])  18.1 us
    all_to_all x1, blocking collectives, on_device(): lax.all_to_all(summed, 'fsdp', split_axis=0, concat_axis=0, tiled=True)  14.1 us
    pallas_call x12, Pallas kernels, call(): pl.pallas_call(kernel, out_shape=[jax.ShapeDtypeStruct(shape, dtype) for...  10.5 us
    ppermute x2, waiting for transfers between devices, on_device(): got = [lax.ppermute(send[way], 'replica', ways[way]) for way in range(2)]  9.6 us
  transfers between devices with their start and end apart: 6, of which 6 were waited for; matrix products, arithmetic and copies ran while one was open for 0% of the time, Pallas kernels for 1%

profile of v7, /device:TPU:0, one launch (start us, length us, event | category | flops | bytes accessed | tf_op | source)
XLA Modules:
  0.0 433.8 jit_solution(6011156228061042149)
XLA Ops:
  0.7 1.2 dynamic-slice_bitcast_fusion
  1.8 0.0 copy-start.1
  1.8 0.0 copy-start.8
  1.8 3.1 collective-permute-start
  4.9 2.1 collective-permute-start.2
  7.0 1.6 copy-done
  8.6 0.2 own_blocks.1
  8.8 5.3 %collective-permute-done.got_ref = bf16[8,64,256]{2,1,0:T(8,128)(2,1)S(1)} collective-permute-done((bf16[8,64,256]{2,1,0:T(8,128)(2,1)S(1)}, bf16[8,64,256]{2,1,0:T(8,128)(2,1)S(1)}, u32[]{:S(2)}, u32[]{:S(2)}) %collective-permute-start) | collective-permute-done | bytes 262176 | tf_op jit(solution)/shard_map/ppermute | solution.py:375
  14.1 0.1 add_right.2
  14.2 0.1 collective-permute-start.1
  14.3 4.3 collective-permute-done.2.got_ref
  18.5 0.1 add_left.2
  18.6 3.1 collective-permute-start.4
  21.7 0.6 prepare_start.1
  22.3 4.7 %collective-permute-done.1.got_ref = bf16[8,64,256]{2,1,0:T(8,128)(2,1)S(1)} collective-permute-done((bf16[8,64,256]{2,1,0:T(8,128)(2,1)S(1)}, bf16[8,64,256]{2,1,0:T(8,128)(2,1)S(1)}, u32[]{:S(2)}, u32[]{:S(2)}) %collective-permute-start.1) | collective-permute-done | bytes 262176 | tf_op jit(solution)/shard_map/ppermute | solution.py:393
  27.0 0.1 add_right.3
  27.1 0.1 collective-permute-start.3
  27.1 0.6 prepare_boost.1
  27.7 4.9 %collective-permute-done.4.got_ref = bf16[8,64,256]{2,1,0:T(8,128)(2,1)S(1)} collective-permute-done((bf16[8,64,256]{2,1,0:T(8,128)(2,1)S(1)}, bf16[8,64,256]{2,1,0:T(8,128)(2,1)S(1)}, u32[]{:S(2)}, u32[]{:S(2)}) %collective-permute-start.4) | collective-permute-done | bytes 262176 | tf_op jit(solution)/shard_map/ppermute | solution.py:393
  32.6 0.1 add_left.3
  32.7 0.3 collective-permute-start.5
  33.0 0.6 prepare_more.1
  33.5 5.3 %collective-permute-done.3.got_right_ref = bf16[8,64,256]{2,1,0:T(8,128)(2,1)S(1)} collective-permute-done((bf16[8,64,256]{2,1,0:T(8,128)(2,1)S(1)}, bf16[8,64,256]{2,1,0:T(8,128)(2,1)S(1)}, u32[]{:S(2)}, u32[]{:S(2)}) %collective-permute-start.3) | collective-permute-done | bytes 262176 | tf_op jit(solution)/shard_map/ppermute | solution.py:393
  38.8 0.7 prepare_last.1
  39.6 0.0 copy-start.6
  39.6 0.0 copy-start.7
  39.6 3.2 collective-permute-done.5.got_left_ref
  42.8 0.7 finish.1
  43.5 14.1 %all_to_all.10 = bf16[8,64,512]{2,1,0:T(8,128)(2,1)S(1)} all-to-all(bf16[8,64,512]{2,1,0:T(8,128)(2,1)S(1)} %finish.1), channel_id=1, replica_groups=mesh['replica'=4,'fsdp'=8] {'fsdp'}, dimensions={0} | all-to-all | bytes 1048576 | tf_op jit(solution)/shard_map/all_to_all | solution.py:400
  57.6 5.5 %update.1 = (bf16[512,512]{1,0:T(8,128)(2,1)S(1)}, f32[512,512]{1,0:T(8,128)}, f32[512,512]{1,0:T(8,128)}) custom-call(s32[32]{0:T(128)S(1)} %copy-done.1, s32[3]{0:T(128)S(1)} %copy-done.8, bf16[512,512]{1,0:T(8,128)(2,1)S(1)} %bitcast.16, bf16[2,512,512]{2,1,0:T(8,128)(2,1)S(1)} %get-tuple-element.78.w_ref, f32[2,512,512]{2,1,0:T(8,128)S(1)} %get-tuple-element.79.q_ref, ...), custom_call_target="tpu_custom_call" | custom-call | flops 13421772800 | bytes 9961472 | tf_op jit(solution)/shard_map/update/pallas_call | solution.py:301
  63.1 369.1 %all_to_all.11.rows_ref = bf16[8,64,512]{2,1,0:T(8,128)(2,1)S(1)} all-to-all(bf16[8,64,512]{2,1,0:T(8,128)(2,1)S(1)} %bitcast.17), channel_id=1, replica_groups=mesh['replica'=4,'fsdp'=8] {'fsdp'}, dimensions={0} | all-to-all | bytes 1048576 | tf_op jit(solution)/shard_map/all_to_all | solution.py:408
  432.2 1.4 place.1
  (13 shorter events, 0.0 us)
Async XLA Ops:
  0.6 21.1 %copy-start.2 = (f32[1,512,512]{2,1,0:T(8,128)S(1)}, f32[1,512,512]{2,1,0:T(8,128)}, u32[]{:S(2)}) copy-start(f32[1,512,512]{2,1,0:T(8,128)} %param.12) | copy-start | bytes 3145732
  1.8 19.9 %copy-start.1 = (s32[32]{0:T(128)S(1)}, s32[32]{0:T(128)}, u32[]{:S(2)}) copy-start(s32[32]{0:T(128)} %order_ref.9) | copy-start | bytes 388
  1.8 19.9 %copy-start.8 = (s32[3]{0:T(128)S(1)}, s32[3]{0:T(128)}, u32[]{:S(2)}) copy-start(s32[3]{0:T(128)} %refresh_ref.9) | copy-start | bytes 40
  1.8 12.3 %collective-permute-start = (bf16[8,64,256]{2,1,0:T(8,128)(2,1)S(1)}, bf16[8,64,256]{2,1,0:T(8,128)(2,1)S(1)}, u32[]{:S(2)}, u32[]{:S(2)}) collective-permute-start(bf16[8,64,256]{2,1,0:T(8,128)(2,1)S(1)} %get-tuple-element.43), channel_id=1, source_target_pairs={{0,8},{8,16},{16,24},{24,0},{1,9},{9,17},{17,25},{25,1},{2,10},{10... | collective-permute-start | bytes 786440 | tf_op jit(solution)/shard_map/ppermute | solution.py:375
  4.9 13.6 %collective-permute-start.2 = (bf16[8,64,256]{2,1,0:T(8,128)(2,1)S(1)}, bf16[8,64,256]{2,1,0:T(8,128)(2,1)S(1)}, u32[]{:S(2)}, u32[]{:S(2)}) collective-permute-start(bf16[8,64,256]{2,1,0:T(8,128)(2,1)S(1)} %get-tuple-element.47), channel_id=1, source_target_pairs={{0,24},{8,0},{16,8},{24,16},{1,25},{9,1},{17,9},{25,17},{2,26},{10... | collective-permute-start | bytes 786440 | tf_op jit(solution)/shard_map/ppermute | solution.py:375
  7.0 1.6 copy-start
  8.6 13.1 %copy-start.3 = (f32[1,512,512]{2,1,0:T(8,128)S(1)}, f32[1,512,512]{2,1,0:T(8,128)}, u32[]{:S(2)}) copy-start(f32[1,512,512]{2,1,0:T(8,128)} %param.13) | copy-start | bytes 3145732
  8.6 13.1 %copy-start.4 = (f32[1,512,512]{2,1,0:T(8,128)S(1)}, f32[1,512,512]{2,1,0:T(8,128)}, u32[]{:S(2)}) copy-start(f32[1,512,512]{2,1,0:T(8,128)} %param.14) | copy-start | bytes 3145732
  8.6 13.1 %copy-start.5 = (f32[1,512,512]{2,1,0:T(8,128)S(1)}, f32[1,512,512]{2,1,0:T(8,128)}, u32[]{:S(2)}) copy-start(f32[1,512,512]{2,1,0:T(8,128)} %param.15) | copy-start | bytes 3145732
  14.2 12.8 %collective-permute-start.1 = (bf16[8,64,256]{2,1,0:T(8,128)(2,1)S(1)}, bf16[8,64,256]{2,1,0:T(8,128)(2,1)S(1)}, u32[]{:S(2)}, u32[]{:S(2)}) collective-permute-start(bf16[8,64,256]{2,1,0:T(8,128)(2,1)S(1)} %add_right.2), channel_id=1, source_target_pairs={{0,8},{8,16},{16,24},{24,0},{1,9},{9,17},{17,25},{25,1},{2,10},{10... | collective-permute-start | bytes 786440 | tf_op jit(solution)/shard_map/ppermute | solution.py:393
  18.6 14.0 %collective-permute-start.4 = (bf16[8,64,256]{2,1,0:T(8,128)(2,1)S(1)}, bf16[8,64,256]{2,1,0:T(8,128)(2,1)S(1)}, u32[]{:S(2)}, u32[]{:S(2)}) collective-permute-start(bf16[8,64,256]{2,1,0:T(8,128)(2,1)S(1)} %add_left.2), channel_id=1, source_target_pairs={{0,24},{8,0},{16,8},{24,16},{1,25},{9,1},{17,9},{25,17},{2,26},{10... | collective-permute-start | bytes 786440 | tf_op jit(solution)/shard_map/ppermute | solution.py:393
  27.1 11.8 %collective-permute-start.3 = (bf16[8,64,256]{2,1,0:T(8,128)(2,1)S(1)}, bf16[8,64,256]{2,1,0:T(8,128)(2,1)S(1)}, u32[]{:S(2)}, u32[]{:S(2)}) collective-permute-start(bf16[8,64,256]{2,1,0:T(8,128)(2,1)S(1)} %add_right.3), channel_id=1, source_target_pairs={{0,8},{8,16},{16,24},{24,0},{1,9},{9,17},{17,25},{25,1},{2,10},{10... | collective-permute-start | bytes 786440 | tf_op jit(solution)/shard_map/ppermute | solution.py:393
  32.7 10.2 %collective-permute-start.5 = (bf16[8,64,256]{2,1,0:T(8,128)(2,1)S(1)}, bf16[8,64,256]{2,1,0:T(8,128)(2,1)S(1)}, u32[]{:S(2)}, u32[]{:S(2)}) collective-permute-start(bf16[8,64,256]{2,1,0:T(8,128)(2,1)S(1)} %add_left.3), channel_id=1, source_target_pairs={{0,24},{8,0},{16,8},{24,16},{1,25},{9,1},{17,9},{25,17},{2,26},{10... | collective-permute-start | bytes 786440 | tf_op jit(solution)/shard_map/ppermute | solution.py:393
  39.6 18.0 %copy-start.6 = (f32[1,512,512]{2,1,0:T(8,128)S(1)}, f32[1,512,512]{2,1,0:T(8,128)}, u32[]{:S(2)}) copy-start(f32[1,512,512]{2,1,0:T(8,128)} %param.10) | copy-start | bytes 3145732
  39.6 18.0 %copy-start.7 = (f32[1,512,512]{2,1,0:T(8,128)S(1)}, f32[1,512,512]{2,1,0:T(8,128)}, u32[]{:S(2)}) copy-start(f32[1,512,512]{2,1,0:T(8,128)} %param.11) | copy-start | bytes 3145732

commit v8 on v7

--- a/solution.py
+++ b/solution.py
@@ -13,7 +13,7 @@
 NT = (((1,), (1,)), ((), ()))
 VMEM_LIMIT = 20 * 1024 * 1024
 
-START_BOUND = 4.0
+START_BOUND = 8.0
 END_BOUND = 0.016
 
 
@@ -121,12 +121,12 @@
         for side, (factor, basis) in enumerate(((lf_ref, lb_ref), (rf_ref, rb_ref))):
             p = dot(factor[...].astype(BF16), basis[...].astype(BF16))
             scale = lax.rsqrt(jnp.sum(p * p, axis=0, keepdims=True))
-            y = (p * scale).astype(BF16)
-            gram = dot(y.T, y).astype(BF16)
+            y = (p * scale).astype(BF16).T
+            gram = dot(y, y, NT).astype(BF16)
             square = jnp.abs(dot(gram, gram))
             reach = jnp.max(jnp.sum(square, axis=0, keepdims=True), axis=1, keepdims=True)
             factor_all = lax.rsqrt(0.5 * jnp.sqrt(reach))
-            h2[side] = (y.astype(F32) * factor_all).astype(BF16).T
+            h2[side] = (y.astype(F32) * factor_all).astype(BF16)
             th2[side] = jnp.where(eye, scale * (factor_all / 0.95), 0.0).astype(BF16)
 
 
@@ -160,8 +160,8 @@
     @pl.when(own_flag(order_ref, refresh_ref))
     def _():
         for side, (factor, basis) in enumerate(((lf_ref, lb_ref), (rf_ref, rb_ref))):
-            basis_hi, basis_lo = split(basis[...].T)
-            w = dot(th_ref[side], basis_hi) + dot(th_ref[side], basis_lo)
+            basis_hi, basis_lo = split(basis[...])
+            w = dot(th_ref[side], basis_hi, NT) + dot(th_ref[side], basis_lo, NT)
             w_hi, w_lo = split(w)
             factor_hi, factor_lo = split(factor[...])
             w2[side] = w_hi

time: 434 us -> 434 us (level)
  no operation moved by 1% of the time
where the time goes in v8:
time: 434 us; the launch traced here: 433 us
  blocking collectives  382 us (88%)
  waiting for transfers between devices  27.9 us (6%)
  Pallas kernels  10.3 us (2%)
  starting transfers between devices  8.71 us (2%)
    all_to_all x1, blocking collectives, on_device(): lax.all_to_all(update.reshape(owners, rows, width), 'fsdp', split_axis=0,...  369 us
    ppermute x4, waiting for transfers between devices, on_device(): got[way] = lax.ppermute(send[way], 'replica', ways[way])  18.3 us
    all_to_all x1, blocking collectives, on_device(): lax.all_to_all(summed, 'fsdp', split_axis=0, concat_axis=0, tiled=True)  13.2 us
    pallas_call x12, Pallas kernels, call(): pl.pallas_call(kernel, out_shape=[jax.ShapeDtypeStruct(shape, dtype) for...  10.3 us
    ppermute x2, waiting for transfers between devices, on_device(): got = [lax.ppermute(send[way], 'replica', ways[way]) for way in range(2)]  9.6 us
  transfers between devices with their start and end apart: 6, of which 6 were waited for; matrix products, arithmetic and copies ran while one was open for 0% of the time, Pallas kernels for 1%

profile of v8, /device:TPU:0, one launch (start us, length us, event | category | flops | bytes accessed | tf_op | source)
XLA Modules:
  0.0 432.6 jit_solution(2993705593493226575)
XLA Ops:
  0.7 1.2 dynamic-slice_bitcast_fusion
  1.8 0.0 copy-start.1
  1.8 0.0 copy-start.8
  1.8 3.1 collective-permute-start
  4.9 2.1 collective-permute-start.2
  7.0 1.6 copy-done
  8.6 0.2 own_blocks.1
  8.8 5.3 %collective-permute-done.got_ref = bf16[8,64,256]{2,1,0:T(8,128)(2,1)S(1)} collective-permute-done((bf16[8,64,256]{2,1,0:T(8,128)(2,1)S(1)}, bf16[8,64,256]{2,1,0:T(8,128)(2,1)S(1)}, u32[]{:S(2)}, u32[]{:S(2)}) %collective-permute-start) | collective-permute-done | bytes 262176 | tf_op jit(solution)/shard_map/ppermute | solution.py:375
  14.1 0.1 add_right.2
  14.2 0.1 collective-permute-start.1
  14.3 4.3 collective-permute-done.2.got_ref
  18.5 0.1 add_left.2
  18.6 3.1 collective-permute-start.4
  21.7 0.6 prepare_start.1
  22.3 4.7 %collective-permute-done.1.got_ref = bf16[8,64,256]{2,1,0:T(8,128)(2,1)S(1)} collective-permute-done((bf16[8,64,256]{2,1,0:T(8,128)(2,1)S(1)}, bf16[8,64,256]{2,1,0:T(8,128)(2,1)S(1)}, u32[]{:S(2)}, u32[]{:S(2)}) %collective-permute-start.1) | collective-permute-done | bytes 262176 | tf_op jit(solution)/shard_map/ppermute | solution.py:393
  27.0 0.1 add_right.3
  27.1 0.1 collective-permute-start.3
  27.1 0.6 prepare_boost.1
  27.7 4.9 %collective-permute-done.4.got_ref = bf16[8,64,256]{2,1,0:T(8,128)(2,1)S(1)} collective-permute-done((bf16[8,64,256]{2,1,0:T(8,128)(2,1)S(1)}, bf16[8,64,256]{2,1,0:T(8,128)(2,1)S(1)}, u32[]{:S(2)}, u32[]{:S(2)}) %collective-permute-start.4) | collective-permute-done | bytes 262176 | tf_op jit(solution)/shard_map/ppermute | solution.py:393
  32.6 0.1 add_left.3
  32.7 0.3 collective-permute-start.5
  33.0 0.6 prepare_more.1
  33.5 5.3 %collective-permute-done.3.got_right_ref = bf16[8,64,256]{2,1,0:T(8,128)(2,1)S(1)} collective-permute-done((bf16[8,64,256]{2,1,0:T(8,128)(2,1)S(1)}, bf16[8,64,256]{2,1,0:T(8,128)(2,1)S(1)}, u32[]{:S(2)}, u32[]{:S(2)}) %collective-permute-start.3) | collective-permute-done | bytes 262176 | tf_op jit(solution)/shard_map/ppermute | solution.py:393
  38.8 0.6 prepare_last.1
  39.4 0.0 copy-start.6
  39.4 0.0 copy-start.7
  39.4 3.4 collective-permute-done.5.got_left_ref
  42.8 0.7 finish.1
  43.5 13.2 %all_to_all.10 = bf16[8,64,512]{2,1,0:T(8,128)(2,1)S(1)} all-to-all(bf16[8,64,512]{2,1,0:T(8,128)(2,1)S(1)} %finish.1), channel_id=1, replica_groups=mesh['replica'=4,'fsdp'=8] {'fsdp'}, dimensions={0} | all-to-all | bytes 1048576 | tf_op jit(solution)/shard_map/all_to_all | solution.py:400
  56.7 5.5 %update.1 = (bf16[512,512]{1,0:T(8,128)(2,1)S(1)}, f32[512,512]{1,0:T(8,128)}, f32[512,512]{1,0:T(8,128)}) custom-call(s32[32]{0:T(128)S(1)} %copy-done.1, s32[3]{0:T(128)S(1)} %copy-done.8, bf16[512,512]{1,0:T(8,128)(2,1)S(1)} %bitcast.16, bf16[2,512,512]{2,1,0:T(8,128)(2,1)S(1)} %get-tuple-element.78.w_ref, f32[2,512,512]{2,1,0:T(8,128)S(1)} %get-tuple-element.79.q_ref, ...), custom_call_target="tpu_custom_call" | custom-call | flops 13421772800 | bytes 9961472 | tf_op jit(solution)/shard_map/update/pallas_call | solution.py:301
  62.3 368.8 %all_to_all.11.rows_ref = bf16[8,64,512]{2,1,0:T(8,128)(2,1)S(1)} all-to-all(bf16[8,64,512]{2,1,0:T(8,128)(2,1)S(1)} %bitcast.17), channel_id=1, replica_groups=mesh['replica'=4,'fsdp'=8] {'fsdp'}, dimensions={0} | all-to-all | bytes 1048576 | tf_op jit(solution)/shard_map/all_to_all | solution.py:408
  431.0 1.4 place.1
  (13 shorter events, 0.0 us)
Async XLA Ops:
  0.6 21.1 %copy-start.2 = (f32[1,512,512]{2,1,0:T(8,128)S(1)}, f32[1,512,512]{2,1,0:T(8,128)}, u32[]{:S(2)}) copy-start(f32[1,512,512]{2,1,0:T(8,128)} %param.12) | copy-start | bytes 3145732
  1.8 19.9 %copy-start.1 = (s32[32]{0:T(128)S(1)}, s32[32]{0:T(128)}, u32[]{:S(2)}) copy-start(s32[32]{0:T(128)} %order_ref.9) | copy-start | bytes 388
  1.8 19.9 %copy-start.8 = (s32[3]{0:T(128)S(1)}, s32[3]{0:T(128)}, u32[]{:S(2)}) copy-start(s32[3]{0:T(128)} %refresh_ref.9) | copy-start | bytes 40
  1.8 12.3 %collective-permute-start = (bf16[8,64,256]{2,1,0:T(8,128)(2,1)S(1)}, bf16[8,64,256]{2,1,0:T(8,128)(2,1)S(1)}, u32[]{:S(2)}, u32[]{:S(2)}) collective-permute-start(bf16[8,64,256]{2,1,0:T(8,128)(2,1)S(1)} %get-tuple-element.43), channel_id=1, source_target_pairs={{0,8},{8,16},{16,24},{24,0},{1,9},{9,17},{17,25},{25,1},{2,10},{10... | collective-permute-start | bytes 786440 | tf_op jit(solution)/shard_map/ppermute | solution.py:375
  4.9 13.6 %collective-permute-start.2 = (bf16[8,64,256]{2,1,0:T(8,128)(2,1)S(1)}, bf16[8,64,256]{2,1,0:T(8,128)(2,1)S(1)}, u32[]{:S(2)}, u32[]{:S(2)}) collective-permute-start(bf16[8,64,256]{2,1,0:T(8,128)(2,1)S(1)} %get-tuple-element.47), channel_id=1, source_target_pairs={{0,24},{8,0},{16,8},{24,16},{1,25},{9,1},{17,9},{25,17},{2,26},{10... | collective-permute-start | bytes 786440 | tf_op jit(solution)/shard_map/ppermute | solution.py:375
  7.0 1.6 copy-start
  8.6 13.1 %copy-start.3 = (f32[1,512,512]{2,1,0:T(8,128)S(1)}, f32[1,512,512]{2,1,0:T(8,128)}, u32[]{:S(2)}) copy-start(f32[1,512,512]{2,1,0:T(8,128)} %param.13) | copy-start | bytes 3145732
  8.6 13.1 %copy-start.4 = (f32[1,512,512]{2,1,0:T(8,128)S(1)}, f32[1,512,512]{2,1,0:T(8,128)}, u32[]{:S(2)}) copy-start(f32[1,512,512]{2,1,0:T(8,128)} %param.14) | copy-start | bytes 3145732
  8.6 13.1 %copy-start.5 = (f32[1,512,512]{2,1,0:T(8,128)S(1)}, f32[1,512,512]{2,1,0:T(8,128)}, u32[]{:S(2)}) copy-start(f32[1,512,512]{2,1,0:T(8,128)} %param.15) | copy-start | bytes 3145732
  14.2 12.8 %collective-permute-start.1 = (bf16[8,64,256]{2,1,0:T(8,128)(2,1)S(1)}, bf16[8,64,256]{2,1,0:T(8,128)(2,1)S(1)}, u32[]{:S(2)}, u32[]{:S(2)}) collective-permute-start(bf16[8,64,256]{2,1,0:T(8,128)(2,1)S(1)} %add_right.2), channel_id=1, source_target_pairs={{0,8},{8,16},{16,24},{24,0},{1,9},{9,17},{17,25},{25,1},{2,10},{10... | collective-permute-start | bytes 786440 | tf_op jit(solution)/shard_map/ppermute | solution.py:393
  18.6 14.0 %collective-permute-start.4 = (bf16[8,64,256]{2,1,0:T(8,128)(2,1)S(1)}, bf16[8,64,256]{2,1,0:T(8,128)(2,1)S(1)}, u32[]{:S(2)}, u32[]{:S(2)}) collective-permute-start(bf16[8,64,256]{2,1,0:T(8,128)(2,1)S(1)} %add_left.2), channel_id=1, source_target_pairs={{0,24},{8,0},{16,8},{24,16},{1,25},{9,1},{17,9},{25,17},{2,26},{10... | collective-permute-start | bytes 786440 | tf_op jit(solution)/shard_map/ppermute | solution.py:393
  27.1 11.8 %collective-permute-start.3 = (bf16[8,64,256]{2,1,0:T(8,128)(2,1)S(1)}, bf16[8,64,256]{2,1,0:T(8,128)(2,1)S(1)}, u32[]{:S(2)}, u32[]{:S(2)}) collective-permute-start(bf16[8,64,256]{2,1,0:T(8,128)(2,1)S(1)} %add_right.3), channel_id=1, source_target_pairs={{0,8},{8,16},{16,24},{24,0},{1,9},{9,17},{17,25},{25,1},{2,10},{10... | collective-permute-start | bytes 786440 | tf_op jit(solution)/shard_map/ppermute | solution.py:393
  32.7 10.2 %collective-permute-start.5 = (bf16[8,64,256]{2,1,0:T(8,128)(2,1)S(1)}, bf16[8,64,256]{2,1,0:T(8,128)(2,1)S(1)}, u32[]{:S(2)}, u32[]{:S(2)}) collective-permute-start(bf16[8,64,256]{2,1,0:T(8,128)(2,1)S(1)} %add_left.3), channel_id=1, source_target_pairs={{0,24},{8,0},{16,8},{24,16},{1,25},{9,1},{17,9},{25,17},{2,26},{10... | collective-permute-start | bytes 786440 | tf_op jit(solution)/shard_map/ppermute | solution.py:393
  39.4 17.3 %copy-start.6 = (f32[1,512,512]{2,1,0:T(8,128)S(1)}, f32[1,512,512]{2,1,0:T(8,128)}, u32[]{:S(2)}) copy-start(f32[1,512,512]{2,1,0:T(8,128)} %param.10) | copy-start | bytes 3145732
  39.4 17.3 %copy-start.7 = (f32[1,512,512]{2,1,0:T(8,128)S(1)}, f32[1,512,512]{2,1,0:T(8,128)}, u32[]{:S(2)}) copy-start(f32[1,512,512]{2,1,0:T(8,128)} %param.11) | copy-start | bytes 3145732

commit v9 on v8

--- a/solution.py
+++ b/solution.py
@@ -363,15 +363,16 @@
         [(i, (i - 1) % replicas) for i in range(replicas)],
     )
     half = width // 2
-    send = [
-        lax.dynamic_slice(
-            grad_parts[0],
-            (passing_group(0, way, replicas) * group_size, 0, way * half),
-            (group_size, rows, half),
+    send = [None, None]
+    start = passing_group(0, 1, replicas) * group_size
+    for way in range(2):
+        first = passing_group(0, 0, replicas) * group_size if way == 0 else start
+        send[way] = lax.dynamic_slice(
+            grad_parts[0], (first, 0, way * half), (group_size, rows, half)
         )
-        for way in range(2)
-    ]
-    tied, *send = lax.optimization_barrier((block_order, *send))
+        if way == 0:
+            start, send[0] = lax.optimization_barrier((start, send[0]))
+    tied, send[1] = lax.optimization_barrier((block_order, send[1]))
     got = [lax.ppermute(send[way], "replica", ways[way]) for way in range(2)]
     own = list(
         call(

time: 434 us -> 433 us (level)
  no operation moved by 1% of the time
where the time goes in v9:
time: 433 us
  blocking collectives  383 us (88%)
  waiting for transfers between devices  27.4 us (6%)
  Pallas kernels  10.3 us (2%)
  starting transfers between devices  7.42 us (2%)
    all_to_all x1, blocking collectives, on_device(): lax.all_to_all(update.reshape(owners, rows, width), 'fsdp', split_axis=0,...  369 us
    ppermute x4, waiting for transfers between devices, on_device(): got[way] = lax.ppermute(send[way], 'replica', ways[way])  17.6 us
    all_to_all x1, blocking collectives, on_device(): lax.all_to_all(summed, 'fsdp', split_axis=0, concat_axis=0, tiled=True)  13.8 us
    pallas_call x12, Pallas kernels, call(): pl.pallas_call(kernel, out_shape=[jax.ShapeDtypeStruct(shape, dtype) for...  10.3 us
    ppermute x2, waiting for transfers between devices, on_device(): got = [lax.ppermute(send[way], 'replica', ways[way]) for way in range(2)]  9.72 us
  transfers between devices with their start and end apart: 6, of which 6 were waited for; matrix products, arithmetic and copies ran while one was open for 0% of the time, Pallas kernels for 1%

profile of v9, /device:TPU:0, one launch (start us, length us, event | category | flops | bytes accessed | tf_op | source)
XLA Modules:
  0.0 432.6 jit_solution(16557474489739070324)
XLA Ops:
  0.7 1.1 dynamic-slice_bitcast_fusion.1
  1.7 3.1 collective-permute-start
  4.8 1.0 dynamic-slice_bitcast_fusion
  5.8 2.1 collective-permute-start.2
  7.9 1.6 copy-done
  9.5 0.2 own_blocks.1
  9.7 4.3 collective-permute-done.got_ref
  14.0 0.1 add_right.2
  14.1 0.1 collective-permute-start.1
  14.1 5.4 %collective-permute-done.2.got_ref = bf16[8,64,256]{2,1,0:T(8,128)(2,1)S(1)} collective-permute-done((bf16[8,64,256]{2,1,0:T(8,128)(2,1)S(1)}, bf16[8,64,256]{2,1,0:T(8,128)(2,1)S(1)}, u32[]{:S(2)}, u32[]{:S(2)}) %collective-permute-start.2) | collective-permute-done | bytes 262176 | tf_op jit(solution)/shard_map/ppermute | solution.py:376
  19.5 0.1 add_left.2
  19.6 2.0 collective-permute-start.4
  21.6 0.0 copy-done.5
  21.6 0.6 prepare_start.1
  22.2 4.7 %collective-permute-done.1.got_ref = bf16[8,64,256]{2,1,0:T(8,128)(2,1)S(1)} collective-permute-done((bf16[8,64,256]{2,1,0:T(8,128)(2,1)S(1)}, bf16[8,64,256]{2,1,0:T(8,128)(2,1)S(1)}, u32[]{:S(2)}, u32[]{:S(2)}) %collective-permute-start.1) | collective-permute-done | bytes 262176 | tf_op jit(solution)/shard_map/ppermute | solution.py:394
  26.9 0.1 add_right.3
  26.9 0.1 collective-permute-start.3
  27.0 0.6 prepare_boost.1
  27.6 5.1 %collective-permute-done.4.got_ref = bf16[8,64,256]{2,1,0:T(8,128)(2,1)S(1)} collective-permute-done((bf16[8,64,256]{2,1,0:T(8,128)(2,1)S(1)}, bf16[8,64,256]{2,1,0:T(8,128)(2,1)S(1)}, u32[]{:S(2)}, u32[]{:S(2)}) %collective-permute-start.4) | collective-permute-done | bytes 262176 | tf_op jit(solution)/shard_map/ppermute | solution.py:394
  32.6 0.1 add_left.3
  32.7 0.1 collective-permute-start.5
  32.8 0.6 prepare_more.1
  33.4 4.7 %collective-permute-done.3.got_right_ref = bf16[8,64,256]{2,1,0:T(8,128)(2,1)S(1)} collective-permute-done((bf16[8,64,256]{2,1,0:T(8,128)(2,1)S(1)}, bf16[8,64,256]{2,1,0:T(8,128)(2,1)S(1)}, u32[]{:S(2)}, u32[]{:S(2)}) %collective-permute-start.3) | collective-permute-done | bytes 262176 | tf_op jit(solution)/shard_map/ppermute | solution.py:394
  38.1 0.6 prepare_last.1
  38.7 0.0 copy-start.6
  38.7 0.0 copy-start.7
  38.7 3.2 collective-permute-done.5.got_left_ref
  41.9 0.7 finish.1
  42.6 13.8 %all_to_all.10 = bf16[8,64,512]{2,1,0:T(8,128)(2,1)S(1)} all-to-all(bf16[8,64,512]{2,1,0:T(8,128)(2,1)S(1)} %finish.1), channel_id=1, replica_groups=mesh['replica'=4,'fsdp'=8] {'fsdp'}, dimensions={0} | all-to-all | bytes 1048576 | tf_op jit(solution)/shard_map/all_to_all | solution.py:401
  56.4 5.5 %update.1 = (bf16[512,512]{1,0:T(8,128)(2,1)S(1)}, f32[512,512]{1,0:T(8,128)}, f32[512,512]{1,0:T(8,128)}) custom-call(s32[32]{0:T(128)S(1)} %copy-done.1, s32[3]{0:T(128)S(1)} %copy-done.8, bf16[512,512]{1,0:T(8,128)(2,1)S(1)} %bitcast.16, bf16[2,512,512]{2,1,0:T(8,128)(2,1)S(1)} %get-tuple-element.80.w_ref, f32[2,512,512]{2,1,0:T(8,128)S(1)} %get-tuple-element.81.q_ref, ...), custom_call_target="tpu_custom_call" | custom-call | flops 13421772800 | bytes 9961472 | tf_op jit(solution)/shard_map/update/pallas_call | solution.py:301
  61.9 369.1 %all_to_all.11.rows_ref = bf16[8,64,512]{2,1,0:T(8,128)(2,1)S(1)} all-to-all(bf16[8,64,512]{2,1,0:T(8,128)(2,1)S(1)} %bitcast.17), channel_id=1, replica_groups=mesh['replica'=4,'fsdp'=8] {'fsdp'}, dimensions={0} | all-to-all | bytes 1048576 | tf_op jit(solution)/shard_map/all_to_all | solution.py:409
  431.0 1.4 place.1
  (14 shorter events, 0.0 us)
Async XLA Ops:
  0.6 20.9 %copy-start.5 = (f32[1,512,512]{2,1,0:T(8,128)S(1)}, f32[1,512,512]{2,1,0:T(8,128)}, u32[]{:S(2)}) copy-start(f32[1,512,512]{2,1,0:T(8,128)} %param.15) | copy-start | bytes 3145732
  1.7 12.3 %collective-permute-start = (bf16[8,64,256]{2,1,0:T(8,128)(2,1)S(1)}, bf16[8,64,256]{2,1,0:T(8,128)(2,1)S(1)}, u32[]{:S(2)}, u32[]{:S(2)}) collective-permute-start(bf16[8,64,256]{2,1,0:T(8,128)(2,1)S(1)} %dynamic-slice_bitcast_fusion.1), channel_id=1, source_target_pairs={{0,8},{8,16},{16,24},{24,0},{1,9},{9,17},{17,25},{25,1},{2,10},{10... | collective-permute-start | bytes 786440 | tf_op jit(solution)/shard_map/ppermute | solution.py:376
  4.8 16.8 %copy-start.1 = (s32[32]{0:T(128)S(1)}, s32[32]{0:T(128)}, u32[]{:S(2)}) copy-start(s32[32]{0:T(128)} %order_ref.9) | copy-start | bytes 388
  4.8 16.8 %copy-start.8 = (s32[3]{0:T(128)S(1)}, s32[3]{0:T(128)}, u32[]{:S(2)}) copy-start(s32[3]{0:T(128)} %refresh_ref.9) | copy-start | bytes 40
  5.8 13.7 %collective-permute-start.2 = (bf16[8,64,256]{2,1,0:T(8,128)(2,1)S(1)}, bf16[8,64,256]{2,1,0:T(8,128)(2,1)S(1)}, u32[]{:S(2)}, u32[]{:S(2)}) collective-permute-start(bf16[8,64,256]{2,1,0:T(8,128)(2,1)S(1)} %dynamic-slice_bitcast_fusion), channel_id=1, source_target_pairs={{0,24},{8,0},{16,8},{24,16},{1,25},{9,1},{17,9},{25,17},{2,26},{10... | collective-permute-start | bytes 786440 | tf_op jit(solution)/shard_map/ppermute | solution.py:376
  7.9 1.6 copy-start
  9.5 12.1 %copy-start.2 = (f32[1,512,512]{2,1,0:T(8,128)S(1)}, f32[1,512,512]{2,1,0:T(8,128)}, u32[]{:S(2)}) copy-start(f32[1,512,512]{2,1,0:T(8,128)} %param.12) | copy-start | bytes 3145732
  9.5 12.1 %copy-start.3 = (f32[1,512,512]{2,1,0:T(8,128)S(1)}, f32[1,512,512]{2,1,0:T(8,128)}, u32[]{:S(2)}) copy-start(f32[1,512,512]{2,1,0:T(8,128)} %param.13) | copy-start | bytes 3145732
  9.5 12.1 %copy-start.4 = (f32[1,512,512]{2,1,0:T(8,128)S(1)}, f32[1,512,512]{2,1,0:T(8,128)}, u32[]{:S(2)}) copy-start(f32[1,512,512]{2,1,0:T(8,128)} %param.14) | copy-start | bytes 3145732
  14.1 12.8 %collective-permute-start.1 = (bf16[8,64,256]{2,1,0:T(8,128)(2,1)S(1)}, bf16[8,64,256]{2,1,0:T(8,128)(2,1)S(1)}, u32[]{:S(2)}, u32[]{:S(2)}) collective-permute-start(bf16[8,64,256]{2,1,0:T(8,128)(2,1)S(1)} %add_right.2), channel_id=1, source_target_pairs={{0,8},{8,16},{16,24},{24,0},{1,9},{9,17},{17,25},{25,1},{2,10},{10... | collective-permute-start | bytes 786440 | tf_op jit(solution)/shard_map/ppermute | solution.py:394
  19.6 13.0 %collective-permute-start.4 = (bf16[8,64,256]{2,1,0:T(8,128)(2,1)S(1)}, bf16[8,64,256]{2,1,0:T(8,128)(2,1)S(1)}, u32[]{:S(2)}, u32[]{:S(2)}) collective-permute-start(bf16[8,64,256]{2,1,0:T(8,128)(2,1)S(1)} %add_left.2), channel_id=1, source_target_pairs={{0,24},{8,0},{16,8},{24,16},{1,25},{9,1},{17,9},{25,17},{2,26},{10... | collective-permute-start | bytes 786440 | tf_op jit(solution)/shard_map/ppermute | solution.py:394
  26.9 11.2 %collective-permute-start.3 = (bf16[8,64,256]{2,1,0:T(8,128)(2,1)S(1)}, bf16[8,64,256]{2,1,0:T(8,128)(2,1)S(1)}, u32[]{:S(2)}, u32[]{:S(2)}) collective-permute-start(bf16[8,64,256]{2,1,0:T(8,128)(2,1)S(1)} %add_right.3), channel_id=1, source_target_pairs={{0,8},{8,16},{16,24},{24,0},{1,9},{9,17},{17,25},{25,1},{2,10},{10... | collective-permute-start | bytes 786440 | tf_op jit(solution)/shard_map/ppermute | solution.py:394
  32.7 9.2 %collective-permute-start.5 = (bf16[8,64,256]{2,1,0:T(8,128)(2,1)S(1)}, bf16[8,64,256]{2,1,0:T(8,128)(2,1)S(1)}, u32[]{:S(2)}, u32[]{:S(2)}) collective-permute-start(bf16[8,64,256]{2,1,0:T(8,128)(2,1)S(1)} %add_left.3), channel_id=1, source_target_pairs={{0,24},{8,0},{16,8},{24,16},{1,25},{9,1},{17,9},{25,17},{2,26},{10... | collective-permute-start | bytes 786440 | tf_op jit(solution)/shard_map/ppermute | solution.py:394
  38.7 17.7 %copy-start.6 = (f32[1,512,512]{2,1,0:T(8,128)S(1)}, f32[1,512,512]{2,1,0:T(8,128)}, u32[]{:S(2)}) copy-start(f32[1,512,512]{2,1,0:T(8,128)} %param.10) | copy-start | bytes 3145732
  38.7 17.7 %copy-start.7 = (f32[1,512,512]{2,1,0:T(8,128)S(1)}, f32[1,512,512]{2,1,0:T(8,128)}, u32[]{:S(2)}) copy-start(f32[1,512,512]{2,1,0:T(8,128)} %param.11) | copy-start | bytes 3145732
